TPU v7x, 128 devices: a whole 4x4x4 slice. The times are simulated.
128 devices in a mesh: rep: 16 (over z_hi, y, core), tp: 8 (over x, z_lo).
Axes of the slice: x: 4, y: 4, z: 4 (z_hi: 2, z_lo: 2; z = z_hi * 2 + z_lo), core: 2. Of those that a mesh axis runs over, the one named last changes fastest.
Arguments:
- step_inputs: bfloat16 [2, 1024, 8192], P(None, 'rep', 'tp'), may hold values from -650 to 650
- norm_gain: bfloat16 [8192], replicated, may hold values from 0.25 to 1.75
- w_query: bfloat16 [8192, 4096], P(('rep', 'tp')), may hold values from -0.25 to 0.25
- w_key: bfloat16 [8192, 1024], P(('rep', 'tp')), may hold values from -0.0625 to 0.0625
- w_value: bfloat16 [8192, 1024], P(('rep', 'tp')), may hold values from -0.0625 to 0.0625
- w_out: bfloat16 [4096, 8192], P(('rep', 'tp')), may hold values from -0.375 to 0.375
- key_cache: bfloat16 [1024, 8, 512, 128], P('rep', 'tp'), may hold values from -420 to 420
- value_cache: bfloat16 [1024, 8, 512, 128], P('rep', 'tp'), may hold values from -6 to 6
- lengths: int32 [1024], P('rep'), may hold values from 128 to 512, as said below
Outputs:
- block_output: bfloat16 [2, 1024, 8192], P(None, 'rep', 'tp')
Inputs may be any that keep to these rules, and one draw needn't show every extreme that they name: `lengths`: some row has exactly 512 cached positions.
All inputs are finite; a program needn't handle non-finite values.
Results may differ from a plain program's by a relative error of at most 0.012.
The roundings to bfloat16 on the way count: a program that leaves them out, or rounds other values in their place, can miss the bound.
Values may be sent and summed in bfloat16 or wider, within the bound.
No kernel may reach another device: no remote copies, remote signals or barrier semaphores. Data moves between devices by JAX's collectives and lax.ppermute only.
A program may use at most 192 MiB of HBM per device.

v0:
```python
import jax
import jax.numpy as jnp
from jax import lax
from jax.sharding import PartitionSpec as P

HD = 128
STEPS = 2


norm_eps = 1e-05
rope_base = 500000.0


def rotate(vectors, positions):
    half_width = vectors.shape[-1] // 2
    ladder = jnp.arange(half_width).astype(jnp.float32)
    frequency = jnp.power(jnp.float32(rope_base), -2.0 * ladder / vectors.shape[-1])
    angles = positions.astype(jnp.float32)[:, None, None] * frequency[None, None, :]
    cosine_part = jnp.cos(angles)
    sine_part = jnp.sin(angles)
    leading = vectors[..., :half_width]
    trailing = vectors[..., half_width:]
    return jnp.concatenate(
        [
            leading * cosine_part - trailing * sine_part,
            trailing * cosine_part + leading * sine_part,
        ],
        axis=-1,
    )


def normalize(inputs, norm_gain):
    values = inputs.astype(jnp.float32)
    factor = lax.rsqrt(jnp.mean(values * values, axis=-1, keepdims=True) + norm_eps)
    return (values * factor * norm_gain.astype(jnp.float32)).astype(jnp.bfloat16)


def reorder(values, replicas, columns):
    pieces = values.shape[-1] // (replicas * columns)
    split = values.reshape(values.shape[:-1] + (replicas, columns, pieces))
    return jnp.swapaxes(split, -3, -2).reshape(values.shape)


def attend_local(queries, key_block, value_block, lengths_block, new_keys, new_values):
    row_count, head_count, head_width = queries.shape
    group_count = key_block.shape[1]
    score_scale = head_width ** (-0.5)
    grouped = queries.reshape(row_count, group_count, head_count // group_count, head_width)
    cache_scores = (
        jnp.einsum("rkgd,rkld->rkgl", grouped, key_block, preferred_element_type=jnp.float32)
        * score_scale
    )
    new_scores = (
        jnp.einsum("rkgd,rksd->rkgs", grouped, new_keys, preferred_element_type=jnp.float32)
        * score_scale
    )
    visible = jnp.arange(key_block.shape[2])[None, :] < lengths_block[:, None]
    cache_scores = jnp.where(visible[:, None, None, :], cache_scores, -jnp.inf)
    highest = jnp.maximum(
        jnp.max(cache_scores, axis=-1, keepdims=True), jnp.max(new_scores, axis=-1, keepdims=True)
    )
    cache_weights = jnp.exp(cache_scores - highest)
    new_weights = jnp.exp(new_scores - highest)
    denominator = jnp.sum(cache_weights, axis=-1, keepdims=True) + jnp.sum(
        new_weights, axis=-1, keepdims=True
    )
    cache_probs = (cache_weights / denominator).astype(jnp.bfloat16)
    new_probs = (new_weights / denominator).astype(jnp.bfloat16)
    combined = jnp.einsum(
        "rkgl,rkld->rkgd", cache_probs, value_block, preferred_element_type=jnp.float32
    )
    combined = combined + jnp.einsum(
        "rkgs,rksd->rkgd", new_probs, new_values, preferred_element_type=jnp.float32
    )
    return combined.reshape(row_count, head_count * head_width).astype(jnp.bfloat16)


def shards(step_inputs, norm_gain, w_query, w_key, w_value, w_out, key_cache, value_cache, lengths):
    replicas = lax.axis_size("rep")
    columns = lax.axis_size("tp")
    gathered_query, gathered_key, gathered_value, gathered_out = (
        lax.all_gather(w_query, "rep", axis=0, tiled=True),
        lax.all_gather(w_key, "rep", axis=0, tiled=True),
        lax.all_gather(w_value, "rep", axis=0, tiled=True),
        lax.all_gather(w_out, "rep", axis=0, tiled=True),
    )
    query_weight, key_weight, value_weight, out_weight = (
        lax.all_to_all(gathered_query, "tp", split_axis=1, concat_axis=0, tiled=True),
        lax.all_to_all(gathered_key, "tp", split_axis=1, concat_axis=0, tiled=True),
        lax.all_to_all(gathered_value, "tp", split_axis=1, concat_axis=0, tiled=True),
        lax.all_to_all(gathered_out, "tp", split_axis=1, concat_axis=0, tiled=True),
    )
    features = lax.all_gather(step_inputs, "tp", axis=2, tiled=True)
    row_count = features.shape[1]
    local_heads = query_weight.shape[1] // HD
    local_groups = key_weight.shape[1] // HD
    kept_keys = []
    kept_values = []
    results = []
    for step_index in range(STEPS):
        normed = normalize(features[step_index], norm_gain)
        normed = reorder(normed, replicas, columns)
        positions = lengths + step_index
        queries = jnp.dot(normed, query_weight, preferred_element_type=jnp.float32).reshape(
            row_count, local_heads, HD
        )
        queries = rotate(queries, positions).astype(jnp.bfloat16)
        fresh_key = jnp.dot(normed, key_weight, preferred_element_type=jnp.float32).reshape(
            row_count, local_groups, HD
        )
        kept_keys.append(rotate(fresh_key, positions).astype(jnp.bfloat16))
        fresh_value = jnp.dot(normed, value_weight, preferred_element_type=jnp.float32).astype(
            jnp.bfloat16
        )
        kept_values.append(fresh_value.reshape(row_count, local_groups, HD))
        attention = attend_local(
            queries,
            key_cache,
            value_cache,
            lengths,
            jnp.stack(kept_keys, axis=2),
            jnp.stack(kept_values, axis=2),
        )
        joined = lax.all_gather(attention, "tp", axis=1, tiled=True)
        joined = reorder(joined, replicas, columns)
        results.append(
            jnp.dot(joined, out_weight, preferred_element_type=jnp.float32).astype(jnp.bfloat16)
        )
    return jnp.stack(results, axis=0)


def solution(mesh):
    in_specs = (
        P(None, "rep", "tp"),
        P(),
        P(("rep", "tp"), None),
        P(("rep", "tp"), None),
        P(("rep", "tp"), None),
        P(("rep", "tp"), None),
        P("rep", "tp", None, None),
        P("rep", "tp", None, None),
        P("rep"),
    )
    out_specs = P(None, "rep", "tp")
    return jax.shard_map(shards, mesh=mesh, in_specs=in_specs, out_specs=out_specs, check_vma=False)
```

profile of v0, /device:TPU:0, one launch (start us, length us, event | category | flops | bytes accessed | tf_op | source)
XLA Modules:
  0.0 689.4 jit_solution(13415737024411897324)
XLA Ops:
  6.5 0.7 all-gather.10.cloned.1.call-update
  7.3 0.7 all-gather.12.cloned.1.call-update
  8.1 0.7 all-gather.8.cloned.1.call-update
  8.8 0.5 all-gather.14.cloned.1.call-update
  9.3 51.5 %all-gather.10.cloned.1.call-done = bf16[1024,1024]{1,0:T(8,128)(2,1)} async-done(((bf16[64,1024]{1,0:T(8,128)(2,1)}), bf16[1024,1024]{1,0:T(8,128)(2,1)}) %all-gather.10.cloned.1.call-update) | async-done | bytes 2097168 | tf_op jit(solution)/shard_map/all_gather | solution.py:83
  60.8 4.0 copy.91
  64.7 4.3 all-to-all-start.1
  69.1 52.3 %all-gather.12.cloned.1.call-done = bf16[1024,1024]{1,0:T(8,128)(2,1)} async-done(((bf16[64,1024]{1,0:T(8,128)(2,1)}), bf16[1024,1024]{1,0:T(8,128)(2,1)}) %all-gather.12.cloned.1.call-update) | async-done | bytes 2097168 | tf_op jit(solution)/shard_map/all_gather | solution.py:84
  121.4 4.0 copy.93
  125.3 4.3 all-to-all-start.2
  129.7 83.9 %all-gather.8.cloned.1.call-done = bf16[1024,4096]{1,0:T(8,128)(2,1)} async-done(((bf16[64,4096]{1,0:T(8,128)(2,1)}), bf16[1024,4096]{1,0:T(8,128)(2,1)}) %all-gather.8.cloned.1.call-update) | async-done | bytes 8388624 | tf_op jit(solution)/shard_map/all_gather | solution.py:82
  213.6 12.0 %copy.87 = bf16[1024,4096]{0,1:T(8,128)(2,1)} copy(bf16[1024,4096]{1,0:T(8,128)(2,1)} %all-gather.8.cloned.1.call-done) | data formatting | bytes 16777216 | tf_op jit(solution)/shard_map/all_gather | solution.py:82
  225.6 11.4 %copy.88 = bf16[1024,8,512]{2,0,1:T(8,128)(2,1)} copy(bf16[1024,8,512]{0,2,1:T(8,128)(2,1)} %bitcast.114) | data formatting | bytes 16777216 | tf_op jit(solution)/shard_map/all_to_all | solution.py:88
  237.0 5.1 all-to-all-start
  242.2 0.5 all-gather.6.cloned.1.call-update
  242.9 0.3 multiply_cosine_fusion.3
  243.3 124.4 %all-gather.14.cloned.1.call-done = bf16[512,8192]{1,0:T(8,128)(2,1)} async-done(((bf16[32,8192]{1,0:T(8,128)(2,1)}), bf16[512,8192]{1,0:T(8,128)(2,1)}) %all-gather.14.cloned.1.call-update) | async-done | bytes 8388624 | tf_op jit(solution)/shard_map/all_gather | solution.py:85
  367.6 11.8 %copy.97 = bf16[512,8192]{0,1:T(8,128)(2,1)} copy(bf16[512,8192]{1,0:T(8,128)(2,1)} %all-gather.14.cloned.1.call-done) | data formatting | bytes 16777216 | tf_op jit(solution)/shard_map/all_gather | solution.py:85
  379.5 5.1 all-to-all-start.3
  384.6 131.4 %all-gather.6.cloned.1.call-done = bf16[2,64,8192]{2,1,0:T(8,128)(2,1)} async-done(((bf16[2,64,1024]{2,1,0:T(8,128)(2,1)}), bf16[2,64,8192]{2,1,0:T(8,128)(2,1)}) %all-gather.6.cloned.1.call-update) | async-done | bytes 2097168 | tf_op jit(solution)/shard_map/all_gather | solution.py:93
  516.0 3.3 slice_convert_fusion.1
  519.3 4.6 reshape.559
  523.9 3.0 reshape.561
  526.9 2.0 multiply_reduce_fusion.1
  529.0 5.6 fusion.8
  534.6 0.6 copy.99
  535.2 2.5 reshape.565
  537.7 1.7 reshape.553
  539.4 2.2 copy.86
  541.6 2.5 reshape.547
  544.1 2.5 reshape.562
  546.6 3.9 copy.92
  550.5 3.0 copy.94
  553.5 2.5 convolution_bitcast_fusion.1
  556.0 2.1 convolution_bitcast_fusion
  558.1 0.3 fusion.57
  558.5 0.5 fusion.31
  559.0 0.5 fusion.73
  559.7 11.5 %copy.89 = bf16[8192,512]{0,1:T(8,128)(2,1)} copy(bf16[8192,512]{1,0:T(8,128)(2,1)} %bitcast.3) | data formatting | bytes 16777216 | tf_op jit(solution)/shard_map/all_to_all | solution.py:88
  571.1 6.2 fusion.75
  577.3 0.1 subtract_convert_fusion
  577.4 0.1 pad_maximum_fusion.2
  577.5 0.2 fusion.71
  577.8 5.9 fusion.70
  583.7 0.1 fusion.51
  583.8 0.3 fusion.33
  584.2 1.2 fusion
  585.4 0.3 fusion.18
  585.7 0.1 copy.109
  585.9 31.8 %all_gather.27 = bf16[64,4096]{0,1:T(8,128)(2,1)S(1)} all-gather(bf16[64,512]{0,1:T(8,128)(2,1)S(1)} %bitcast.130), channel_id=1, replica_groups=mesh['rep'=16,'tp'=8] {'tp'}, dimensions={1}, use_global_device_ids=true | all-gather | bytes 589824 | tf_op jit(solution)/shard_map/all_gather | solution.py:124
  617.8 11.6 %copy.98 = bf16[8,512,1024]{2,1,0:T(8,128)(2,1)} copy(bf16[8,512,1024]{1,2,0:T(8,128)(2,1)} %bitcast.25) | data formatting | bytes 16777216 | tf_op jit(solution)/shard_map/all_to_all | solution.py:91
  629.4 6.2 fusion.74
  635.6 0.1 subtract_convert_fusion.1
  635.8 0.1 pad_maximum_fusion.1
  635.9 5.9 fusion.72
  641.7 0.2 fusion.40
  642.0 0.3 fusion.32
  642.4 1.3 fusion.22
  643.7 0.1 copy.108
  643.9 30.8 %all_gather.25 = bf16[64,4096]{0,1:T(8,128)(2,1)S(1)} all-gather(bf16[64,512]{0,1:T(8,128)(2,1)S(1)} %bitcast.131), channel_id=1, replica_groups=mesh['rep'=16,'tp'=8] {'tp'}, dimensions={1}, use_global_device_ids=true | all-gather | bytes 589824 | tf_op jit(solution)/shard_map/all_gather | solution.py:124
  674.8 5.1 fusion.17
  679.9 0.6 slice-done.1
  680.6 1.6 fusion.16
  682.2 0.7 pad_maximum_fusion
  (49 shorter events, 0.8 us)
Async XLA Ops:
  6.5 54.2 %all-gather.10.cloned.1.call-start = ((), (), s32[]{:S(2)}) async-start(), calls=%async_computation.6 | async-start | bytes 2228224 | tf_op jit(solution)/shard_map/all_gather | solution.py:83
  7.3 114.1 %all-gather.12.cloned.1.call-start = ((), (), s32[]{:S(2)}) async-start(), calls=%async_computation.7 | async-start | bytes 2228224 | tf_op jit(solution)/shard_map/all_gather | solution.py:84
  8.0 205.6 %all-gather.8.cloned.1.call-start = ((), (), s32[]{:S(2)}) async-start(), calls=%async_computation.5 | async-start | bytes 8912896 | tf_op jit(solution)/shard_map/all_gather | solution.py:82
  8.7 358.9 %all-gather.14.cloned.1.call-start = ((), (), s32[]{:S(2)}) async-start(), calls=%async_computation.8 | async-start | bytes 8912896 | tf_op jit(solution)/shard_map/all_gather | solution.py:85
  64.7 60.6 %all-to-all-start.1 = ((bf16[1024,8,128]{0,2,1:T(8,128)(2,1)}), bf16[1024,8,128]{0,2,1:T(8,128)(2,1)S(1)}, u32[]{:S(2)}, u32[]{:S(2)}) async-start(bf16[1024,8,128]{0,2,1:T(8,128)(2,1)} %bitcast.125), calls=%async_computation.1 | async-start | bytes 4194304 | tf_op jit(solution)/shard_map/all_to_all | solution.py:89
  125.3 100.3 %copy-start.1 = (bf16[1024,8,128]{0,2,1:T(8,128)(2,1)}, bf16[1024,8,128]{0,2,1:T(8,128)(2,1)S(1)}, u32[]{:S(2)}) copy-start(bf16[1024,8,128]{0,2,1:T(8,128)(2,1)S(1)} %all-to-all-done.1) | copy-start | bytes 6291460
  125.3 111.7 %all-to-all-start.2 = ((bf16[1024,8,128]{0,2,1:T(8,128)(2,1)}), bf16[1024,8,128]{0,2,1:T(8,128)(2,1)}, u32[]{:S(2)}, u32[]{:S(2)}) async-start(bf16[1024,8,128]{0,2,1:T(8,128)(2,1)} %bitcast.124), calls=%async_computation.2 | async-start | bytes 4194304 | tf_op jit(solution)/shard_map/all_to_all | solution.py:90
  237.0 5.7 copy-start.4
  237.0 5.8 copy-start.5
  237.0 142.4 %all-to-all-start = ((bf16[1024,8,512]{2,0,1:T(8,128)(2,1)}), bf16[1024,8,512]{2,0,1:T(8,128)(2,1)}, u32[]{:S(2)}, u32[]{:S(2)}) async-start(bf16[1024,8,512]{2,0,1:T(8,128)(2,1)} %copy.88), calls=%async_computation | async-start | bytes 16777216 | tf_op jit(solution)/shard_map/all_to_all | solution.py:88
  242.1 273.9 %all-gather.6.cloned.1.call-start = ((), (), s32[]{:S(2)}) async-start(), calls=%async_computation.4 | async-start | bytes 2359296 | tf_op jit(solution)/shard_map/all_gather | solution.py:93
  379.5 238.4 %all-to-all-start.3 = ((bf16[512,8,1024]{0,2,1:T(8,128)(2,1)}), bf16[512,8,1024]{0,2,1:T(8,128)(2,1)}, u32[]{:S(2)}, u32[]{:S(2)}) async-start(bf16[512,8,1024]{0,2,1:T(8,128)(2,1)} %bitcast.113), calls=%async_computation.3 | async-start | bytes 16777216 | tf_op jit(solution)/shard_map/all_to_all | solution.py:91
  553.5 5.5 copy-start
  559.6 11.5 %copy-start.3 = (bf16[64,8192,1]{1,0,2:T(8,128)(2,1)S(1)}, bf16[64,8192,1]{1,0,2:T(8,128)(2,1)}, u32[]{:S(2)}) copy-start(bf16[64,8192,1]{1,0,2:T(8,128)(2,1)} %reshape.565) | copy-start | bytes 3145732
  571.1 13.0 %slice-start.2 = ((s8[8388608]{0:T(1024)(128)(4,1)}), s8[4194304]{0:T(1024)(128)(4,1)S(1)}, s32[]{:S(2)}) async-start(s8[8388608]{0:T(1024)(128)(4,1)} %bitcast.119), calls=%async_computation.11 | async-start | bytes 8388608
  577.5 6.6 slice-start.3
  617.8 11.6 %copy-start.2 = (bf16[64,8192,1]{1,0,2:T(8,128)(2,1)S(1)}, bf16[64,8192,1]{1,0,2:T(8,128)(2,1)}, u32[]{:S(2)}) copy-start(bf16[64,8192,1]{1,0,2:T(8,128)(2,1)} %reshape.562) | copy-start | bytes 3145732
  629.4 12.9 %slice-start.4 = ((s8[8388608]{0:T(1024)(128)(4,1)}), s8[4194304]{0:T(1024)(128)(4,1)S(1)}, s32[]{:S(2)}) async-start(s8[8388608]{0:T(1024)(128)(4,1)} %bitcast.121), calls=%async_computation.13 | async-start | bytes 8388608
  635.7 6.6 slice-start.5
  674.7 5.2 slice-start
  674.8 5.8 slice-start.1
Sparse Core Ops, SparseCore 0:
  9.8 50.9 all-gather.9
  63.2 58.1 all-gather.11
  123.8 89.7 all-gather.7
  215.9 151.6 all-gather.13
  369.1 146.8 all-gather.5
where the time goes:
time: 692 us; the launch traced here: 689 us
  waiting for transfers between devices  447 us (65%)
  local copies, waits for them, and re-layouts  93.9 us (14%)
  blocking collectives  62.7 us (9%)
  matrix products  39.8 us (6%)
  starting transfers between devices  19.1 us (3%)
  other arithmetic  13.8 us (2%)
  between operations  13.5 us (2%)
    all_gather x1, waiting for transfers between devices, shards(): features = lax.all_gather(step_inputs, 'tp', axis=2, tiled=True)  131 us
    all_gather x1, waiting for transfers between devices, shards(): lax.all_gather(w_out, 'rep', axis=0, tiled=True)  124 us
    all_gather x1, waiting for transfers between devices, shards(): lax.all_gather(w_query, 'rep', axis=0, tiled=True)  83.9 us
    all_gather x2, blocking collectives, shards(): joined = lax.all_gather(attention, 'tp', axis=1, tiled=True)  62.7 us
    all_gather x1, waiting for transfers between devices, shards(): lax.all_gather(w_value, 'rep', axis=0, tiled=True)  52.3 us
    all_gather x1, waiting for transfers between devices, shards(): lax.all_gather(w_key, 'rep', axis=0, tiled=True)  51.5 us
    all_to_all x2, local copies, waits for them, and re-layouts, shards(): lax.all_to_all(gathered_query, 'tp', split_axis=1, concat_axis=0, tiled=T...  22.9 us
  transfers between devices with their start and end apart: 9, of which 5 were waited for; matrix products, arithmetic and copies ran while one was open for 16% of the time, Pallas kernels for 0%

commit v1 on v0

v1 whole, which is shorter than its diff:
```python
import functools

import jax
import jax.numpy as jnp
from jax import lax
from jax.experimental import pallas as pl
from jax.experimental.pallas import tpu as pltpu
from jax.sharding import Mesh, PartitionSpec as P

HD = 128
STEPS = 2
GROUP = 4

VMEM_BYTES = 60 * 1024 * 1024

norm_eps = 1e-05
rope_base = 500000.0

AXES = ("zh", "y1", "y0", "c", "x1", "x0", "zl")
REP = ("zh", "y1", "y0", "c")
TP = ("x1", "x0", "zl")
SPLIT = ("y1", "y0")
REST = "zh"


def pairs_of(change):
    pairs = []
    for device in range(128):
        bits = {axis: (device >> (6 - i)) & 1 for i, axis in enumerate(AXES)}
        moved = change(dict(bits))
        pairs.append((device, sum(moved[axis] << (6 - i) for i, axis in enumerate(AXES))))
    return pairs


def flipped(axis):
    def change(bits):
        bits[axis] ^= 1
        return bits

    return change


def permute(block, change):
    return lax.ppermute(block, AXES, pairs_of(change))


def shifted(high, low, by):
    def change(bits):
        place = (bits[high] * 2 + bits[low] + by) % 4
        bits[high], bits[low] = place >> 1, place & 1
        return bits

    return change


def ring_gather(block, pair, high, low):
    half = block.shape[0] // 2
    up, down = shifted(high, low, 1), shifted(high, low, -1)
    mate = permute(block, flipped(pair))
    own_side = [block, permute(block, up), permute(block, down)]
    mate_side = [mate, permute(mate, up), permute(mate, down)]
    for side in (own_side, mate_side):
        side.append(permute(side[1][:half], up))
        side.append(permute(side[2][half:], down))
    return own_side + mate_side


def ring_places(mine):
    return [mine, (mine + 3) % 4, (mine + 1) % 4, (mine + 2) % 4]


def turns(positions):
    half = HD // 2
    ladder = jnp.arange(half).astype(jnp.float32)
    frequency = jnp.power(jnp.float32(rope_base), -2.0 * ladder / HD)
    angles = positions.astype(jnp.float32)[:, None] * frequency[None, :]
    cosine, sine = jnp.cos(angles), jnp.sin(angles)
    return jnp.concatenate([cosine, cosine], axis=-1), jnp.concatenate([-sine, sine], axis=-1)


def settle(place, blocks, spots, sems):
    ring, pair = place[2], place[3]
    half = blocks[3].shape[0]
    copies = []
    for side in range(2):
        for k, spot in enumerate(ring_places(ring)):
            index = spot * 2 + (pair ^ side)
            first = side * 5 + k
            for low in range(1 if k < 3 else 2):
                rows = pl.ds(low * half, half if k == 3 else 2 * half)
                for source, target, sem in spots(blocks[first + low], index, rows, first + low):
                    copies.append(pltpu.make_async_copy(source, target, sems.at[sem]))
    for copy in copies:
        copy.start()
    return copies


def pack_kernel(query, key, value, out_weight, inputs, packed):
    rows = inputs.shape[0] // 8
    deep = out_weight.shape[0]
    wide, narrow = query.shape[1] // 8, key.shape[1] // 8
    width = inputs.shape[1]
    quarter = query.shape[0] // 4
    strip = width // 4
    for t in range(8):
        packed[t, :rows] = inputs[t * rows : (t + 1) * rows]
        packed[t, rows : rows + deep] = out_weight[:, t * width : (t + 1) * width]
        first = rows + deep
        for q in range(4):
            part = slice(q * quarter, (q + 1) * quarter)
            begin = q * strip
            for n in range(wide // strip):
                packed[t, first + n * quarter : first + (n + 1) * quarter, begin : begin + strip] = query[
                    part, t * wide + n * strip : t * wide + (n + 1) * strip
                ]
            last = slice(first + wide // strip * quarter, first + (wide // strip + 1) * quarter)
            packed[t, last, begin : begin + narrow] = key[part, t * narrow : (t + 1) * narrow]
            packed[t, last, begin + narrow : begin + strip] = value[part, t * narrow : (t + 1) * narrow]


def pack(query, key, value, out_weight, inputs):
    batch, width = inputs.shape
    depth = query.shape[0]
    rows = batch // 8 + out_weight.shape[0] + depth * 3 // 4
    vmem = pl.BlockSpec(memory_space=pltpu.VMEM)
    return pl.pallas_call(
        pack_kernel,
        out_shape=jax.ShapeDtypeStruct((8, rows, width), jnp.bfloat16),
        in_specs=[vmem] * 5,
        out_specs=vmem,
        compiler_params=pltpu.CompilerParams(vmem_limit_bytes=VMEM_BYTES),
    )(query, key, value, out_weight, inputs)


def unpack_kernel(packed, gain, normed, weight, out_weight):
    rows, width = normed.shape[2:]
    deep = out_weight.shape[0] // 8
    depth = weight.shape[0] // 8
    quarter, strip = depth // 4, width // 4
    total = None
    for t in range(8):
        values = packed[t, :rows].astype(jnp.float32)
        squares = jnp.sum(values * values, axis=-1, keepdims=True)
        total = squares if total is None else total + squares
    factor = lax.rsqrt(total / (8 * width) + norm_eps)
    for t in range(8):
        values = packed[t, :rows].astype(jnp.float32) * factor
        values = values * gain[t : t + 1, :].astype(jnp.float32)
        normed[t & 3, t >> 2] = values.astype(jnp.bfloat16)
        out_weight[t * deep : (t + 1) * deep] = packed[t, rows : rows + deep]
        first = rows + deep
        for n in range(3):
            for q in range(4):
                begin = t * depth + q * quarter
                weight[begin : begin + quarter, n * strip : (n + 1) * strip] = packed[
                    t, first + n * quarter : first + (n + 1) * quarter, q * strip : (q + 1) * strip
                ]


def unpack(packed, gain, rows, deep, depth):
    width = packed.shape[2]
    vmem = pl.BlockSpec(memory_space=pltpu.VMEM)
    return pl.pallas_call(
        unpack_kernel,
        out_shape=[
            jax.ShapeDtypeStruct((4, 2, rows, width), jnp.bfloat16),
            jax.ShapeDtypeStruct((8 * depth, width * 3 // 4), jnp.bfloat16),
            jax.ShapeDtypeStruct((8 * deep, width), jnp.bfloat16),
        ],
        in_specs=[vmem] * 2,
        out_specs=[vmem] * 3,
        compiler_params=pltpu.CompilerParams(vmem_limit_bytes=VMEM_BYTES),
    )(packed, gain)


def partial_kernel(place, *refs):
    blocks, weights, outs, acts, held, sums, sems, more = refs[:10], refs[10:14], refs[14:18], *refs[18:]

    width = blocks[0].shape[3]
    half = weights[0].shape[0]

    def spots(block, index, part, sem):
        return [
            (block.at[:, k], acts.at[part, index, :, pl.ds(k * width, width)], (sem, k)) for k in range(2)
        ]

    copies = settle(place, blocks, spots, sems)
    ring, core, rest = place[0], place[1], place[4]
    for i in range(4):
        first = ((rest ^ (i >> 1)) * 2 + (core ^ (i & 1))) * half
        copies.append(
            pltpu.make_async_copy(weights[i], held.at[pl.ds(pl.multiple_of(first, half), half)], more.at[i])
        )
        copies[-1].start()
    for copy in copies:
        copy.wait()
    batch = outs[0].shape[0]
    product = jnp.dot(acts[...].reshape(4 * batch, 2 * width), held[...], preferred_element_type=jnp.float32)
    sums[...] = product.astype(sums.dtype).reshape(sums.shape)
    for k in range(4):
        outs[k][...] = sums[ring ^ k]


def partial_products(place, blocks, weights):
    _, _, rows, width = blocks[0].shape
    depth, columns = weights[0].shape
    vmem = pl.BlockSpec(memory_space=pltpu.VMEM)
    return pl.pallas_call(
        partial_kernel,
        out_shape=[jax.ShapeDtypeStruct((8 * rows, columns), jnp.bfloat16)] * 4,
        in_specs=[pl.BlockSpec(memory_space=pltpu.SMEM)] + [pl.BlockSpec(memory_space=pl.ANY)] * 14,
        out_specs=[vmem] * 4,
        scratch_shapes=[
            pltpu.VMEM((4, 8, rows, 2 * width), jnp.bfloat16),
            pltpu.VMEM((4 * depth, columns), jnp.bfloat16),
            pltpu.VMEM((4, 8 * rows, columns), jnp.bfloat16),
            pltpu.SemaphoreType.DMA((10, 2)),
            pltpu.SemaphoreType.DMA((4,)),
        ],
        compiler_params=pltpu.CompilerParams(vmem_limit_bytes=VMEM_BYTES),
        cost_estimate=pl.CostEstimate(
            flops=2 * 32 * rows * 2 * width * columns, bytes_accessed=8 * 1024 * 1024, transcendentals=0
        ),
    )(place, *blocks, *weights)


def output_kernel(place, *refs):
    blocks, weight, out, acts, held, sems, more = refs[:10], *refs[10:]
    width = blocks[0].shape[1]

    def spots(block, index, part, sem):
        columns = pl.ds(pl.multiple_of(index * width, width), width)
        return [(block, acts.at[part, columns], (sem,))]

    copies = settle(place, blocks, spots, more)
    for group in range(8):
        rows = pl.ds(group * width, width)
        copies.append(pltpu.make_async_copy(weight.at[rows], held.at[rows], sems.at[group]))
        copies[-1].start()
    for copy in copies:
        copy.wait()
    out[...] = jnp.dot(acts[...], held[...], preferred_element_type=jnp.float32).astype(out.dtype)


def output_product(place, blocks, weight):
    batch, width = blocks[0].shape
    columns = weight.shape[1]
    return pl.pallas_call(
        output_kernel,
        out_shape=jax.ShapeDtypeStruct((batch, columns), jnp.bfloat16),
        in_specs=[pl.BlockSpec(memory_space=pltpu.SMEM)] + [pl.BlockSpec(memory_space=pl.ANY)] * 11,
        out_specs=pl.BlockSpec(memory_space=pltpu.VMEM),
        scratch_shapes=[
            pltpu.VMEM((batch, 8 * width), jnp.bfloat16),
            pltpu.VMEM((8 * width, columns), jnp.bfloat16),
            pltpu.SemaphoreType.DMA((8,)),
            pltpu.SemaphoreType.DMA((10,)),
        ],
        compiler_params=pltpu.CompilerParams(vmem_limit_bytes=VMEM_BYTES),
        cost_estimate=pl.CostEstimate(
            flops=2 * batch * 8 * width * columns, bytes_accessed=10 * 1024 * 1024, transcendentals=0
        ),
    )(place, *blocks, weight)


def tie(block, *others):
    anywhere = pl.BlockSpec(memory_space=pl.ANY)

    def kernel(*refs):
        pass

    return pl.pallas_call(
        kernel,
        out_shape=jax.ShapeDtypeStruct(block.shape, block.dtype),
        in_specs=[anywhere] * (1 + len(others)),
        out_specs=anywhere,
        input_output_aliases={0: 0},
    )(block, *others)


def attention_kernel(lengths, *refs):
    parts, (cosine, sine, key, value, out), scratch = refs[:4], refs[4:9], refs[9:]
    queries, fresh_keys, fresh_values, scores, sums = scratch
    rows, heads, _ = queries.shape
    chunk = key.shape[0]
    step = pl.program_id(0)

    @pl.when(step == 0)
    def _():
        projected = parts[0][...].astype(jnp.float32)
        for part in parts[1:]:
            projected = projected + part[...].astype(jnp.float32)

        def head(k):
            return projected[:, k * HD : (k + 1) * HD]

        def turned(vectors):
            moved = vectors * cosine[...] + pltpu.roll(vectors, HD // 2, 1) * sine[...]
            return moved.astype(jnp.bfloat16).astype(jnp.float32)

        for k in range(GROUP):
            query = turned(head(k))
            for s in range(STEPS):
                queries[:, s * GROUP + k, :] = query[s * rows : (s + 1) * rows]
        fresh_key = turned(head(GROUP))
        fresh_value = head(GROUP + 1).astype(jnp.bfloat16).astype(jnp.float32)
        for s in range(STEPS):
            fresh_keys[s] = fresh_key[s * rows : (s + 1) * rows]
            fresh_values[s] = fresh_value[s * rows : (s + 1) * rows]

    scale = HD ** (-0.5)
    here = pl.ds(pl.multiple_of(step * chunk, chunk), chunk)
    query = queries[here].reshape(chunk * heads, HD)
    for r in range(chunk):
        scores[r * heads : (r + 1) * heads] = lax.dot_general(
            query[r * heads : (r + 1) * heads].astype(jnp.bfloat16),
            key[r],
            (((1,), (1,)), ((), ())),
            preferred_element_type=jnp.float32,
        )
    cached = scores[...] * scale
    spot = lax.broadcasted_iota(jnp.int32, cached.shape, 1)
    cached = jnp.where(spot < lengths[...], cached, -jnp.inf)
    at_step = lax.broadcasted_iota(jnp.int32, (chunk * heads, 1), 0) % heads // GROUP

    def repeated(vectors):
        return jnp.broadcast_to(vectors[:, None, :], (chunk, heads, HD)).reshape(chunk * heads, HD)

    new = []
    highest = jnp.max(cached, axis=-1, keepdims=True)
    for s in range(STEPS):
        score = jnp.sum(query * repeated(fresh_keys[s, here]), axis=-1, keepdims=True) * scale
        new.append(jnp.where(at_step >= s, score, -jnp.inf))
        highest = jnp.maximum(highest, new[s])
    cached = jnp.exp(cached - highest)
    new = [jnp.exp(score - highest) for score in new]
    total = jnp.sum(cached, axis=-1, keepdims=True) + new[0] + new[1]
    share = 1.0 / total
    scores[...] = cached * share
    result = None
    for s in range(STEPS):
        prob = (new[s] * share).astype(jnp.bfloat16).astype(jnp.float32)
        term = prob * repeated(fresh_values[s, here])
        result = term if result is None else result + term
    result = result.reshape(chunk, heads, HD)
    for r in range(chunk):
        prob = scores[r * heads : (r + 1) * heads].astype(jnp.bfloat16)
        sums[step * chunk + r] = result[r] + jnp.dot(prob, value[r], preferred_element_type=jnp.float32)

    @pl.when(step == pl.num_programs(0) - 1)
    def _():
        for s in range(STEPS):
            for k in range(GROUP):
                out[s * rows : (s + 1) * rows, k * HD : (k + 1) * HD] = sums[:, s * GROUP + k, :].astype(out.dtype)


def attention_of(parts, cosine, sine, key_cache, value_cache, lengths, chunk=8):
    batch, columns = parts[0].shape
    rows, spots, _ = key_cache.shape
    heads = STEPS * GROUP
    whole = lambda *shape: pl.BlockSpec(shape, lambda i: (0,) * len(shape))
    cache = pl.BlockSpec((chunk, spots, HD), lambda i: (i, 0, 0))
    return pl.pallas_call(
        attention_kernel,
        grid=(rows // chunk,),
        out_shape=jax.ShapeDtypeStruct((batch, GROUP * HD), jnp.bfloat16),
        in_specs=[pl.BlockSpec((chunk * heads, 1), lambda i: (i, 0))]
        + [whole(batch, columns)] * 4
        + [whole(batch, HD), whole(batch, HD), cache, cache],
        out_specs=whole(batch, GROUP * HD),
        scratch_shapes=[
            pltpu.VMEM((rows, heads, HD), jnp.float32),
            pltpu.VMEM((STEPS, rows, HD), jnp.float32),
            pltpu.VMEM((STEPS, rows, HD), jnp.float32),
            pltpu.VMEM((chunk * heads, spots), jnp.float32),
            pltpu.VMEM((rows, heads, HD), jnp.float32),
        ],
        compiler_params=pltpu.CompilerParams(
            vmem_limit_bytes=VMEM_BYTES, dimension_semantics=("arbitrary",)
        ),
        cost_estimate=pl.CostEstimate(
            flops=4 * rows * heads * spots * HD,
            bytes_accessed=4 * rows * spots * HD,
            transcendentals=rows * heads * spots,
        ),
    )(jnp.repeat(lengths, heads)[:, None], *parts, cosine, sine, key_cache, value_cache)


def shards(step_inputs, norm_gain, w_query, w_key, w_value, w_out, key_cache, value_cache, lengths):
    steps, rows, width = step_inputs.shape
    batch = steps * rows
    place = jnp.stack(
        [
            lax.axis_index(("y1", "y0")),
            lax.axis_index("c"),
            lax.axis_index(("x1", "x0")),
            lax.axis_index("zl"),
            lax.axis_index("zh"),
        ]
    ).astype(jnp.int32)

    packed = pack(w_query, w_key, w_value, w_out, step_inputs.reshape(batch, width))
    packed = lax.all_to_all(packed, TP, 0, 0, tiled=True)
    normed, mine, out_mine = unpack(
        packed, norm_gain.reshape(8, width), batch // 8, w_out.shape[0], w_query.shape[0]
    )
    far = permute(mine, flipped(REST))
    weights = (mine, permute(mine, flipped("c")), far, permute(far, flipped("c")))
    out_weight = lax.all_gather(out_mine, REP, axis=0, tiled=True)

    moved = lax.all_to_all(normed, SPLIT, 0, 0, tiled=True)
    gathered = ring_gather(moved, "zl", "x1", "x0")
    partial = partial_products(place, gathered, weights)
    changes = [flipped(SPLIT[0]), flipped(SPLIT[1])]
    parts = [
        partial[0],
        permute(partial[3], lambda bits: changes[0](changes[1](bits))),
        permute(partial[2], changes[0]),
        permute(partial[1], changes[1]),
    ]
    positions = (lengths[None, :] + jnp.arange(steps)[:, None]).reshape(batch)
    cosine, sine = turns(positions)
    attention = attention_of(
        parts, cosine, sine, key_cache[:, 0], value_cache[:, 0], lengths
    )
    joined = ring_gather(attention, "zl", "x1", "x0")
    result = output_product(place, joined, out_weight)
    return result.reshape(steps, rows, width)


def solution(mesh):
    fine = Mesh(mesh.devices.reshape((2,) * 7), AXES)
    in_specs = (
        P(None, REP, TP),
        P(),
        P(AXES, None),
        P(AXES, None),
        P(AXES, None),
        P(AXES, None),
        P(REP, TP, None, None),
        P(REP, TP, None, None),
        P(REP),
    )
    out_specs = P(None, REP, TP)
    return jax.shard_map(shards, mesh=fine, in_specs=in_specs, out_specs=out_specs, check_vma=False)
```

time: 692 us -> 161 us (0.23)
  waiting for transfers between devices: 447 us -> 58.7 us
  local copies, waits for them, and re-layouts: 93.9 us -> 5.46 us
  blocking collectives: 62.7 us -> 13.1 us
  matrix products: 39.8 us -> 0 us
  Pallas kernels: 0 us -> 30.1 us
  starting transfers between devices: 19.1 us -> 36.3 us
  other arithmetic: 13.8 us -> 1.07 us
    all_gather x5 -> x1, waiting for transfers between devices: 443 us -> 0.02 us  [shards(): out_weight = lax.all_gather(out_mine, REP, axis=0, tiled=True)]
    all_gather x2 -> x0, blocking collectives: 62.7 us -> none  [shards(): joined = lax.all_gather(attention, 'tp', axis=1, tiled=True)]
    all_to_all x5 -> x0, local copies, waits for them, and re-layouts: 41.5 us -> none  [the longest x2 22.9 us: shards(): lax.all_to_all(gathered_query, 'tp', split_axis=1, concat_axis=0, tiled=T...]
    dot_general x15 -> x0, matrix products: 39.8 us -> none  [the longest x2 12.4 us: shards(): jnp.dot(normed, query_weight, preferred_element_type=jnp.float32)]
    ppermute x0 -> x24, waiting for transfers between devices: none -> 36.3 us  [permute(): return lax.ppermute(block, AXES, pairs_of(change))]
    all_gather x4 -> x0, local copies, waits for them, and re-layouts: 31.7 us -> none  [the longest x1 12 us: shards(): lax.all_gather(w_query, 'rep', axis=0, tiled=True)]
    ppermute x0 -> x24, starting transfers between devices: none -> 30.5 us  [permute(): return lax.ppermute(block, AXES, pairs_of(change))]
    pallas_call x0 -> x5, Pallas kernels: none -> 30.1 us  [the longest x1 12 us: attention_of(): pl.pallas_call(attention_kernel, grid=(rows // chunk,), out_shape=jax.Sha...]
  transfers between devices with their start and end apart: 9 -> 26, of which waited for: 5 -> 12; matrix products, arithmetic and copies ran while one was open for 16% -> 3% of each run, Pallas kernels for 0% -> 12%
where the time goes in v1:
time: 161 us; the launch traced here: 158 us
  waiting for transfers between devices  58.7 us (36%)
  starting transfers between devices  36.3 us (23%)
  Pallas kernels  30.1 us (19%)
  between operations  13.7 us (9%)
  blocking collectives  13.1 us (8%)
  local copies, waits for them, and re-layouts  5.46 us (3%)
    ppermute x24, waiting for transfers between devices, permute(): return lax.ppermute(block, AXES, pairs_of(change))  36.3 us
    ppermute x24, starting transfers between devices, permute(): return lax.ppermute(block, AXES, pairs_of(change))  30.5 us
    all_to_all x1, waiting for transfers between devices, shards(): packed = lax.all_to_all(packed, TP, 0, 0, tiled=True)  22.3 us
    all_to_all x1, blocking collectives, shards(): moved = lax.all_to_all(normed, SPLIT, 0, 0, tiled=True)  13.1 us
    pallas_call x1, Pallas kernels, attention_of(): pl.pallas_call(attention_kernel, grid=(rows // chunk,), out_shape=jax.Sha...  12 us
    pallas_call x1, Pallas kernels, output_product(): pl.pallas_call(output_kernel, out_shape=jax.ShapeDtypeStruct((batch, colu...  6.47 us
    pallas_call x1, Pallas kernels, partial_products(): pl.pallas_call(partial_kernel, out_shape=[jax.ShapeDtypeStruct((8 * rows,...  6.24 us
    all_to_all x1, starting transfers between devices, shards(): packed = lax.all_to_all(packed, TP, 0, 0, tiled=True)  5.74 us
  transfers between devices with their start and end apart: 26, of which 12 were waited for; matrix products, arithmetic and copies ran while one was open for 3% of the time, Pallas kernels for 12%

profile of v1, /device:TPU:0, one launch (start us, length us, event | category | flops | bytes accessed | tf_op | source)
XLA Modules:
  0.0 158.3 jit_solution(12533149643462214679)
XLA Ops:
  6.5 2.7 %shard_map.91 = bf16[8,96,1024]{2,1,0:T(8,128)(2,1)} custom-call(bf16[64,4096]{1,0:T(8,128)(2,1)} %query.1, bf16[64,1024]{1,0:T(8,128)(2,1)} %key.1, bf16[64,1024]{1,0:T(8,128)(2,1)} %value.1, bf16[32,8192]{1,0:T(8,128)(2,1)} %out_weight.1, bf16[128,1024]{1,0:T(8,128)(2,1)} %bitcast.11), custom_call_target="tpu_custom_call" | custom-call | tf_op jit(solution)/shard_map/pallas_call | solution.py:126
  9.2 5.7 %all-to-all-start = ((bf16[8,96,1024]{2,1,0:T(8,128)(2,1)}), bf16[8,96,1024]{2,1,0:T(8,128)(2,1)S(1)}, u32[]{:S(2)}, u32[]{:S(2)}) async-start(bf16[8,96,1024]{2,1,0:T(8,128)(2,1)} %shard_map.91), calls=%async_computation | async-start | bytes 3145728 | tf_op jit(solution)/shard_map/all_to_all | solution.py:403
  15.0 0.0 all-gather.2.cloned.1.call-start
  15.0 1.3 reshape.32.gain
  16.3 22.3 %all-to-all-done.packed = bf16[8,96,1024]{2,1,0:T(8,128)(2,1)S(1)} async-done(((bf16[8,96,1024]{2,1,0:T(8,128)(2,1)}), bf16[8,96,1024]{2,1,0:T(8,128)(2,1)S(1)}, u32[]{:S(2)}, u32[]{:S(2)}) %all-to-all-start) | async-done | bytes 1572896 | tf_op jit(solution)/shard_map/all_to_all | solution.py:403
  38.7 1.2 copy-done
  39.8 2.6 %shard_map.92 = (bf16[4,2,16,1024]{3,2,1,0:T(8,128)(2,1)}, bf16[512,768]{1,0:T(8,128)(2,1)}, bf16[256,1024]{1,0:T(8,128)(2,1)}) custom-call(bf16[8,96,1024]{2,1,0:T(8,128)(2,1)} %copy-done, bf16[8,1024]{1,0:T(8,128)(2,1)} %reshape.32.gain), custom_call_target="tpu_custom_call" | custom-call | tf_op jit(solution)/shard_map/pallas_call | solution.py:163
  42.5 0.0 all-gather.2.cloned.1.call-update
  42.5 3.7 %collective-permute-start.10 = (bf16[512,768]{1,0:T(8,128)(2,1)}, bf16[512,768]{1,0:T(8,128)(2,1)S(1)}, u32[]{:S(2)}, u32[]{:S(2)}) collective-permute-start(bf16[512,768]{1,0:T(8,128)(2,1)} %get-tuple-element.13.refs_10_), channel_id=1, source_target_pairs={{0,64},{1,65},{2,66},{3,67},{4,68},{5,69},{6,70},{7,71},{8,72},{9,... | collective-permute-start | bytes 2359304 | tf_op jit(solution)/shard_map/ppermute | solution.py:44
  46.2 13.1 %all_to_all.10.refs_0_ = bf16[4,2,16,1024]{3,2,1,0:T(8,128)(2,1)S(1)} all-to-all(bf16[4,2,16,1024]{3,2,1,0:T(8,128)(2,1)} %get-tuple-element.12), channel_id=1, replica_groups=mesh['zh'=2,'y1'=2,'y0'=2,'c'=2,'x1'=2,'x0'=2,'zl'=2] {'y1','y0'}, dimensions={0} | all-to-all | bytes 524288 | tf_op jit(solution)/shard_map/all_to_all | solution.py:411
  59.2 0.0 collective-permute-start.4
  59.2 0.0 collective-permute-start
  59.2 0.1 collective-permute-start.9
  59.3 11.1 %collective-permute-done.10.refs_12_ = bf16[512,768]{1,0:T(8,128)(2,1)S(1)} collective-permute-done((bf16[512,768]{1,0:T(8,128)(2,1)}, bf16[512,768]{1,0:T(8,128)(2,1)S(1)}, u32[]{:S(2)}, u32[]{:S(2)}) %collective-permute-start.10) | collective-permute-done | bytes 786464 | tf_op jit(solution)/shard_map/ppermute | solution.py:44
  70.5 0.0 collective-permute-start.11
  70.5 0.0 collective-permute-start.1
  70.5 3.0 %collective-permute-done.4.refs_5_ = bf16[4,2,16,1024]{3,2,1,0:T(8,128)(2,1)S(1)} collective-permute-done((bf16[4,2,16,1024]{3,2,1,0:T(8,128)(2,1)S(1)}, bf16[4,2,16,1024]{3,2,1,0:T(8,128)(2,1)S(1)}, u32[]{:S(2)}, u32[]{:S(2)}) %collective-permute-start.4) | collective-permute-done | bytes 262176 | tf_op jit(solution)/shard_map/ppermute | solution.py:44
  73.5 0.0 collective-permute-start.5
  73.5 0.0 collective-permute-done.refs_1_
  73.5 3.2 %collective-permute-start.6 = (bf16[4,2,16,1024]{3,2,1,0:T(8,128)(2,1)S(1)}, bf16[4,2,16,1024]{3,2,1,0:T(8,128)(2,1)S(1)}, u32[]{:S(2)}, u32[]{:S(2)}) collective-permute-start(bf16[4,2,16,1024]{3,2,1,0:T(8,128)(2,1)S(1)} %collective-permute-done.4.refs_5_), channel_id=1, source_target_pairs={{0,6},{1,7},{2,0},{3,1},{4,2},{5,3},{6,4},{7,5},{8,14},{9,15},{10,... | collective-permute-start | bytes 786440 | tf_op jit(solution)/shard_map/ppermute | solution.py:44
  76.7 2.8 %collective-permute-done.1.refs_2_ = bf16[4,2,16,1024]{3,2,1,0:T(8,128)(2,1)S(1)} collective-permute-done((bf16[4,2,16,1024]{3,2,1,0:T(8,128)(2,1)S(1)}, bf16[4,2,16,1024]{3,2,1,0:T(8,128)(2,1)S(1)}, u32[]{:S(2)}, u32[]{:S(2)}) %collective-permute-start.1) | collective-permute-done | bytes 262176 | tf_op jit(solution)/shard_map/ppermute | solution.py:44
  79.6 0.0 collective-permute-start.2
  79.6 1.5 collective-permute-done.5.refs_6_
  81.1 1.9 %collective-permute-start.3 = (bf16[2,2,16,1024]{3,2,1,0:T(8,128)(2,1)S(1)}, bf16[2,2,16,1024]{3,2,1,0:T(8,128)(2,1)}, u32[]{:S(2)}, u32[]{:S(2)}) collective-permute-start(bf16[2,2,16,1024]{3,2,1,0:T(8,128)(2,1)S(1)} %slice.33), channel_id=1, source_target_pairs={{0,6},{1,7},{2,0},{3,1},{4,2},{5,3},{6,4},{7,5},{8,14},{9,15},{10,... | collective-permute-start | bytes 393224 | tf_op jit(solution)/shard_map/ppermute | solution.py:44
  82.9 2.3 %collective-permute-done.6.refs_7_ = bf16[4,2,16,1024]{3,2,1,0:T(8,128)(2,1)S(1)} collective-permute-done((bf16[4,2,16,1024]{3,2,1,0:T(8,128)(2,1)S(1)}, bf16[4,2,16,1024]{3,2,1,0:T(8,128)(2,1)S(1)}, u32[]{:S(2)}, u32[]{:S(2)}) %collective-permute-start.6) | collective-permute-done | bytes 262176 | tf_op jit(solution)/shard_map/ppermute | solution.py:44
  85.2 0.0 collective-permute-start.7
  85.2 0.5 collective-permute-done.2.refs_3_
  85.7 2.8 %collective-permute-start.8 = (bf16[2,2,16,1024]{3,2,1,0:T(8,128)(2,1)S(1)}, bf16[2,2,16,1024]{3,2,1,0:T(8,128)(2,1)}, u32[]{:S(2)}, u32[]{:S(2)}) collective-permute-start(bf16[2,2,16,1024]{3,2,1,0:T(8,128)(2,1)S(1)} %slice.35), channel_id=1, source_target_pairs={{0,6},{1,7},{2,0},{3,1},{4,2},{5,3},{6,4},{7,5},{8,14},{9,15},{10,... | collective-permute-start | bytes 393224 | tf_op jit(solution)/shard_map/ppermute | solution.py:44
  88.5 0.1 convert_element_type.18
  88.6 0.6 stack.23.place
  89.3 2.2 %collective-permute-done.7.refs_8_ = bf16[2,2,16,1024]{3,2,1,0:T(8,128)(2,1)} collective-permute-done((bf16[2,2,16,1024]{3,2,1,0:T(8,128)(2,1)S(1)}, bf16[2,2,16,1024]{3,2,1,0:T(8,128)(2,1)}, u32[]{:S(2)}, u32[]{:S(2)}) %collective-permute-start.7) | collective-permute-done | bytes 131104 | tf_op jit(solution)/shard_map/ppermute | solution.py:44
  91.5 0.0 collective-permute-done.11.refs_13_
  91.5 6.2 %shard_map.93 = (bf16[128,768]{1,0:T(8,128)(2,1)}, bf16[128,768]{1,0:T(8,128)(2,1)}, bf16[128,768]{1,0:T(8,128)(2,1)}, bf16[128,768]{1,0:T(8,128)(2,1)}) custom-call(s32[5]{0:T(128)} %stack.23.place, bf16[4,2,16,1024]{3,2,1,0:T(8,128)(2,1)} %copy-done.5, bf16[4,2,16,1024]{3,2,1,0:T(8,128)(2,1)} %copy-done.14, bf16[4,2,16,1024]{3,2,1,0:T(8,128)(2,1)} %copy-done.15, ...), custom_call_target="tpu_custom_call" | custom-call | flops 1610612736 | bytes 8388608 | tf_op jit(solution)/shard_map/pallas_call | solution.py:208
  97.8 3.1 %collective-permute-start.12 = (bf16[128,768]{1,0:T(8,128)(2,1)}, bf16[128,768]{1,0:T(8,128)(2,1)S(1)}, u32[]{:S(2)}, u32[]{:S(2)}) collective-permute-start(bf16[128,768]{1,0:T(8,128)(2,1)} %get-tuple-element.15), channel_id=1, source_target_pairs={{0,48},{1,49},{2,50},{3,51},{4,52},{5,53},{6,54},{7,55},{8,56},{9,... | collective-permute-start | bytes 589832 | tf_op jit(solution)/shard_map/ppermute | solution.py:44
  100.9 0.6 collective-permute-start.13
  101.5 0.4 collective-permute-start.14
  102.0 0.3 fusion
  102.3 0.1 broadcast_in_dim.2
  102.4 0.8 broadcast_in_dim_reshape.4.lengths
  103.2 0.7 pad_maximum_fusion
  103.9 7.8 %collective-permute-done.12.refs_1_ = bf16[128,768]{1,0:T(8,128)(2,1)S(1)} collective-permute-done((bf16[128,768]{1,0:T(8,128)(2,1)}, bf16[128,768]{1,0:T(8,128)(2,1)S(1)}, u32[]{:S(2)}, u32[]{:S(2)}) %collective-permute-start.12) | collective-permute-done | bytes 196640 | tf_op jit(solution)/shard_map/ppermute | solution.py:44
  111.8 2.3 %collective-permute-done.14.refs_3_ = bf16[128,768]{1,0:T(8,128)(2,1)S(1)} collective-permute-done((bf16[128,768]{1,0:T(8,128)(2,1)}, bf16[128,768]{1,0:T(8,128)(2,1)S(1)}, u32[]{:S(2)}, u32[]{:S(2)}) %collective-permute-start.14) | collective-permute-done | bytes 196640 | tf_op jit(solution)/shard_map/ppermute | solution.py:44
  114.1 0.7 copy-done.8
  114.8 12.0 %shard_map.94.refs_0_ = bf16[128,512]{1,0:T(8,128)(2,1)} custom-call(s32[512,1]{1,0:T(8,128)} %broadcast_in_dim_reshape.4.lengths, bf16[128,768]{1,0:T(8,128)(2,1)} %get-tuple-element.14.refs_0_, bf16[128,768]{1,0:T(8,128)(2,1)} %copy-done.6, bf16[128,768]{1,0:T(8,128)(2,1)} %copy-done.7, bf16[128,768]{1,0:T(8,128)(2,1)} %copy-done.8, ...), custom_call_target="tpu_custom_call" | custom-call | flops 134217728 | bytes 16777216 | tf_op jit(solution)/shard_map/pallas_call | solution.py:363
  126.8 1.4 collective-permute-start.19
  128.2 3.2 %collective-permute-start.16 = (bf16[128,512]{1,0:T(8,128)(2,1)}, bf16[128,512]{1,0:T(8,128)(2,1)S(1)}, u32[]{:S(2)}, u32[]{:S(2)}) collective-permute-start(bf16[128,512]{1,0:T(8,128)(2,1)} %shard_map.94.refs_0_), channel_id=1, source_target_pairs={{0,6},{1,7},{2,0},{3,1},{4,2},{5,3},{6,4},{7,5},{8,14},{9,15},{10,... | collective-permute-start | bytes 393224 | tf_op jit(solution)/shard_map/ppermute | solution.py:44
  131.4 0.6 collective-permute-done.19.refs_5_
  132.0 0.0 collective-permute-start.20
  132.0 3.4 %collective-permute-start.21 = (bf16[128,512]{1,0:T(8,128)(2,1)S(1)}, bf16[128,512]{1,0:T(8,128)(2,1)S(1)}, u32[]{:S(2)}, u32[]{:S(2)}) collective-permute-start(bf16[128,512]{1,0:T(8,128)(2,1)S(1)} %collective-permute-done.19.refs_5_), channel_id=1, source_target_pairs={{0,6},{1,7},{2,0},{3,1},{4,2},{5,3},{6,4},{7,5},{8,14},{9,15},{10,... | collective-permute-start | bytes 393224 | tf_op jit(solution)/shard_map/ppermute | solution.py:44
  135.4 0.0 collective-permute-done.15.refs_1_
  135.4 0.1 collective-permute-start.17
  135.5 0.0 collective-permute-done.16.refs_2_
  135.5 3.3 %collective-permute-start.18 = (bf16[64,512]{1,0:T(8,128)(2,1)S(1)}, bf16[64,512]{1,0:T(8,128)(2,1)S(1)}, u32[]{:S(2)}, u32[]{:S(2)}) collective-permute-start(bf16[64,512]{1,0:T(8,128)(2,1)S(1)} %slice.37), channel_id=1, source_target_pairs={{0,6},{1,7},{2,0},{3,1},{4,2},{5,3},{6,4},{7,5},{8,14},{9,15},{10,... | collective-permute-start | bytes 196616 | tf_op jit(solution)/shard_map/ppermute | solution.py:44
  138.8 0.0 collective-permute-done.20.refs_6_
  138.8 0.1 collective-permute-start.22
  138.9 0.0 collective-permute-done.21.refs_7_
  138.9 3.3 %collective-permute-start.23 = (bf16[64,512]{1,0:T(8,128)(2,1)S(1)}, bf16[64,512]{1,0:T(8,128)(2,1)S(1)}, u32[]{:S(2)}, u32[]{:S(2)}) collective-permute-start(bf16[64,512]{1,0:T(8,128)(2,1)S(1)} %slice.39), channel_id=1, source_target_pairs={{0,6},{1,7},{2,0},{3,1},{4,2},{5,3},{6,4},{7,5},{8,14},{9,15},{10,... | collective-permute-start | bytes 196616 | tf_op jit(solution)/shard_map/ppermute | solution.py:44
  142.2 0.0 collective-permute-done.17.refs_3_
  142.2 2.1 %collective-permute-done.22.refs_8_ = bf16[64,512]{1,0:T(8,128)(2,1)S(1)} collective-permute-done((bf16[64,512]{1,0:T(8,128)(2,1)S(1)}, bf16[64,512]{1,0:T(8,128)(2,1)S(1)}, u32[]{:S(2)}, u32[]{:S(2)}) %collective-permute-start.22) | collective-permute-done | bytes 65568 | tf_op jit(solution)/shard_map/ppermute | solution.py:44
  144.4 0.0 collective-permute-done.23.refs_9_
  144.4 0.0 all-gather.2.cloned.1.call-done.refs_10_
  144.5 0.5 copy-done.12
  145.0 0.0 copy-done.13
  145.0 6.5 %shard_map.95 = bf16[128,1024]{1,0:T(8,128)(2,1)} custom-call(s32[5]{0:T(128)} %stack.23.place, bf16[128,512]{1,0:T(8,128)(2,1)} %shard_map.94.refs_0_, bf16[128,512]{1,0:T(8,128)(2,1)} %copy-done.1, bf16[128,512]{1,0:T(8,128)(2,1)} %copy-done.2, bf16[64,512]{1,0:T(8,128)(2,1)} %copy-done.10, bf16[64,512]{1,0:T(8,128)(2,1)} %copy-done.11, ...), custom_call_target="tpu_custom_call" | custom-call | flops 1073741824 | bytes 10485760 | tf_op jit(solution)/shard_map/pallas_call | solution.py:248
  (58 shorter events, 0.2 us)
Async XLA Ops:
  6.5 82.0 %copy-start.18 = (s32[64]{0:T(128)S(1)}, s32[64]{0:T(128)}, u32[]{:S(2)}) copy-start(s32[64]{0:T(128)} %param.17) | copy-start | bytes 772
  9.2 29.4 %all-to-all-start = ((bf16[8,96,1024]{2,1,0:T(8,128)(2,1)}), bf16[8,96,1024]{2,1,0:T(8,128)(2,1)S(1)}, u32[]{:S(2)}, u32[]{:S(2)}) async-start(bf16[8,96,1024]{2,1,0:T(8,128)(2,1)} %shard_map.91), calls=%async_computation | async-start | bytes 3145728 | tf_op jit(solution)/shard_map/all_to_all | solution.py:403
  15.0 129.4 %all-gather.2.cloned.1.call-start = ((), (), s32[]{:S(2)}) async-start(), calls=%async_computation.2 | async-start | bytes 8912896 | tf_op jit(solution)/shard_map/all_gather | solution.py:409
  38.7 1.2 copy-start
  42.5 27.9 %collective-permute-start.10 = (bf16[512,768]{1,0:T(8,128)(2,1)}, bf16[512,768]{1,0:T(8,128)(2,1)S(1)}, u32[]{:S(2)}, u32[]{:S(2)}) collective-permute-start(bf16[512,768]{1,0:T(8,128)(2,1)} %get-tuple-element.13.refs_10_), channel_id=1, source_target_pairs={{0,64},{1,65},{2,66},{3,67},{4,68},{5,69},{6,70},{7,71},{8,72},{9,... | collective-permute-start | bytes 2359304 | tf_op jit(solution)/shard_map/ppermute | solution.py:44
  59.2 32.2 %copy-start.5 = (bf16[4,2,16,1024]{3,2,1,0:T(8,128)(2,1)}, bf16[4,2,16,1024]{3,2,1,0:T(8,128)(2,1)S(1)}, u32[]{:S(2)}) copy-start(bf16[4,2,16,1024]{3,2,1,0:T(8,128)(2,1)S(1)} %all_to_all.10.refs_0_) | copy-start | bytes 786436
  59.2 14.2 %collective-permute-start.4 = (bf16[4,2,16,1024]{3,2,1,0:T(8,128)(2,1)S(1)}, bf16[4,2,16,1024]{3,2,1,0:T(8,128)(2,1)S(1)}, u32[]{:S(2)}, u32[]{:S(2)}) collective-permute-start(bf16[4,2,16,1024]{3,2,1,0:T(8,128)(2,1)S(1)} %all_to_all.10.refs_0_), channel_id=1, source_target_pairs={{0,1},{1,0},{2,3},{3,2},{4,5},{5,4},{6,7},{7,6},{8,9},{9,8},{10,11... | collective-permute-start | bytes 786440 | tf_op jit(solution)/shard_map/ppermute | solution.py:44
  59.2 14.2 %collective-permute-start = (bf16[4,2,16,1024]{3,2,1,0:T(8,128)(2,1)S(1)}, bf16[4,2,16,1024]{3,2,1,0:T(8,128)(2,1)S(1)}, u32[]{:S(2)}, u32[]{:S(2)}) collective-permute-start(bf16[4,2,16,1024]{3,2,1,0:T(8,128)(2,1)S(1)} %all_to_all.10.refs_0_), channel_id=1, source_target_pairs={{0,2},{1,3},{2,4},{3,5},{4,6},{5,7},{6,0},{7,1},{8,10},{9,11},{10,... | collective-permute-start | bytes 786440 | tf_op jit(solution)/shard_map/ppermute | solution.py:44
  59.2 30.0 %collective-permute-start.9 = (bf16[512,768]{1,0:T(8,128)(2,1)}, bf16[512,768]{1,0:T(8,128)(2,1)S(1)}, u32[]{:S(2)}, u32[]{:S(2)}) collective-permute-start(bf16[512,768]{1,0:T(8,128)(2,1)} %get-tuple-element.13.refs_10_), channel_id=1, source_target_pairs={{0,8},{1,9},{2,10},{3,11},{4,12},{5,13},{6,14},{7,15},{8,0},{9,1},... | collective-permute-start | bytes 2359304 | tf_op jit(solution)/shard_map/ppermute | solution.py:44
  70.5 21.0 %copy-start.19 = (bf16[512,768]{1,0:T(8,128)(2,1)}, bf16[512,768]{1,0:T(8,128)(2,1)S(1)}, u32[]{:S(2)}) copy-start(bf16[512,768]{1,0:T(8,128)(2,1)S(1)} %collective-permute-done.10.refs_12_) | copy-start | bytes 2359300
  70.5 21.0 %collective-permute-start.11 = (bf16[512,768]{1,0:T(8,128)(2,1)S(1)}, bf16[512,768]{1,0:T(8,128)(2,1)}, u32[]{:S(2)}, u32[]{:S(2)}) collective-permute-start(bf16[512,768]{1,0:T(8,128)(2,1)S(1)} %collective-permute-done.10.refs_12_), channel_id=1, source_target_pairs={{0,8},{1,9},{2,10},{3,11},{4,12},{5,13},{6,14},{7,15},{8,0},{9,1},... | collective-permute-start | bytes 2359304 | tf_op jit(solution)/shard_map/ppermute | solution.py:44
  70.5 9.1 %collective-permute-start.1 = (bf16[4,2,16,1024]{3,2,1,0:T(8,128)(2,1)S(1)}, bf16[4,2,16,1024]{3,2,1,0:T(8,128)(2,1)S(1)}, u32[]{:S(2)}, u32[]{:S(2)}) collective-permute-start(bf16[4,2,16,1024]{3,2,1,0:T(8,128)(2,1)S(1)} %all_to_all.10.refs_0_), channel_id=1, source_target_pairs={{0,6},{1,7},{2,0},{3,1},{4,2},{5,3},{6,4},{7,5},{8,14},{9,15},{10,... | collective-permute-start | bytes 786440 | tf_op jit(solution)/shard_map/ppermute | solution.py:44
  73.5 18.0 %copy-start.21 = (bf16[4,2,16,1024]{3,2,1,0:T(8,128)(2,1)}, bf16[4,2,16,1024]{3,2,1,0:T(8,128)(2,1)S(1)}, u32[]{:S(2)}) copy-start(bf16[4,2,16,1024]{3,2,1,0:T(8,128)(2,1)S(1)} %collective-permute-done.4.refs_5_) | copy-start | bytes 786436
  73.5 7.6 %collective-permute-start.5 = (bf16[4,2,16,1024]{3,2,1,0:T(8,128)(2,1)S(1)}, bf16[4,2,16,1024]{3,2,1,0:T(8,128)(2,1)S(1)}, u32[]{:S(2)}, u32[]{:S(2)}) collective-permute-start(bf16[4,2,16,1024]{3,2,1,0:T(8,128)(2,1)S(1)} %collective-permute-done.4.refs_5_), channel_id=1, source_target_pairs={{0,2},{1,3},{2,4},{3,5},{4,6},{5,7},{6,0},{7,1},{8,10},{9,11},{10,... | collective-permute-start | bytes 786440 | tf_op jit(solution)/shard_map/ppermute | solution.py:44
  73.5 18.0 %copy-start.14 = (bf16[4,2,16,1024]{3,2,1,0:T(8,128)(2,1)}, bf16[4,2,16,1024]{3,2,1,0:T(8,128)(2,1)S(1)}, u32[]{:S(2)}) copy-start(bf16[4,2,16,1024]{3,2,1,0:T(8,128)(2,1)S(1)} %collective-permute-done.refs_1_) | copy-start | bytes 786436
  73.5 11.7 %collective-permute-start.6 = (bf16[4,2,16,1024]{3,2,1,0:T(8,128)(2,1)S(1)}, bf16[4,2,16,1024]{3,2,1,0:T(8,128)(2,1)S(1)}, u32[]{:S(2)}, u32[]{:S(2)}) collective-permute-start(bf16[4,2,16,1024]{3,2,1,0:T(8,128)(2,1)S(1)} %collective-permute-done.4.refs_5_), channel_id=1, source_target_pairs={{0,6},{1,7},{2,0},{3,1},{4,2},{5,3},{6,4},{7,5},{8,14},{9,15},{10,... | collective-permute-start | bytes 786440 | tf_op jit(solution)/shard_map/ppermute | solution.py:44
  79.6 11.9 %copy-start.15 = (bf16[4,2,16,1024]{3,2,1,0:T(8,128)(2,1)}, bf16[4,2,16,1024]{3,2,1,0:T(8,128)(2,1)S(1)}, u32[]{:S(2)}) copy-start(bf16[4,2,16,1024]{3,2,1,0:T(8,128)(2,1)S(1)} %collective-permute-done.1.refs_2_) | copy-start | bytes 786436
  79.6 6.2 %collective-permute-start.2 = (bf16[2,2,16,1024]{3,2,1,0:T(8,128)(2,1)S(1)}, bf16[2,2,16,1024]{3,2,1,0:T(8,128)(2,1)S(1)}, u32[]{:S(2)}, u32[]{:S(2)}) collective-permute-start(bf16[2,2,16,1024]{3,2,1,0:T(8,128)(2,1)S(1)} %slice.32), channel_id=1, source_target_pairs={{0,2},{1,3},{2,4},{3,5},{4,6},{5,7},{6,0},{7,1},{8,10},{9,11},{10,... | collective-permute-start | bytes 393224 | tf_op jit(solution)/shard_map/ppermute | solution.py:44
  81.0 10.5 %copy-start.16 = (bf16[4,2,16,1024]{3,2,1,0:T(8,128)(2,1)}, bf16[4,2,16,1024]{3,2,1,0:T(8,128)(2,1)S(1)}, u32[]{:S(2)}) copy-start(bf16[4,2,16,1024]{3,2,1,0:T(8,128)(2,1)S(1)} %collective-permute-done.5.refs_6_) | copy-start | bytes 786436
  81.1 8.2 %collective-permute-start.3 = (bf16[2,2,16,1024]{3,2,1,0:T(8,128)(2,1)S(1)}, bf16[2,2,16,1024]{3,2,1,0:T(8,128)(2,1)}, u32[]{:S(2)}, u32[]{:S(2)}) collective-permute-start(bf16[2,2,16,1024]{3,2,1,0:T(8,128)(2,1)S(1)} %slice.33), channel_id=1, source_target_pairs={{0,6},{1,7},{2,0},{3,1},{4,2},{5,3},{6,4},{7,5},{8,14},{9,15},{10,... | collective-permute-start | bytes 393224 | tf_op jit(solution)/shard_map/ppermute | solution.py:44
  85.2 6.4 %copy-start.17 = (bf16[4,2,16,1024]{3,2,1,0:T(8,128)(2,1)}, bf16[4,2,16,1024]{3,2,1,0:T(8,128)(2,1)S(1)}, u32[]{:S(2)}) copy-start(bf16[4,2,16,1024]{3,2,1,0:T(8,128)(2,1)S(1)} %collective-permute-done.6.refs_7_) | copy-start | bytes 786436
  85.2 6.3 %collective-permute-start.7 = (bf16[2,2,16,1024]{3,2,1,0:T(8,128)(2,1)S(1)}, bf16[2,2,16,1024]{3,2,1,0:T(8,128)(2,1)}, u32[]{:S(2)}, u32[]{:S(2)}) collective-permute-start(bf16[2,2,16,1024]{3,2,1,0:T(8,128)(2,1)S(1)} %slice.34), channel_id=1, source_target_pairs={{0,2},{1,3},{2,4},{3,5},{4,6},{5,7},{6,0},{7,1},{8,10},{9,11},{10,... | collective-permute-start | bytes 393224 | tf_op jit(solution)/shard_map/ppermute | solution.py:44
  85.7 2.8 %copy-start.22 = (bf16[2,2,16,1024]{3,2,1,0:T(8,128)(2,1)}, bf16[2,2,16,1024]{3,2,1,0:T(8,128)(2,1)S(1)}, u32[]{:S(2)}) copy-start(bf16[2,2,16,1024]{3,2,1,0:T(8,128)(2,1)S(1)} %collective-permute-done.2.refs_3_) | copy-start | bytes 393220
  85.7 5.7 %collective-permute-start.8 = (bf16[2,2,16,1024]{3,2,1,0:T(8,128)(2,1)S(1)}, bf16[2,2,16,1024]{3,2,1,0:T(8,128)(2,1)}, u32[]{:S(2)}, u32[]{:S(2)}) collective-permute-start(bf16[2,2,16,1024]{3,2,1,0:T(8,128)(2,1)S(1)} %slice.35), channel_id=1, source_target_pairs={{0,6},{1,7},{2,0},{3,1},{4,2},{5,3},{6,4},{7,5},{8,14},{9,15},{10,... | collective-permute-start | bytes 393224 | tf_op jit(solution)/shard_map/ppermute | solution.py:44
  89.3 2.3 %copy-start.20 = (bf16[512,768]{1,0:T(8,128)(2,1)}, bf16[512,768]{1,0:T(8,128)(2,1)S(1)}, u32[]{:S(2)}) copy-start(bf16[512,768]{1,0:T(8,128)(2,1)S(1)} %collective-permute-done.9.refs_11_) | copy-start | bytes 2359300
  97.8 14.0 %collective-permute-start.12 = (bf16[128,768]{1,0:T(8,128)(2,1)}, bf16[128,768]{1,0:T(8,128)(2,1)S(1)}, u32[]{:S(2)}, u32[]{:S(2)}) collective-permute-start(bf16[128,768]{1,0:T(8,128)(2,1)} %get-tuple-element.15), channel_id=1, source_target_pairs={{0,48},{1,49},{2,50},{3,51},{4,52},{5,53},{6,54},{7,55},{8,56},{9,... | collective-permute-start | bytes 589832 | tf_op jit(solution)/shard_map/ppermute | solution.py:44
  100.9 10.9 %collective-permute-start.13 = (bf16[128,768]{1,0:T(8,128)(2,1)}, bf16[128,768]{1,0:T(8,128)(2,1)S(1)}, u32[]{:S(2)}, u32[]{:S(2)}) collective-permute-start(bf16[128,768]{1,0:T(8,128)(2,1)} %get-tuple-element.16), channel_id=1, source_target_pairs={{0,32},{1,33},{2,34},{3,35},{4,36},{5,37},{6,38},{7,39},{8,40},{9,... | collective-permute-start | bytes 589832 | tf_op jit(solution)/shard_map/ppermute | solution.py:44
  101.5 12.6 %collective-permute-start.14 = (bf16[128,768]{1,0:T(8,128)(2,1)}, bf16[128,768]{1,0:T(8,128)(2,1)S(1)}, u32[]{:S(2)}, u32[]{:S(2)}) collective-permute-start(bf16[128,768]{1,0:T(8,128)(2,1)} %get-tuple-element.17), channel_id=1, source_target_pairs={{0,16},{1,17},{2,18},{3,19},{4,20},{5,21},{6,22},{7,23},{8,24},{9,... | collective-permute-start | bytes 589832 | tf_op jit(solution)/shard_map/ppermute | solution.py:44
  111.8 2.3 %copy-start.6 = (bf16[128,768]{1,0:T(8,128)(2,1)}, bf16[128,768]{1,0:T(8,128)(2,1)S(1)}, u32[]{:S(2)}) copy-start(bf16[128,768]{1,0:T(8,128)(2,1)S(1)} %collective-permute-done.12.refs_1_) | copy-start | bytes 589828
  111.8 2.3 %copy-start.7 = (bf16[128,768]{1,0:T(8,128)(2,1)}, bf16[128,768]{1,0:T(8,128)(2,1)S(1)}, u32[]{:S(2)}) copy-start(bf16[128,768]{1,0:T(8,128)(2,1)S(1)} %collective-permute-done.13.refs_2_) | copy-start | bytes 589828
  114.1 0.7 copy-start.8
  126.8 5.2 %collective-permute-start.19 = (bf16[128,512]{1,0:T(8,128)(2,1)}, bf16[128,512]{1,0:T(8,128)(2,1)S(1)}, u32[]{:S(2)}, u32[]{:S(2)}) collective-permute-start(bf16[128,512]{1,0:T(8,128)(2,1)} %shard_map.94.refs_0_), channel_id=1, source_target_pairs={{0,1},{1,0},{2,3},{3,2},{4,5},{5,4},{6,7},{7,6},{8,9},{9,8},{10,11... | collective-permute-start | bytes 393224 | tf_op jit(solution)/shard_map/ppermute | solution.py:44
  128.2 7.2 %collective-permute-start.15 = (bf16[128,512]{1,0:T(8,128)(2,1)}, bf16[128,512]{1,0:T(8,128)(2,1)S(1)}, u32[]{:S(2)}, u32[]{:S(2)}) collective-permute-start(bf16[128,512]{1,0:T(8,128)(2,1)} %shard_map.94.refs_0_), channel_id=1, source_target_pairs={{0,2},{1,3},{2,4},{3,5},{4,6},{5,7},{6,0},{7,1},{8,10},{9,11},{10,... | collective-permute-start | bytes 393224 | tf_op jit(solution)/shard_map/ppermute | solution.py:44
  128.2 7.3 %collective-permute-start.16 = (bf16[128,512]{1,0:T(8,128)(2,1)}, bf16[128,512]{1,0:T(8,128)(2,1)S(1)}, u32[]{:S(2)}, u32[]{:S(2)}) collective-permute-start(bf16[128,512]{1,0:T(8,128)(2,1)} %shard_map.94.refs_0_), channel_id=1, source_target_pairs={{0,6},{1,7},{2,0},{3,1},{4,2},{5,3},{6,4},{7,5},{8,14},{9,15},{10,... | collective-permute-start | bytes 393224 | tf_op jit(solution)/shard_map/ppermute | solution.py:44
  132.0 12.4 %copy-start.9 = (bf16[128,512]{1,0:T(8,128)(2,1)}, bf16[128,512]{1,0:T(8,128)(2,1)S(1)}, u32[]{:S(2)}) copy-start(bf16[128,512]{1,0:T(8,128)(2,1)S(1)} %collective-permute-done.19.refs_5_) | copy-start | bytes 393220
  132.0 6.8 %collective-permute-start.20 = (bf16[128,512]{1,0:T(8,128)(2,1)S(1)}, bf16[128,512]{1,0:T(8,128)(2,1)S(1)}, u32[]{:S(2)}, u32[]{:S(2)}) collective-permute-start(bf16[128,512]{1,0:T(8,128)(2,1)S(1)} %collective-permute-done.19.refs_5_), channel_id=1, source_target_pairs={{0,2},{1,3},{2,4},{3,5},{4,6},{5,7},{6,0},{7,1},{8,10},{9,11},{10,... | collective-permute-start | bytes 393224 | tf_op jit(solution)/shard_map/ppermute | solution.py:44
  132.0 6.9 %collective-permute-start.21 = (bf16[128,512]{1,0:T(8,128)(2,1)S(1)}, bf16[128,512]{1,0:T(8,128)(2,1)S(1)}, u32[]{:S(2)}, u32[]{:S(2)}) collective-permute-start(bf16[128,512]{1,0:T(8,128)(2,1)S(1)} %collective-permute-done.19.refs_5_), channel_id=1, source_target_pairs={{0,6},{1,7},{2,0},{3,1},{4,2},{5,3},{6,4},{7,5},{8,14},{9,15},{10,... | collective-permute-start | bytes 393224 | tf_op jit(solution)/shard_map/ppermute | solution.py:44
  135.4 9.0 %copy-start.1 = (bf16[128,512]{1,0:T(8,128)(2,1)}, bf16[128,512]{1,0:T(8,128)(2,1)S(1)}, u32[]{:S(2)}) copy-start(bf16[128,512]{1,0:T(8,128)(2,1)S(1)} %collective-permute-done.15.refs_1_) | copy-start | bytes 393220
  135.4 6.8 %collective-permute-start.17 = (bf16[64,512]{1,0:T(8,128)(2,1)S(1)}, bf16[64,512]{1,0:T(8,128)(2,1)S(1)}, u32[]{:S(2)}, u32[]{:S(2)}) collective-permute-start(bf16[64,512]{1,0:T(8,128)(2,1)S(1)} %slice.36), channel_id=1, source_target_pairs={{0,2},{1,3},{2,4},{3,5},{4,6},{5,7},{6,0},{7,1},{8,10},{9,11},{10,... | collective-permute-start | bytes 196616 | tf_op jit(solution)/shard_map/ppermute | solution.py:44
  135.5 8.9 %copy-start.2 = (bf16[128,512]{1,0:T(8,128)(2,1)}, bf16[128,512]{1,0:T(8,128)(2,1)S(1)}, u32[]{:S(2)}) copy-start(bf16[128,512]{1,0:T(8,128)(2,1)S(1)} %collective-permute-done.16.refs_2_) | copy-start | bytes 393220
  135.5 6.7 %collective-permute-start.18 = (bf16[64,512]{1,0:T(8,128)(2,1)S(1)}, bf16[64,512]{1,0:T(8,128)(2,1)S(1)}, u32[]{:S(2)}, u32[]{:S(2)}) collective-permute-start(bf16[64,512]{1,0:T(8,128)(2,1)S(1)} %slice.37), channel_id=1, source_target_pairs={{0,6},{1,7},{2,0},{3,1},{4,2},{5,3},{6,4},{7,5},{8,14},{9,15},{10,... | collective-permute-start | bytes 196616 | tf_op jit(solution)/shard_map/ppermute | solution.py:44
  138.8 5.6 %copy-start.3 = (bf16[128,512]{1,0:T(8,128)(2,1)}, bf16[128,512]{1,0:T(8,128)(2,1)S(1)}, u32[]{:S(2)}) copy-start(bf16[128,512]{1,0:T(8,128)(2,1)S(1)} %collective-permute-done.20.refs_6_) | copy-start | bytes 393220
  138.8 5.5 %collective-permute-start.22 = (bf16[64,512]{1,0:T(8,128)(2,1)S(1)}, bf16[64,512]{1,0:T(8,128)(2,1)S(1)}, u32[]{:S(2)}, u32[]{:S(2)}) collective-permute-start(bf16[64,512]{1,0:T(8,128)(2,1)S(1)} %slice.38), channel_id=1, source_target_pairs={{0,2},{1,3},{2,4},{3,5},{4,6},{5,7},{6,0},{7,1},{8,10},{9,11},{10,... | collective-permute-start | bytes 196616 | tf_op jit(solution)/shard_map/ppermute | solution.py:44
  138.9 5.5 %copy-start.4 = (bf16[128,512]{1,0:T(8,128)(2,1)}, bf16[128,512]{1,0:T(8,128)(2,1)S(1)}, u32[]{:S(2)}) copy-start(bf16[128,512]{1,0:T(8,128)(2,1)S(1)} %collective-permute-done.21.refs_7_) | copy-start | bytes 393220
  138.9 5.4 %collective-permute-start.23 = (bf16[64,512]{1,0:T(8,128)(2,1)S(1)}, bf16[64,512]{1,0:T(8,128)(2,1)S(1)}, u32[]{:S(2)}, u32[]{:S(2)}) collective-permute-start(bf16[64,512]{1,0:T(8,128)(2,1)S(1)} %slice.39), channel_id=1, source_target_pairs={{0,6},{1,7},{2,0},{3,1},{4,2},{5,3},{6,4},{7,5},{8,14},{9,15},{10,... | collective-permute-start | bytes 196616 | tf_op jit(solution)/shard_map/ppermute | solution.py:44
  142.2 2.2 %copy-start.10 = (bf16[64,512]{1,0:T(8,128)(2,1)}, bf16[64,512]{1,0:T(8,128)(2,1)S(1)}, u32[]{:S(2)}) copy-start(bf16[64,512]{1,0:T(8,128)(2,1)S(1)} %collective-permute-done.17.refs_3_) | copy-start | bytes 196612
  142.2 2.2 %copy-start.11 = (bf16[64,512]{1,0:T(8,128)(2,1)}, bf16[64,512]{1,0:T(8,128)(2,1)S(1)}, u32[]{:S(2)}) copy-start(bf16[64,512]{1,0:T(8,128)(2,1)S(1)} %collective-permute-done.18.refs_4_) | copy-start | bytes 196612
  144.4 0.6 copy-start.12
  144.4 0.6 copy-start.13
Sparse Core Ops, SparseCore 0:
  42.6 77.2 all-gather.1

commit v2 on v1

--- a/solution.py
+++ b/solution.py
@@ -19,8 +19,8 @@
 AXES = ("zh", "y1", "y0", "c", "x1", "x0", "zl")
 REP = ("zh", "y1", "y0", "c")
 TP = ("x1", "x0", "zl")
-SPLIT = ("y1", "y0")
-REST = "zh"
+SPLIT = ("zh", "y0")
+REST = "y1"
 
 
 def pairs_of(change):
@@ -146,7 +146,7 @@
     for t in range(8):
         values = packed[t, :rows].astype(jnp.float32) * factor
         values = values * gain[t : t + 1, :].astype(jnp.float32)
-        normed[t & 3, t >> 2] = values.astype(jnp.bfloat16)
+        normed[(t >> 2) * 2 + (t & 1), (t >> 1) & 1] = values.astype(jnp.bfloat16)
         out_weight[t * deep : (t + 1) * deep] = packed[t, rows : rows + deep]
         first = rows + deep
         for n in range(3):
@@ -185,7 +185,7 @@
         ]
 
     copies = settle(place, blocks, spots, sems)
-    ring, core, rest = place[0], place[1], place[4]
+    here, core, rest = place[4] * 2 + place[0] % 2, place[1], place[0] // 2
     for i in range(4):
         first = ((rest ^ (i >> 1)) * 2 + (core ^ (i & 1))) * half
         copies.append(
@@ -198,7 +198,7 @@
     product = jnp.dot(acts[...].reshape(4 * batch, 2 * width), held[...], preferred_element_type=jnp.float32)
     sums[...] = product.astype(sums.dtype).reshape(sums.shape)
     for k in range(4):
-        outs[k][...] = sums[ring ^ k]
+        outs[k][...] = sums[here ^ k]
 
 
 def partial_products(place, blocks, weights):
@@ -225,21 +225,16 @@
 
 
 def output_kernel(place, *refs):
-    blocks, weight, out, acts, held, sems, more = refs[:10], *refs[10:]
+    blocks, weight, out, acts, sems = refs[:10], *refs[10:]
     width = blocks[0].shape[1]
 
     def spots(block, index, part, sem):
         columns = pl.ds(pl.multiple_of(index * width, width), width)
         return [(block, acts.at[part, columns], (sem,))]
 
-    copies = settle(place, blocks, spots, more)
-    for group in range(8):
-        rows = pl.ds(group * width, width)
-        copies.append(pltpu.make_async_copy(weight.at[rows], held.at[rows], sems.at[group]))
-        copies[-1].start()
-    for copy in copies:
+    for copy in settle(place, blocks, spots, sems):
         copy.wait()
-    out[...] = jnp.dot(acts[...], held[...], preferred_element_type=jnp.float32).astype(out.dtype)
+    out[...] = jnp.dot(acts[...], weight[...], preferred_element_type=jnp.float32).astype(out.dtype)
 
 
 def output_product(place, blocks, weight):
@@ -248,15 +243,15 @@
     return pl.pallas_call(
         output_kernel,
         out_shape=jax.ShapeDtypeStruct((batch, columns), jnp.bfloat16),
-        in_specs=[pl.BlockSpec(memory_space=pltpu.SMEM)] + [pl.BlockSpec(memory_space=pl.ANY)] * 11,
+        in_specs=[pl.BlockSpec(memory_space=pltpu.SMEM)]
+        + [pl.BlockSpec(memory_space=pl.ANY)] * 10
+        + [pl.BlockSpec(memory_space=pltpu.VMEM)],
         out_specs=pl.BlockSpec(memory_space=pltpu.VMEM),
         scratch_shapes=[
             pltpu.VMEM((batch, 8 * width), jnp.bfloat16),
-            pltpu.VMEM((8 * width, columns), jnp.bfloat16),
-            pltpu.SemaphoreType.DMA((8,)),
             pltpu.SemaphoreType.DMA((10,)),
         ],
-        compiler_params=pltpu.CompilerParams(vmem_limit_bytes=VMEM_BYTES),
+        compiler_params=pltpu.CompilerParams(vmem_limit_bytes=32 * 1024 * 1024),
         cost_estimate=pl.CostEstimate(
             flops=2 * batch * 8 * width * columns, bytes_accessed=10 * 1024 * 1024, transcendentals=0
         ),
@@ -278,15 +273,43 @@
     )(block, *others)
 
 
+def stage_kernel(count, arrays, *refs):
+    sources, targets, sems = refs[:arrays], refs[count:-1], refs[-1]
+    copies = []
+    for i in range(arrays):
+        pieces = sems.shape[1]
+        size = sources[i].shape[0] // pieces
+        for k in range(pieces):
+            part = pl.ds(k * size, size)
+            copies.append(pltpu.make_async_copy(sources[i].at[part], targets[i].at[part], sems.at[i, k]))
+    for copy in copies:
+        copy.start()
+    for copy in copies:
+        copy.wait()
+
+
+def stage(arrays, *others):
+    anywhere = pl.BlockSpec(memory_space=pl.ANY)
+    count = len(arrays) + len(others)
+    size = sum(array.size * array.dtype.itemsize for array in arrays)
+    return pl.pallas_call(
+        functools.partial(stage_kernel, count, len(arrays)),
+        out_shape=[jax.ShapeDtypeStruct(array.shape, array.dtype) for array in arrays],
+        in_specs=[anywhere] * count,
+        out_specs=[anywhere] * len(arrays),
+        scratch_shapes=[pltpu.SemaphoreType.DMA((len(arrays), 8))],
+        compiler_params=pltpu.CompilerParams(vmem_limit_bytes=1024 * 1024),
+        cost_estimate=pl.CostEstimate(flops=0, bytes_accessed=2 * size, transcendentals=0),
+    )(*arrays, *others)
+
+
 def attention_kernel(lengths, *refs):
     parts, (cosine, sine, key, value, out), scratch = refs[:4], refs[4:9], refs[9:]
     queries, fresh_keys, fresh_values, scores, sums = scratch
     rows, heads, _ = queries.shape
-    chunk = key.shape[0]
-    step = pl.program_id(0)
-
-    @pl.when(step == 0)
-    def _():
+    chunk = scores.shape[0] // heads
+
+    if True:
         projected = parts[0][...].astype(jnp.float32)
         for part in parts[1:]:
             projected = projected + part[...].astype(jnp.float32)
@@ -309,65 +332,64 @@
             fresh_values[s] = fresh_value[s * rows : (s + 1) * rows]
 
     scale = HD ** (-0.5)
-    here = pl.ds(pl.multiple_of(step * chunk, chunk), chunk)
-    query = queries[here].reshape(chunk * heads, HD)
-    for r in range(chunk):
-        scores[r * heads : (r + 1) * heads] = lax.dot_general(
-            query[r * heads : (r + 1) * heads].astype(jnp.bfloat16),
-            key[r],
-            (((1,), (1,)), ((), ())),
-            preferred_element_type=jnp.float32,
-        )
-    cached = scores[...] * scale
-    spot = lax.broadcasted_iota(jnp.int32, cached.shape, 1)
-    cached = jnp.where(spot < lengths[...], cached, -jnp.inf)
     at_step = lax.broadcasted_iota(jnp.int32, (chunk * heads, 1), 0) % heads // GROUP
 
     def repeated(vectors):
         return jnp.broadcast_to(vectors[:, None, :], (chunk, heads, HD)).reshape(chunk * heads, HD)
 
-    new = []
-    highest = jnp.max(cached, axis=-1, keepdims=True)
+    def some_rows(step, carry):
+        begin = pl.multiple_of(step * chunk, chunk)
+        here = pl.ds(begin, chunk)
+        query = queries[here].reshape(chunk * heads, HD)
+        for r in range(chunk):
+            scores[r * heads : (r + 1) * heads] = lax.dot_general(
+                query[r * heads : (r + 1) * heads].astype(jnp.bfloat16),
+                key[begin + r],
+                (((1,), (1,)), ((), ())),
+                preferred_element_type=jnp.float32,
+            )
+        cached = scores[...] * scale
+        spot = lax.broadcasted_iota(jnp.int32, cached.shape, 1)
+        limit = lengths[pl.ds(pl.multiple_of(step * chunk * heads, chunk * heads), chunk * heads)]
+        cached = jnp.where(spot < limit, cached, -jnp.inf)
+        new = []
+        highest = jnp.max(cached, axis=-1, keepdims=True)
+        for s in range(STEPS):
+            score = jnp.sum(query * repeated(fresh_keys[s, here]), axis=-1, keepdims=True) * scale
+            new.append(jnp.where(at_step >= s, score, -jnp.inf))
+            highest = jnp.maximum(highest, new[s])
+        cached = jnp.exp(cached - highest)
+        new = [jnp.exp(score - highest) for score in new]
+        total = jnp.sum(cached, axis=-1, keepdims=True) + new[0] + new[1]
+        share = 1.0 / total
+        scores[...] = cached * share
+        result = None
+        for s in range(STEPS):
+            prob = (new[s] * share).astype(jnp.bfloat16).astype(jnp.float32)
+            term = prob * repeated(fresh_values[s, here])
+            result = term if result is None else result + term
+        result = result.reshape(chunk, heads, HD)
+        for r in range(chunk):
+            prob = scores[r * heads : (r + 1) * heads].astype(jnp.bfloat16)
+            sums[begin + r] = result[r] + jnp.dot(prob, value[begin + r], preferred_element_type=jnp.float32)
+        return carry
+
+    lax.fori_loop(0, rows // chunk, some_rows, 0)
     for s in range(STEPS):
-        score = jnp.sum(query * repeated(fresh_keys[s, here]), axis=-1, keepdims=True) * scale
-        new.append(jnp.where(at_step >= s, score, -jnp.inf))
-        highest = jnp.maximum(highest, new[s])
-    cached = jnp.exp(cached - highest)
-    new = [jnp.exp(score - highest) for score in new]
-    total = jnp.sum(cached, axis=-1, keepdims=True) + new[0] + new[1]
-    share = 1.0 / total
-    scores[...] = cached * share
-    result = None
-    for s in range(STEPS):
-        prob = (new[s] * share).astype(jnp.bfloat16).astype(jnp.float32)
-        term = prob * repeated(fresh_values[s, here])
-        result = term if result is None else result + term
-    result = result.reshape(chunk, heads, HD)
-    for r in range(chunk):
-        prob = scores[r * heads : (r + 1) * heads].astype(jnp.bfloat16)
-        sums[step * chunk + r] = result[r] + jnp.dot(prob, value[r], preferred_element_type=jnp.float32)
-
-    @pl.when(step == pl.num_programs(0) - 1)
-    def _():
-        for s in range(STEPS):
-            for k in range(GROUP):
-                out[s * rows : (s + 1) * rows, k * HD : (k + 1) * HD] = sums[:, s * GROUP + k, :].astype(out.dtype)
+        for k in range(GROUP):
+            out[s * rows : (s + 1) * rows, k * HD : (k + 1) * HD] = sums[:, s * GROUP + k, :].astype(out.dtype)
 
 
 def attention_of(parts, cosine, sine, key_cache, value_cache, lengths, chunk=8):
     batch, columns = parts[0].shape
     rows, spots, _ = key_cache.shape
     heads = STEPS * GROUP
-    whole = lambda *shape: pl.BlockSpec(shape, lambda i: (0,) * len(shape))
-    cache = pl.BlockSpec((chunk, spots, HD), lambda i: (i, 0, 0))
+    vmem = pl.BlockSpec(memory_space=pltpu.VMEM)
     return pl.pallas_call(
         attention_kernel,
-        grid=(rows // chunk,),
         out_shape=jax.ShapeDtypeStruct((batch, GROUP * HD), jnp.bfloat16),
-        in_specs=[pl.BlockSpec((chunk * heads, 1), lambda i: (i, 0))]
-        + [whole(batch, columns)] * 4
-        + [whole(batch, HD), whole(batch, HD), cache, cache],
-        out_specs=whole(batch, GROUP * HD),
+        in_specs=[vmem] * 9,
+        out_specs=vmem,
         scratch_shapes=[
             pltpu.VMEM((rows, heads, HD), jnp.float32),
             pltpu.VMEM((STEPS, rows, HD), jnp.float32),
@@ -375,9 +397,7 @@
             pltpu.VMEM((chunk * heads, spots), jnp.float32),
             pltpu.VMEM((rows, heads, HD), jnp.float32),
         ],
-        compiler_params=pltpu.CompilerParams(
-            vmem_limit_bytes=VMEM_BYTES, dimension_semantics=("arbitrary",)
-        ),
+        compiler_params=pltpu.CompilerParams(vmem_limit_bytes=32 * 1024 * 1024),
         cost_estimate=pl.CostEstimate(
             flops=4 * rows * heads * spots * HD,
             bytes_accessed=4 * rows * spots * HD,
@@ -404,13 +424,16 @@
     normed, mine, out_mine = unpack(
         packed, norm_gain.reshape(8, width), batch // 8, w_out.shape[0], w_query.shape[0]
     )
+    out_weight = lax.all_gather(out_mine, REP, axis=0, tiled=True)
+
+    moved = lax.all_to_all(normed, SPLIT, 0, 0, tiled=True)
+    mine = tie(mine, moved)
     far = permute(mine, flipped(REST))
+    gathered = ring_gather(moved, "zl", "x1", "x0")
+    far = tie(far, gathered[3], gathered[4], gathered[6], gathered[7])
     weights = (mine, permute(mine, flipped("c")), far, permute(far, flipped("c")))
-    out_weight = lax.all_gather(out_mine, REP, axis=0, tiled=True)
-
-    moved = lax.all_to_all(normed, SPLIT, 0, 0, tiled=True)
-    gathered = ring_gather(moved, "zl", "x1", "x0")
     partial = partial_products(place, gathered, weights)
+    caches = stage((key_cache[:, 0], value_cache[:, 0]), partial[0])
     changes = [flipped(SPLIT[0]), flipped(SPLIT[1])]
     parts = [
         partial[0],
@@ -421,9 +444,10 @@
     positions = (lengths[None, :] + jnp.arange(steps)[:, None]).reshape(batch)
     cosine, sine = turns(positions)
     attention = attention_of(
-        parts, cosine, sine, key_cache[:, 0], value_cache[:, 0], lengths
+        parts, cosine, sine, *caches, lengths
     )
     joined = ring_gather(attention, "zl", "x1", "x0")
+    out_weight = stage((out_weight,), attention)[0]
     result = output_product(place, joined, out_weight)
     return result.reshape(steps, rows, width)
 

time: 161 us -> 153 us (0.950); the launches traced: 158 us -> 153 us
  waiting for transfers between devices: 58.7 us -> 42.5 us
  local copies, waits for them, and re-layouts: 5.46 us -> 19 us
  Pallas kernels: 30.1 us -> 22.3 us
  starting transfers between devices: 36.3 us -> 41.5 us
    ppermute x24, waiting for transfers between devices: 36.3 us -> 20.1 us  [permute(): return lax.ppermute(block, AXES, pairs_of(change))]
    unnamed x46 -> x40, local copies, waits for them, and re-layouts: 2.47 us -> 14.9 us
    ppermute x24, starting transfers between devices: 30.5 us -> 35.7 us  [permute(): return lax.ppermute(block, AXES, pairs_of(change))]
    pallas_call x1 -> x5, Pallas kernels: 12 us -> 7.98 us  [the longest x1 6.05 us: attention_of(): pl.pallas_call(attention_kernel, out_shape=jax.ShapeDtypeStruct((batch, G...]
    pallas_call x1, Pallas kernels: 6.47 us -> 2.76 us  [output_product(): pl.pallas_call(output_kernel, out_shape=jax.ShapeDtypeStruct((batch, colu...]
  transfers between devices with their start and end apart: 26 -> 26, of which waited for: 12 -> 10; matrix products, arithmetic and copies ran while one was open for 3% -> 3% of each run, Pallas kernels for 12% -> 9%
where the time goes in v2:
time: 153 us
  waiting for transfers between devices  42.5 us (28%)
  starting transfers between devices  41.5 us (27%)
  Pallas kernels  22.3 us (15%)
  local copies, waits for them, and re-layouts  19 us (12%)
  between operations  13.7 us (9%)
  blocking collectives  13.2 us (9%)
    ppermute x24, starting transfers between devices, permute(): return lax.ppermute(block, AXES, pairs_of(change))  35.7 us
    all_to_all x1, waiting for transfers between devices, shards(): packed = lax.all_to_all(packed, TP, 0, 0, tiled=True)  22.3 us
    ppermute x24, waiting for transfers between devices, permute(): return lax.ppermute(block, AXES, pairs_of(change))  20.1 us
    unnamed x40, local copies, waits for them, and re-layouts  14.9 us
    all_to_all x1, blocking collectives, shards(): moved = lax.all_to_all(normed, SPLIT, 0, 0, tiled=True)  13.2 us
    pallas_call x1, Pallas kernels, partial_products(): pl.pallas_call(partial_kernel, out_shape=[jax.ShapeDtypeStruct((8 * rows,...  6.22 us
    pallas_call x1, Pallas kernels, attention_of(): pl.pallas_call(attention_kernel, out_shape=jax.ShapeDtypeStruct((batch, G...  6.05 us
    all_to_all x1, starting transfers between devices, shards(): packed = lax.all_to_all(packed, TP, 0, 0, tiled=True)  5.74 us
  transfers between devices with their start and end apart: 26, of which 10 were waited for; matrix products, arithmetic and copies ran while one was open for 3% of the time, Pallas kernels for 9%

profile of v2, /device:TPU:0, one launch (start us, length us, event | category | flops | bytes accessed | tf_op | source)
XLA Modules:
  0.0 152.5 jit_solution(9988969754675630365)
XLA Ops:
  6.5 2.7 %shard_map.91 = bf16[8,96,1024]{2,1,0:T(8,128)(2,1)} custom-call(bf16[64,4096]{1,0:T(8,128)(2,1)} %query.1, bf16[64,1024]{1,0:T(8,128)(2,1)} %key.1, bf16[64,1024]{1,0:T(8,128)(2,1)} %value.1, bf16[32,8192]{1,0:T(8,128)(2,1)} %out_weight.1, bf16[128,1024]{1,0:T(8,128)(2,1)} %bitcast.11), custom_call_target="tpu_custom_call" | custom-call | tf_op jit(solution)/shard_map/pallas_call | solution.py:126
  9.2 5.7 %all-to-all-start = ((bf16[8,96,1024]{2,1,0:T(8,128)(2,1)}), bf16[8,96,1024]{2,1,0:T(8,128)(2,1)S(1)}, u32[]{:S(2)}, u32[]{:S(2)}) async-start(bf16[8,96,1024]{2,1,0:T(8,128)(2,1)} %shard_map.91), calls=%async_computation | async-start | bytes 3145728 | tf_op jit(solution)/shard_map/all_to_all | solution.py:423
  15.0 0.0 all-gather.2.cloned.1.call-start
  15.0 1.3 reshape.32.gain
  16.3 22.3 %all-to-all-done.packed = bf16[8,96,1024]{2,1,0:T(8,128)(2,1)S(1)} async-done(((bf16[8,96,1024]{2,1,0:T(8,128)(2,1)}), bf16[8,96,1024]{2,1,0:T(8,128)(2,1)S(1)}, u32[]{:S(2)}, u32[]{:S(2)}) %all-to-all-start) | async-done | bytes 1572896 | tf_op jit(solution)/shard_map/all_to_all | solution.py:423
  38.7 1.2 copy-done.6
  39.8 2.6 %shard_map.92 = (bf16[4,2,16,1024]{3,2,1,0:T(8,128)(2,1)}, bf16[512,768]{1,0:T(8,128)(2,1)}, bf16[256,1024]{1,0:T(8,128)(2,1)}) custom-call(bf16[8,96,1024]{2,1,0:T(8,128)(2,1)} %copy-done.6, bf16[8,1024]{1,0:T(8,128)(2,1)} %reshape.32.gain), custom_call_target="tpu_custom_call" | custom-call | tf_op jit(solution)/shard_map/pallas_call | solution.py:163
  42.5 0.0 all-gather.2.cloned.1.call-update
  42.5 13.2 %all_to_all.10.refs_1_.refs_0_ = bf16[4,2,16,1024]{3,2,1,0:T(8,128)(2,1)} all-to-all(bf16[4,2,16,1024]{3,2,1,0:T(8,128)(2,1)} %get-tuple-element.14), channel_id=1, replica_groups=mesh['zh'=2,'y1'=2,'y0'=2,'c'=2,'x1'=2,'x0'=2,'zl'=2] {'zh','y0'}, dimensions={0} | all-to-all | bytes 524288 | tf_op jit(solution)/shard_map/all_to_all | solution.py:429
  55.7 2.9 %collective-permute-start.10 = (bf16[512,768]{1,0:T(8,128)(2,1)}, bf16[512,768]{1,0:T(8,128)(2,1)S(1)}, u32[]{:S(2)}, u32[]{:S(2)}) collective-permute-start(bf16[512,768]{1,0:T(8,128)(2,1)} %shard_map.93.refs_10_), channel_id=1, source_target_pairs={{0,32},{1,33},{2,34},{3,35},{4,36},{5,37},{6,38},{7,39},{8,40},{9,... | collective-permute-start | bytes 2359304 | tf_op jit(solution)/shard_map/ppermute | solution.py:44
  58.6 3.2 %collective-permute-start.1 = (bf16[4,2,16,1024]{3,2,1,0:T(8,128)(2,1)}, bf16[4,2,16,1024]{3,2,1,0:T(8,128)(2,1)S(1)}, u32[]{:S(2)}, u32[]{:S(2)}) collective-permute-start(bf16[4,2,16,1024]{3,2,1,0:T(8,128)(2,1)} %all_to_all.10.refs_1_.refs_0_), channel_id=1, source_target_pairs={{0,6},{1,7},{2,0},{3,1},{4,2},{5,3},{6,4},{7,5},{8,14},{9,15},{10,... | collective-permute-start | bytes 786440 | tf_op jit(solution)/shard_map/ppermute | solution.py:44
  61.9 4.6 %collective-permute-done.4.refs_5_ = bf16[4,2,16,1024]{3,2,1,0:T(8,128)(2,1)S(1)} collective-permute-done((bf16[4,2,16,1024]{3,2,1,0:T(8,128)(2,1)}, bf16[4,2,16,1024]{3,2,1,0:T(8,128)(2,1)S(1)}, u32[]{:S(2)}, u32[]{:S(2)}) %collective-permute-start.4) | collective-permute-done | bytes 262176 | tf_op jit(solution)/shard_map/ppermute | solution.py:44
  66.4 1.5 collective-permute-start.5
  67.9 1.8 %collective-permute-start.6 = (bf16[4,2,16,1024]{3,2,1,0:T(8,128)(2,1)S(1)}, bf16[4,2,16,1024]{3,2,1,0:T(8,128)(2,1)S(1)}, u32[]{:S(2)}, u32[]{:S(2)}) collective-permute-start(bf16[4,2,16,1024]{3,2,1,0:T(8,128)(2,1)S(1)} %collective-permute-done.4.refs_5_), channel_id=1, source_target_pairs={{0,6},{1,7},{2,0},{3,1},{4,2},{5,3},{6,4},{7,5},{8,14},{9,15},{10,... | collective-permute-start | bytes 786440 | tf_op jit(solution)/shard_map/ppermute | solution.py:44
  69.7 0.0 collective-permute-done.refs_1_
  69.7 0.3 collective-permute-start.2
  70.0 3.0 %collective-permute-start.3 = (bf16[2,2,16,1024]{3,2,1,0:T(8,128)(2,1)S(1)}, bf16[2,2,16,1024]{3,2,1,0:T(8,128)(2,1)S(1)}, u32[]{:S(2)}, u32[]{:S(2)}) collective-permute-start(bf16[2,2,16,1024]{3,2,1,0:T(8,128)(2,1)S(1)} %slice.33), channel_id=1, source_target_pairs={{0,6},{1,7},{2,0},{3,1},{4,2},{5,3},{6,4},{7,5},{8,14},{9,15},{10,... | collective-permute-start | bytes 393224 | tf_op jit(solution)/shard_map/ppermute | solution.py:44
  73.1 4.2 %collective-permute-done.2.refs_1_.refs_3_ = bf16[2,2,16,1024]{3,2,1,0:T(8,128)(2,1)S(1)} collective-permute-done((bf16[2,2,16,1024]{3,2,1,0:T(8,128)(2,1)S(1)}, bf16[2,2,16,1024]{3,2,1,0:T(8,128)(2,1)S(1)}, u32[]{:S(2)}, u32[]{:S(2)}) %collective-permute-start.2) | collective-permute-done | bytes 131104 | tf_op jit(solution)/shard_map/ppermute | solution.py:44
  77.3 0.0 collective-permute-start.9
  77.3 0.3 collective-permute-done.3.refs_2_.refs_4_
  77.6 0.0 collective-permute-done.6.refs_4_.refs_7_
  77.6 4.1 %collective-permute-done.10.refs_0_ = bf16[512,768]{1,0:T(8,128)(2,1)S(1)} collective-permute-done((bf16[512,768]{1,0:T(8,128)(2,1)}, bf16[512,768]{1,0:T(8,128)(2,1)S(1)}, u32[]{:S(2)}, u32[]{:S(2)}) %collective-permute-start.10) | collective-permute-done | bytes 786464 | tf_op jit(solution)/shard_map/ppermute | solution.py:44
  81.8 0.9 copy-done.7
  82.6 0.0 collective-permute-start.11
  82.6 0.9 slice.34
  83.5 0.8 collective-permute-start.7
  84.3 0.9 slice.35
  85.2 2.6 %collective-permute-start.8 = (bf16[2,2,16,1024]{3,2,1,0:T(8,128)(2,1)S(1)}, bf16[2,2,16,1024]{3,2,1,0:T(8,128)(2,1)S(1)}, u32[]{:S(2)}, u32[]{:S(2)}) collective-permute-start(bf16[2,2,16,1024]{3,2,1,0:T(8,128)(2,1)S(1)} %slice.35), channel_id=1, source_target_pairs={{0,6},{1,7},{2,0},{3,1},{4,2},{5,3},{6,4},{7,5},{8,14},{9,15},{10,... | collective-permute-start | bytes 393224 | tf_op jit(solution)/shard_map/ppermute | solution.py:44
  87.8 0.1 convert_element_type.18
  87.9 0.6 stack.23.place
  88.5 2.2 %collective-permute-done.7.refs_8_ = bf16[2,2,16,1024]{3,2,1,0:T(8,128)(2,1)S(1)} collective-permute-done((bf16[2,2,16,1024]{3,2,1,0:T(8,128)(2,1)S(1)}, bf16[2,2,16,1024]{3,2,1,0:T(8,128)(2,1)S(1)}, u32[]{:S(2)}, u32[]{:S(2)}) %collective-permute-start.7) | collective-permute-done | bytes 131104 | tf_op jit(solution)/shard_map/ppermute | solution.py:44
  90.7 0.2 collective-permute-done.8.refs_9_
  91.0 0.4 copy-done.18
  91.4 0.2 copy-done.19
  91.6 0.3 copy-done.15
  91.9 0.9 copy-done.16
  92.8 6.2 %shard_map.95 = (bf16[128,768]{1,0:T(8,128)(2,1)}, bf16[128,768]{1,0:T(8,128)(2,1)}, bf16[128,768]{1,0:T(8,128)(2,1)}, bf16[128,768]{1,0:T(8,128)(2,1)}) custom-call(s32[5]{0:T(128)} %stack.23.place, bf16[4,2,16,1024]{3,2,1,0:T(8,128)(2,1)} %all_to_all.10.refs_1_.refs_0_, bf16[4,2,16,1024]{3,2,1,0:T(8,128)(2,1)} %copy-done.12, ...), custom_call_target="tpu_custom_call" | custom-call | flops 1610612736 | bytes 8388608 | tf_op jit(solution)/shard_map/pallas_call | solution.py:208
  99.0 2.0 %collective-permute-start.12 = (bf16[128,768]{1,0:T(8,128)(2,1)}, bf16[128,768]{1,0:T(8,128)(2,1)S(1)}, u32[]{:S(2)}, u32[]{:S(2)}) collective-permute-start(bf16[128,768]{1,0:T(8,128)(2,1)} %get-tuple-element.17), channel_id=1, source_target_pairs={{0,80},{1,81},{2,82},{3,83},{4,84},{5,85},{6,86},{7,87},{8,88},{9,... | collective-permute-start | bytes 589832 | tf_op jit(solution)/shard_map/ppermute | solution.py:44
  101.0 1.9 %collective-permute-start.13 = (bf16[128,768]{1,0:T(8,128)(2,1)}, bf16[128,768]{1,0:T(8,128)(2,1)S(1)}, u32[]{:S(2)}, u32[]{:S(2)}) collective-permute-start(bf16[128,768]{1,0:T(8,128)(2,1)} %get-tuple-element.18), channel_id=1, source_target_pairs={{0,64},{1,65},{2,66},{3,67},{4,68},{5,69},{6,70},{7,71},{8,72},{9,... | collective-permute-start | bytes 589832 | tf_op jit(solution)/shard_map/ppermute | solution.py:44
  102.9 1.2 collective-permute-start.14
  104.1 0.3 fusion
  104.4 0.1 broadcast_in_dim.2
  104.5 0.1 broadcast_in_dim_reshape.4.lengths
  104.6 0.1 pad_maximum_fusion
  104.7 0.0 copy-start
  104.7 3.4 %copy-done = bf16[64,1,512,128]{3,2,1,0:T(8,128)(2,1)S(1)} copy-done((bf16[64,1,512,128]{3,2,1,0:T(8,128)(2,1)S(1)}, bf16[64,1,512,128]{3,2,1,0:T(8,128)(2,1)}, u32[]{:S(2)}) %copy-start) | copy-done | bytes 8388632
  108.1 3.4 %copy-done.1 = bf16[64,1,512,128]{3,2,1,0:T(8,128)(2,1)S(1)} copy-done((bf16[64,1,512,128]{3,2,1,0:T(8,128)(2,1)S(1)}, bf16[64,1,512,128]{3,2,1,0:T(8,128)(2,1)}, u32[]{:S(2)}) %copy-start.1) | copy-done | bytes 8388632
  111.5 0.9 copy-done.3
  112.4 1.3 shard_map.96
  113.7 3.0 %collective-permute-done.13.refs_2_ = bf16[128,768]{1,0:T(8,128)(2,1)S(1)} collective-permute-done((bf16[128,768]{1,0:T(8,128)(2,1)}, bf16[128,768]{1,0:T(8,128)(2,1)S(1)}, u32[]{:S(2)}, u32[]{:S(2)}) %collective-permute-start.13) | collective-permute-done | bytes 196640 | tf_op jit(solution)/shard_map/ppermute | solution.py:44
  116.8 6.0 %shard_map.97.refs_1_.refs_0_ = bf16[128,512]{1,0:T(8,128)(2,1)S(1)} custom-call(s32[512,1]{1,0:T(8,128)S(1)} %broadcast_in_dim_reshape.4.lengths, bf16[128,768]{1,0:T(8,128)(2,1)S(1)} %copy-done.4, bf16[128,768]{1,0:T(8,128)(2,1)S(1)} %collective-permute-done.12.refs_1_, bf16[128,768]{1,0:T(8,128)(2,1)S(1)} %collective-permute-done.13.refs_2_, ...), custom_call_target="tpu_custom_call" | custom-call | flops 134217728 | bytes 16777216 | tf_op jit(solution)/shard_map/pallas_call | solution.py:388
  122.8 0.1 collective-permute-start.19
  122.9 0.4 collective-permute-start.15
  123.3 3.8 %collective-permute-start.16 = (bf16[128,512]{1,0:T(8,128)(2,1)S(1)}, bf16[128,512]{1,0:T(8,128)(2,1)S(1)}, u32[]{:S(2)}, u32[]{:S(2)}) collective-permute-start(bf16[128,512]{1,0:T(8,128)(2,1)S(1)} %shard_map.97.refs_1_.refs_0_), channel_id=1, source_target_pairs={{0,6},{1,7},{2,0},{3,1},{4,2},{5,3},{6,4},{7,5},{8,14},{9,15},{10,... | collective-permute-start | bytes 393224 | tf_op jit(solution)/shard_map/ppermute | solution.py:44
  127.0 1.1 collective-permute-done.19.refs_5_
  128.2 0.7 collective-permute-start.20
  128.8 3.0 %collective-permute-start.21 = (bf16[128,512]{1,0:T(8,128)(2,1)S(1)}, bf16[128,512]{1,0:T(8,128)(2,1)S(1)}, u32[]{:S(2)}, u32[]{:S(2)}) collective-permute-start(bf16[128,512]{1,0:T(8,128)(2,1)S(1)} %collective-permute-done.19.refs_5_), channel_id=1, source_target_pairs={{0,6},{1,7},{2,0},{3,1},{4,2},{5,3},{6,4},{7,5},{8,14},{9,15},{10,... | collective-permute-start | bytes 393224 | tf_op jit(solution)/shard_map/ppermute | solution.py:44
  131.9 0.1 collective-permute-start.17
  132.0 3.3 %collective-permute-start.18 = (bf16[64,512]{1,0:T(8,128)(2,1)S(1)}, bf16[64,512]{1,0:T(8,128)(2,1)S(1)}, u32[]{:S(2)}, u32[]{:S(2)}) collective-permute-start(bf16[64,512]{1,0:T(8,128)(2,1)S(1)} %slice.37), channel_id=1, source_target_pairs={{0,6},{1,7},{2,0},{3,1},{4,2},{5,3},{6,4},{7,5},{8,14},{9,15},{10,... | collective-permute-start | bytes 196616 | tf_op jit(solution)/shard_map/ppermute | solution.py:44
  135.3 0.2 collective-permute-done.20.refs_6_
  135.5 3.3 %collective-permute-start.23 = (bf16[64,512]{1,0:T(8,128)(2,1)S(1)}, bf16[64,512]{1,0:T(8,128)(2,1)S(1)}, u32[]{:S(2)}, u32[]{:S(2)}) collective-permute-start(bf16[64,512]{1,0:T(8,128)(2,1)S(1)} %slice.39), channel_id=1, source_target_pairs={{0,6},{1,7},{2,0},{3,1},{4,2},{5,3},{6,4},{7,5},{8,14},{9,15},{10,... | collective-permute-start | bytes 196616 | tf_op jit(solution)/shard_map/ppermute | solution.py:44
  138.8 3.4 %copy-done.2 = bf16[4096,1024]{1,0:T(8,128)(2,1)S(1)} copy-done((bf16[4096,1024]{1,0:T(8,128)(2,1)S(1)}, bf16[4096,1024]{1,0:T(8,128)(2,1)}, u32[]{:S(2)}) %copy-start.2) | copy-done | bytes 8388632
  142.2 0.6 shard_map.98.refs_10_
  142.9 2.8 %shard_map.99 = bf16[128,1024]{1,0:T(8,128)(2,1)} custom-call(s32[5]{0:T(128)S(1)} %copy-done.5, bf16[128,512]{1,0:T(8,128)(2,1)S(1)} %shard_map.97.refs_1_.refs_0_, bf16[128,512]{1,0:T(8,128)(2,1)S(1)} %collective-permute-done.15.refs_1_, bf16[128,512]{1,0:T(8,128)(2,1)S(1)} %collective-permute-done.16.refs_2_, ...), custom_call_target="tpu_custom_call" | custom-call | flops 1073741824 | bytes 10485760 | tf_op jit(solution)/shard_map/pallas_call | solution.py:243
  (56 shorter events, 0.2 us)
Async XLA Ops:
  6.5 81.3 %copy-start.14 = (s32[64]{0:T(128)S(1)}, s32[64]{0:T(128)}, u32[]{:S(2)}) copy-start(s32[64]{0:T(128)} %param.17) | copy-start | bytes 772
  9.2 29.4 %all-to-all-start = ((bf16[8,96,1024]{2,1,0:T(8,128)(2,1)}), bf16[8,96,1024]{2,1,0:T(8,128)(2,1)S(1)}, u32[]{:S(2)}, u32[]{:S(2)}) async-start(bf16[8,96,1024]{2,1,0:T(8,128)(2,1)} %shard_map.91), calls=%async_computation | async-start | bytes 3145728 | tf_op jit(solution)/shard_map/all_to_all | solution.py:423
  15.0 123.9 %all-gather.2.cloned.1.call-start = ((), (), s32[]{:S(2)}) async-start(), calls=%async_computation.2 | async-start | bytes 8912896 | tf_op jit(solution)/shard_map/all_gather | solution.py:427
  38.7 1.2 copy-start.6
  55.7 26.0 %collective-permute-start.10 = (bf16[512,768]{1,0:T(8,128)(2,1)}, bf16[512,768]{1,0:T(8,128)(2,1)S(1)}, u32[]{:S(2)}, u32[]{:S(2)}) collective-permute-start(bf16[512,768]{1,0:T(8,128)(2,1)} %shard_map.93.refs_10_), channel_id=1, source_target_pairs={{0,32},{1,33},{2,34},{3,35},{4,36},{5,37},{6,38},{7,39},{8,40},{9,... | collective-permute-start | bytes 2359304 | tf_op jit(solution)/shard_map/ppermute | solution.py:44
  58.6 7.8 %collective-permute-start.4 = (bf16[4,2,16,1024]{3,2,1,0:T(8,128)(2,1)}, bf16[4,2,16,1024]{3,2,1,0:T(8,128)(2,1)S(1)}, u32[]{:S(2)}, u32[]{:S(2)}) collective-permute-start(bf16[4,2,16,1024]{3,2,1,0:T(8,128)(2,1)} %all_to_all.10.refs_1_.refs_0_), channel_id=1, source_target_pairs={{0,1},{1,0},{2,3},{3,2},{4,5},{5,4},{6,7},{7,6},{8,9},{9,8},{10,11... | collective-permute-start | bytes 786440 | tf_op jit(solution)/shard_map/ppermute | solution.py:44
  58.6 11.1 %collective-permute-start = (bf16[4,2,16,1024]{3,2,1,0:T(8,128)(2,1)}, bf16[4,2,16,1024]{3,2,1,0:T(8,128)(2,1)S(1)}, u32[]{:S(2)}, u32[]{:S(2)}) collective-permute-start(bf16[4,2,16,1024]{3,2,1,0:T(8,128)(2,1)} %all_to_all.10.refs_1_.refs_0_), channel_id=1, source_target_pairs={{0,2},{1,3},{2,4},{3,5},{4,6},{5,7},{6,0},{7,1},{8,10},{9,11},{10,... | collective-permute-start | bytes 786440 | tf_op jit(solution)/shard_map/ppermute | solution.py:44
  58.6 11.4 %collective-permute-start.1 = (bf16[4,2,16,1024]{3,2,1,0:T(8,128)(2,1)}, bf16[4,2,16,1024]{3,2,1,0:T(8,128)(2,1)S(1)}, u32[]{:S(2)}, u32[]{:S(2)}) collective-permute-start(bf16[4,2,16,1024]{3,2,1,0:T(8,128)(2,1)} %all_to_all.10.refs_1_.refs_0_), channel_id=1, source_target_pairs={{0,6},{1,7},{2,0},{3,1},{4,2},{5,3},{6,4},{7,5},{8,14},{9,15},{10,... | collective-permute-start | bytes 786440 | tf_op jit(solution)/shard_map/ppermute | solution.py:44
  66.4 24.5 %copy-start.17 = (bf16[4,2,16,1024]{3,2,1,0:T(8,128)(2,1)}, bf16[4,2,16,1024]{3,2,1,0:T(8,128)(2,1)S(1)}, u32[]{:S(2)}) copy-start(bf16[4,2,16,1024]{3,2,1,0:T(8,128)(2,1)S(1)} %collective-permute-done.4.refs_5_) | copy-start | bytes 786436
  66.4 11.1 %collective-permute-start.5 = (bf16[4,2,16,1024]{3,2,1,0:T(8,128)(2,1)S(1)}, bf16[4,2,16,1024]{3,2,1,0:T(8,128)(2,1)S(1)}, u32[]{:S(2)}, u32[]{:S(2)}) collective-permute-start(bf16[4,2,16,1024]{3,2,1,0:T(8,128)(2,1)S(1)} %collective-permute-done.4.refs_5_), channel_id=1, source_target_pairs={{0,2},{1,3},{2,4},{3,5},{4,6},{5,7},{6,0},{7,1},{8,10},{9,11},{10,... | collective-permute-start | bytes 786440 | tf_op jit(solution)/shard_map/ppermute | solution.py:44
  67.9 9.7 %collective-permute-start.6 = (bf16[4,2,16,1024]{3,2,1,0:T(8,128)(2,1)S(1)}, bf16[4,2,16,1024]{3,2,1,0:T(8,128)(2,1)S(1)}, u32[]{:S(2)}, u32[]{:S(2)}) collective-permute-start(bf16[4,2,16,1024]{3,2,1,0:T(8,128)(2,1)S(1)} %collective-permute-done.4.refs_5_), channel_id=1, source_target_pairs={{0,6},{1,7},{2,0},{3,1},{4,2},{5,3},{6,4},{7,5},{8,14},{9,15},{10,... | collective-permute-start | bytes 786440 | tf_op jit(solution)/shard_map/ppermute | solution.py:44
  69.7 21.3 %copy-start.12 = (bf16[4,2,16,1024]{3,2,1,0:T(8,128)(2,1)}, bf16[4,2,16,1024]{3,2,1,0:T(8,128)(2,1)S(1)}, u32[]{:S(2)}) copy-start(bf16[4,2,16,1024]{3,2,1,0:T(8,128)(2,1)S(1)} %collective-permute-done.refs_1_) | copy-start | bytes 786436
  69.7 7.6 %collective-permute-start.2 = (bf16[2,2,16,1024]{3,2,1,0:T(8,128)(2,1)S(1)}, bf16[2,2,16,1024]{3,2,1,0:T(8,128)(2,1)S(1)}, u32[]{:S(2)}, u32[]{:S(2)}) collective-permute-start(bf16[2,2,16,1024]{3,2,1,0:T(8,128)(2,1)S(1)} %slice.32), channel_id=1, source_target_pairs={{0,2},{1,3},{2,4},{3,5},{4,6},{5,7},{6,0},{7,1},{8,10},{9,11},{10,... | collective-permute-start | bytes 393224 | tf_op jit(solution)/shard_map/ppermute | solution.py:44
  70.0 21.0 %copy-start.13 = (bf16[4,2,16,1024]{3,2,1,0:T(8,128)(2,1)}, bf16[4,2,16,1024]{3,2,1,0:T(8,128)(2,1)S(1)}, u32[]{:S(2)}) copy-start(bf16[4,2,16,1024]{3,2,1,0:T(8,128)(2,1)S(1)} %collective-permute-done.1.refs_2_) | copy-start | bytes 786436
  70.0 7.5 %collective-permute-start.3 = (bf16[2,2,16,1024]{3,2,1,0:T(8,128)(2,1)S(1)}, bf16[2,2,16,1024]{3,2,1,0:T(8,128)(2,1)S(1)}, u32[]{:S(2)}, u32[]{:S(2)}) collective-permute-start(bf16[2,2,16,1024]{3,2,1,0:T(8,128)(2,1)S(1)} %slice.33), channel_id=1, source_target_pairs={{0,6},{1,7},{2,0},{3,1},{4,2},{5,3},{6,4},{7,5},{8,14},{9,15},{10,... | collective-permute-start | bytes 393224 | tf_op jit(solution)/shard_map/ppermute | solution.py:44
  77.3 4.5 %copy-start.10 = (bf16[2,2,16,1024]{3,2,1,0:T(8,128)(2,1)}, bf16[2,2,16,1024]{3,2,1,0:T(8,128)(2,1)S(1)}, u32[]{:S(2)}) copy-start(bf16[2,2,16,1024]{3,2,1,0:T(8,128)(2,1)S(1)} %collective-permute-done.2.refs_1_.refs_3_) | copy-start | bytes 393220
  77.3 13.7 %collective-permute-start.9 = (bf16[512,768]{1,0:T(8,128)(2,1)}, bf16[512,768]{1,0:T(8,128)(2,1)S(1)}, u32[]{:S(2)}, u32[]{:S(2)}) collective-permute-start(bf16[512,768]{1,0:T(8,128)(2,1)} %shard_map.93.refs_10_), channel_id=1, source_target_pairs={{0,8},{1,9},{2,10},{3,11},{4,12},{5,13},{6,14},{7,15},{8,0},{9,1},... | collective-permute-start | bytes 2359304 | tf_op jit(solution)/shard_map/ppermute | solution.py:44
  77.6 4.2 %copy-start.11 = (bf16[2,2,16,1024]{3,2,1,0:T(8,128)(2,1)}, bf16[2,2,16,1024]{3,2,1,0:T(8,128)(2,1)S(1)}, u32[]{:S(2)}) copy-start(bf16[2,2,16,1024]{3,2,1,0:T(8,128)(2,1)S(1)} %collective-permute-done.3.refs_2_.refs_4_) | copy-start | bytes 393220
  77.6 4.2 %copy-start.8 = (bf16[4,2,16,1024]{3,2,1,0:T(8,128)(2,1)}, bf16[4,2,16,1024]{3,2,1,0:T(8,128)(2,1)S(1)}, u32[]{:S(2)}) copy-start(bf16[4,2,16,1024]{3,2,1,0:T(8,128)(2,1)S(1)} %collective-permute-done.5.refs_3_.refs_6_) | copy-start | bytes 786436
  77.6 4.2 %copy-start.9 = (bf16[4,2,16,1024]{3,2,1,0:T(8,128)(2,1)}, bf16[4,2,16,1024]{3,2,1,0:T(8,128)(2,1)S(1)}, u32[]{:S(2)}) copy-start(bf16[4,2,16,1024]{3,2,1,0:T(8,128)(2,1)S(1)} %collective-permute-done.6.refs_4_.refs_7_) | copy-start | bytes 786436
  81.7 0.9 copy-start.7
  82.6 8.4 %collective-permute-start.11 = (bf16[512,768]{1,0:T(8,128)(2,1)}, bf16[512,768]{1,0:T(8,128)(2,1)S(1)}, u32[]{:S(2)}, u32[]{:S(2)}) collective-permute-start(bf16[512,768]{1,0:T(8,128)(2,1)} %shard_map.94.refs_12_), channel_id=1, source_target_pairs={{0,8},{1,9},{2,10},{3,11},{4,12},{5,13},{6,14},{7,15},{8,0},{9,1},... | collective-permute-start | bytes 2359304 | tf_op jit(solution)/shard_map/ppermute | solution.py:44
  83.5 7.2 %collective-permute-start.7 = (bf16[2,2,16,1024]{3,2,1,0:T(8,128)(2,1)S(1)}, bf16[2,2,16,1024]{3,2,1,0:T(8,128)(2,1)S(1)}, u32[]{:S(2)}, u32[]{:S(2)}) collective-permute-start(bf16[2,2,16,1024]{3,2,1,0:T(8,128)(2,1)S(1)} %slice.34), channel_id=1, source_target_pairs={{0,2},{1,3},{2,4},{3,5},{4,6},{5,7},{6,0},{7,1},{8,10},{9,11},{10,... | collective-permute-start | bytes 393224 | tf_op jit(solution)/shard_map/ppermute | solution.py:44
  85.2 5.8 %collective-permute-start.8 = (bf16[2,2,16,1024]{3,2,1,0:T(8,128)(2,1)S(1)}, bf16[2,2,16,1024]{3,2,1,0:T(8,128)(2,1)S(1)}, u32[]{:S(2)}, u32[]{:S(2)}) collective-permute-start(bf16[2,2,16,1024]{3,2,1,0:T(8,128)(2,1)S(1)} %slice.35), channel_id=1, source_target_pairs={{0,6},{1,7},{2,0},{3,1},{4,2},{5,3},{6,4},{7,5},{8,14},{9,15},{10,... | collective-permute-start | bytes 393224 | tf_op jit(solution)/shard_map/ppermute | solution.py:44
  90.7 0.7 copy-start.18
  91.0 0.6 copy-start.19
  91.0 0.9 copy-start.15
  91.9 0.9 copy-start.16
  99.0 14.7 %collective-permute-start.12 = (bf16[128,768]{1,0:T(8,128)(2,1)}, bf16[128,768]{1,0:T(8,128)(2,1)S(1)}, u32[]{:S(2)}, u32[]{:S(2)}) collective-permute-start(bf16[128,768]{1,0:T(8,128)(2,1)} %get-tuple-element.17), channel_id=1, source_target_pairs={{0,80},{1,81},{2,82},{3,83},{4,84},{5,85},{6,86},{7,87},{8,88},{9,... | collective-permute-start | bytes 589832 | tf_op jit(solution)/shard_map/ppermute | solution.py:44
  101.0 15.7 %collective-permute-start.13 = (bf16[128,768]{1,0:T(8,128)(2,1)}, bf16[128,768]{1,0:T(8,128)(2,1)S(1)}, u32[]{:S(2)}, u32[]{:S(2)}) collective-permute-start(bf16[128,768]{1,0:T(8,128)(2,1)} %get-tuple-element.18), channel_id=1, source_target_pairs={{0,64},{1,65},{2,66},{3,67},{4,68},{5,69},{6,70},{7,71},{8,72},{9,... | collective-permute-start | bytes 589832 | tf_op jit(solution)/shard_map/ppermute | solution.py:44
  102.9 13.9 %collective-permute-start.14 = (bf16[128,768]{1,0:T(8,128)(2,1)}, bf16[128,768]{1,0:T(8,128)(2,1)S(1)}, u32[]{:S(2)}, u32[]{:S(2)}) collective-permute-start(bf16[128,768]{1,0:T(8,128)(2,1)} %get-tuple-element.19), channel_id=1, source_target_pairs={{0,16},{1,17},{2,18},{3,19},{4,20},{5,21},{6,22},{7,23},{8,24},{9,... | collective-permute-start | bytes 589832 | tf_op jit(solution)/shard_map/ppermute | solution.py:44
  104.7 3.4 %copy-start = (bf16[64,1,512,128]{3,2,1,0:T(8,128)(2,1)S(1)}, bf16[64,1,512,128]{3,2,1,0:T(8,128)(2,1)}, u32[]{:S(2)}) copy-start(bf16[64,1,512,128]{3,2,1,0:T(8,128)(2,1)} %param.15) | copy-start | bytes 25165828
  108.1 3.4 %copy-start.1 = (bf16[64,1,512,128]{3,2,1,0:T(8,128)(2,1)S(1)}, bf16[64,1,512,128]{3,2,1,0:T(8,128)(2,1)}, u32[]{:S(2)}) copy-start(bf16[64,1,512,128]{3,2,1,0:T(8,128)(2,1)} %param.16) | copy-start | bytes 25165828
  111.5 0.9 copy-start.3
  112.4 4.4 %copy-start.4 = (bf16[128,768]{1,0:T(8,128)(2,1)S(1)}, bf16[128,768]{1,0:T(8,128)(2,1)}, u32[]{:S(2)}) copy-start(bf16[128,768]{1,0:T(8,128)(2,1)} %get-tuple-element.16.refs_2_.refs_0_) | copy-start | bytes 589828
  122.8 5.4 %collective-permute-start.19 = (bf16[128,512]{1,0:T(8,128)(2,1)S(1)}, bf16[128,512]{1,0:T(8,128)(2,1)S(1)}, u32[]{:S(2)}, u32[]{:S(2)}) collective-permute-start(bf16[128,512]{1,0:T(8,128)(2,1)S(1)} %shard_map.97.refs_1_.refs_0_), channel_id=1, source_target_pairs={{0,1},{1,0},{2,3},{3,2},{4,5},{5,4},{6,7},{7,6},{8,9},{9,8},{10,11... | collective-permute-start | bytes 393224 | tf_op jit(solution)/shard_map/ppermute | solution.py:44
  122.9 8.9 %collective-permute-start.15 = (bf16[128,512]{1,0:T(8,128)(2,1)S(1)}, bf16[128,512]{1,0:T(8,128)(2,1)S(1)}, u32[]{:S(2)}, u32[]{:S(2)}) collective-permute-start(bf16[128,512]{1,0:T(8,128)(2,1)S(1)} %shard_map.97.refs_1_.refs_0_), channel_id=1, source_target_pairs={{0,2},{1,3},{2,4},{3,5},{4,6},{5,7},{6,0},{7,1},{8,10},{9,11},{10,... | collective-permute-start | bytes 393224 | tf_op jit(solution)/shard_map/ppermute | solution.py:44
  123.3 8.7 %collective-permute-start.16 = (bf16[128,512]{1,0:T(8,128)(2,1)S(1)}, bf16[128,512]{1,0:T(8,128)(2,1)S(1)}, u32[]{:S(2)}, u32[]{:S(2)}) collective-permute-start(bf16[128,512]{1,0:T(8,128)(2,1)S(1)} %shard_map.97.refs_1_.refs_0_), channel_id=1, source_target_pairs={{0,6},{1,7},{2,0},{3,1},{4,2},{5,3},{6,4},{7,5},{8,14},{9,15},{10,... | collective-permute-start | bytes 393224 | tf_op jit(solution)/shard_map/ppermute | solution.py:44
  128.2 7.3 %collective-permute-start.20 = (bf16[128,512]{1,0:T(8,128)(2,1)S(1)}, bf16[128,512]{1,0:T(8,128)(2,1)S(1)}, u32[]{:S(2)}, u32[]{:S(2)}) collective-permute-start(bf16[128,512]{1,0:T(8,128)(2,1)S(1)} %collective-permute-done.19.refs_5_), channel_id=1, source_target_pairs={{0,2},{1,3},{2,4},{3,5},{4,6},{5,7},{6,0},{7,1},{8,10},{9,11},{10,... | collective-permute-start | bytes 393224 | tf_op jit(solution)/shard_map/ppermute | solution.py:44
  128.8 6.7 %collective-permute-start.21 = (bf16[128,512]{1,0:T(8,128)(2,1)S(1)}, bf16[128,512]{1,0:T(8,128)(2,1)S(1)}, u32[]{:S(2)}, u32[]{:S(2)}) collective-permute-start(bf16[128,512]{1,0:T(8,128)(2,1)S(1)} %collective-permute-done.19.refs_5_), channel_id=1, source_target_pairs={{0,6},{1,7},{2,0},{3,1},{4,2},{5,3},{6,4},{7,5},{8,14},{9,15},{10,... | collective-permute-start | bytes 393224 | tf_op jit(solution)/shard_map/ppermute | solution.py:44
  131.9 11.0 %collective-permute-start.17 = (bf16[64,512]{1,0:T(8,128)(2,1)S(1)}, bf16[64,512]{1,0:T(8,128)(2,1)S(1)}, u32[]{:S(2)}, u32[]{:S(2)}) collective-permute-start(bf16[64,512]{1,0:T(8,128)(2,1)S(1)} %slice.36), channel_id=1, source_target_pairs={{0,2},{1,3},{2,4},{3,5},{4,6},{5,7},{6,0},{7,1},{8,10},{9,11},{10,... | collective-permute-start | bytes 196616 | tf_op jit(solution)/shard_map/ppermute | solution.py:44
  132.0 10.9 %collective-permute-start.18 = (bf16[64,512]{1,0:T(8,128)(2,1)S(1)}, bf16[64,512]{1,0:T(8,128)(2,1)S(1)}, u32[]{:S(2)}, u32[]{:S(2)}) collective-permute-start(bf16[64,512]{1,0:T(8,128)(2,1)S(1)} %slice.37), channel_id=1, source_target_pairs={{0,6},{1,7},{2,0},{3,1},{4,2},{5,3},{6,4},{7,5},{8,14},{9,15},{10,... | collective-permute-start | bytes 196616 | tf_op jit(solution)/shard_map/ppermute | solution.py:44
  135.5 7.4 %collective-permute-start.22 = (bf16[64,512]{1,0:T(8,128)(2,1)S(1)}, bf16[64,512]{1,0:T(8,128)(2,1)S(1)}, u32[]{:S(2)}, u32[]{:S(2)}) collective-permute-start(bf16[64,512]{1,0:T(8,128)(2,1)S(1)} %slice.38), channel_id=1, source_target_pairs={{0,2},{1,3},{2,4},{3,5},{4,6},{5,7},{6,0},{7,1},{8,10},{9,11},{10,... | collective-permute-start | bytes 196616 | tf_op jit(solution)/shard_map/ppermute | solution.py:44
  135.5 7.4 %copy-start.5 = (s32[5]{0:T(128)S(1)}, s32[5]{0:T(128)}, u32[]{:S(2)}) copy-start(s32[5]{0:T(128)} %stack.23.place) | copy-start | bytes 64
  135.5 7.3 %collective-permute-start.23 = (bf16[64,512]{1,0:T(8,128)(2,1)S(1)}, bf16[64,512]{1,0:T(8,128)(2,1)S(1)}, u32[]{:S(2)}, u32[]{:S(2)}) collective-permute-start(bf16[64,512]{1,0:T(8,128)(2,1)S(1)} %slice.39), channel_id=1, source_target_pairs={{0,6},{1,7},{2,0},{3,1},{4,2},{5,3},{6,4},{7,5},{8,14},{9,15},{10,... | collective-permute-start | bytes 196616 | tf_op jit(solution)/shard_map/ppermute | solution.py:44
  138.8 3.4 %copy-start.2 = (bf16[4096,1024]{1,0:T(8,128)(2,1)S(1)}, bf16[4096,1024]{1,0:T(8,128)(2,1)}, u32[]{:S(2)}) copy-start(bf16[4096,1024]{1,0:T(8,128)(2,1)} %all-gather.2.cloned.1.call-done.refs_0_) | copy-start | bytes 25165828
Sparse Core Ops, SparseCore 0:
  42.6 92.3 all-gather.1

commit v3 on v2

--- a/solution.py
+++ b/solution.py
@@ -95,48 +95,53 @@
     return copies
 
 
-def pack_kernel(query, key, value, out_weight, inputs, packed):
+def pack_kernel(count, *refs):
+    arrays, out = refs[:count], refs[-1]
+    for t in range(out.shape[0]):
+        first = 0
+        for array in arrays:
+            columns = array.shape[1] // 8
+            begin = (t % 8) * columns
+            out[t, :, first : first + columns] = array[:, begin : begin + columns]
+            first += columns
+
+
+def pack(arrays, places):
+    depth = arrays[0].shape[0]
+    columns = sum(array.shape[1] for array in arrays) // 8
+    vmem = pl.BlockSpec(memory_space=pltpu.VMEM)
+    return pl.pallas_call(
+        functools.partial(pack_kernel, len(arrays)),
+        out_shape=jax.ShapeDtypeStruct((places, depth, columns), jnp.bfloat16),
+        in_specs=[vmem] * len(arrays),
+        out_specs=vmem,
+        compiler_params=pltpu.CompilerParams(vmem_limit_bytes=VMEM_BYTES),
+    )(*arrays)
+
+
+def mix_kernel(out_weight, inputs, packed):
     rows = inputs.shape[0] // 8
-    deep = out_weight.shape[0]
-    wide, narrow = query.shape[1] // 8, key.shape[1] // 8
     width = inputs.shape[1]
-    quarter = query.shape[0] // 4
-    strip = width // 4
     for t in range(8):
         packed[t, :rows] = inputs[t * rows : (t + 1) * rows]
-        packed[t, rows : rows + deep] = out_weight[:, t * width : (t + 1) * width]
-        first = rows + deep
-        for q in range(4):
-            part = slice(q * quarter, (q + 1) * quarter)
-            begin = q * strip
-            for n in range(wide // strip):
-                packed[t, first + n * quarter : first + (n + 1) * quarter, begin : begin + strip] = query[
-                    part, t * wide + n * strip : t * wide + (n + 1) * strip
-                ]
-            last = slice(first + wide // strip * quarter, first + (wide // strip + 1) * quarter)
-            packed[t, last, begin : begin + narrow] = key[part, t * narrow : (t + 1) * narrow]
-            packed[t, last, begin + narrow : begin + strip] = value[part, t * narrow : (t + 1) * narrow]
-
-
-def pack(query, key, value, out_weight, inputs):
+        packed[t, rows:] = out_weight[:, t * width : (t + 1) * width]
+
+
+def mix(out_weight, inputs):
     batch, width = inputs.shape
-    depth = query.shape[0]
-    rows = batch // 8 + out_weight.shape[0] + depth * 3 // 4
     vmem = pl.BlockSpec(memory_space=pltpu.VMEM)
     return pl.pallas_call(
-        pack_kernel,
-        out_shape=jax.ShapeDtypeStruct((8, rows, width), jnp.bfloat16),
-        in_specs=[vmem] * 5,
+        mix_kernel,
+        out_shape=jax.ShapeDtypeStruct((8, batch // 8 + out_weight.shape[0], width), jnp.bfloat16),
+        in_specs=[vmem] * 2,
         out_specs=vmem,
         compiler_params=pltpu.CompilerParams(vmem_limit_bytes=VMEM_BYTES),
-    )(query, key, value, out_weight, inputs)
-
-
-def unpack_kernel(packed, gain, normed, weight, out_weight):
+    )(out_weight, inputs)
+
+
+def unpack_kernel(packed, gain, normed, out_weight):
     rows, width = normed.shape[2:]
     deep = out_weight.shape[0] // 8
-    depth = weight.shape[0] // 8
-    quarter, strip = depth // 4, width // 4
     total = None
     for t in range(8):
         values = packed[t, :rows].astype(jnp.float32)
@@ -147,37 +152,29 @@
         values = packed[t, :rows].astype(jnp.float32) * factor
         values = values * gain[t : t + 1, :].astype(jnp.float32)
         normed[(t >> 2) * 2 + (t & 1), (t >> 1) & 1] = values.astype(jnp.bfloat16)
-        out_weight[t * deep : (t + 1) * deep] = packed[t, rows : rows + deep]
-        first = rows + deep
-        for n in range(3):
-            for q in range(4):
-                begin = t * depth + q * quarter
-                weight[begin : begin + quarter, n * strip : (n + 1) * strip] = packed[
-                    t, first + n * quarter : first + (n + 1) * quarter, q * strip : (q + 1) * strip
-                ]
-
-
-def unpack(packed, gain, rows, deep, depth):
-    width = packed.shape[2]
+        out_weight[t * deep : (t + 1) * deep] = packed[t, rows:]
+
+
+def unpack(packed, gain, rows):
+    _, both, width = packed.shape
     vmem = pl.BlockSpec(memory_space=pltpu.VMEM)
     return pl.pallas_call(
         unpack_kernel,
         out_shape=[
             jax.ShapeDtypeStruct((4, 2, rows, width), jnp.bfloat16),
-            jax.ShapeDtypeStruct((8 * depth, width * 3 // 4), jnp.bfloat16),
-            jax.ShapeDtypeStruct((8 * deep, width), jnp.bfloat16),
+            jax.ShapeDtypeStruct((8 * (both - rows), width), jnp.bfloat16),
         ],
         in_specs=[vmem] * 2,
-        out_specs=[vmem] * 3,
+        out_specs=[vmem] * 2,
         compiler_params=pltpu.CompilerParams(vmem_limit_bytes=VMEM_BYTES),
     )(packed, gain)
 
 
 def partial_kernel(place, *refs):
-    blocks, weights, outs, acts, held, sums, sems, more = refs[:10], refs[10:14], refs[14:18], *refs[18:]
+    blocks, weights, outs, acts, held, sums, sems, more = refs[:10], refs[10:12], refs[12:16], *refs[16:]
 
     width = blocks[0].shape[3]
-    half = weights[0].shape[0]
+    half = weights[0].shape[1]
 
     def spots(block, index, part, sem):
         return [
@@ -185,12 +182,10 @@
         ]
 
     copies = settle(place, blocks, spots, sems)
-    here, core, rest = place[4] * 2 + place[0] % 2, place[1], place[0] // 2
+    here, core = place[4] * 2 + place[0] % 2, place[1]
     for i in range(4):
-        first = ((rest ^ (i >> 1)) * 2 + (core ^ (i & 1))) * half
-        copies.append(
-            pltpu.make_async_copy(weights[i], held.at[pl.ds(pl.multiple_of(first, half), half)], more.at[i])
-        )
+        rows = pl.ds(pl.multiple_of(((i >> 1) * 2 + (core ^ (i & 1))) * half, half), half)
+        copies.append(pltpu.make_async_copy(weights[i & 1].at[i >> 1], held.at[rows], more.at[i]))
         copies[-1].start()
     for copy in copies:
         copy.wait()
@@ -203,12 +198,12 @@
 
 def partial_products(place, blocks, weights):
     _, _, rows, width = blocks[0].shape
-    depth, columns = weights[0].shape
+    _, depth, columns = weights[0].shape
     vmem = pl.BlockSpec(memory_space=pltpu.VMEM)
     return pl.pallas_call(
         partial_kernel,
         out_shape=[jax.ShapeDtypeStruct((8 * rows, columns), jnp.bfloat16)] * 4,
-        in_specs=[pl.BlockSpec(memory_space=pltpu.SMEM)] + [pl.BlockSpec(memory_space=pl.ANY)] * 14,
+        in_specs=[pl.BlockSpec(memory_space=pltpu.SMEM)] + [pl.BlockSpec(memory_space=pl.ANY)] * 12,
         out_specs=[vmem] * 4,
         scratch_shapes=[
             pltpu.VMEM((4, 8, rows, 2 * width), jnp.bfloat16),
@@ -419,19 +414,18 @@
         ]
     ).astype(jnp.int32)
 
-    packed = pack(w_query, w_key, w_value, w_out, step_inputs.reshape(batch, width))
+    packed = mix(w_out, step_inputs.reshape(batch, width))
     packed = lax.all_to_all(packed, TP, 0, 0, tiled=True)
-    normed, mine, out_mine = unpack(
-        packed, norm_gain.reshape(8, width), batch // 8, w_out.shape[0], w_query.shape[0]
-    )
+    normed, out_mine = unpack(packed, norm_gain.reshape(8, width), batch // 8)
     out_weight = lax.all_gather(out_mine, REP, axis=0, tiled=True)
 
     moved = lax.all_to_all(normed, SPLIT, 0, 0, tiled=True)
-    mine = tie(mine, moved)
-    far = permute(mine, flipped(REST))
     gathered = ring_gather(moved, "zl", "x1", "x0")
-    far = tie(far, gathered[3], gathered[4], gathered[6], gathered[7])
-    weights = (mine, permute(mine, flipped("c")), far, permute(far, flipped("c")))
+    cut = tie(pack((w_query, w_key, w_value), 16), moved)
+    mine = lax.all_to_all(cut, (REST,) + TP, 0, 0, tiled=True)
+    mine = mine.reshape(2, 8 * cut.shape[1], cut.shape[2])
+    mine = tie(mine, gathered[1], gathered[2], gathered[5])
+    weights = (mine, permute(mine, flipped("c")))
     partial = partial_products(place, gathered, weights)
     caches = stage((key_cache[:, 0], value_cache[:, 0]), partial[0])
     changes = [flipped(SPLIT[0]), flipped(SPLIT[1])]

time: 153 us -> 150 us (0.980)
  blocking collectives: 13.2 us -> 0 us
  starting transfers between devices: 41.5 us -> 51.1 us
    all_to_all x1 -> x0, blocking collectives: 13.2 us -> none  [shards(): moved = lax.all_to_all(normed, SPLIT, 0, 0, tiled=True)]
    all_to_all x1, waiting for transfers between devices: 22.3 us -> 11 us  [shards(): packed = lax.all_to_all(packed, TP, 0, 0, tiled=True)]
    all_to_all x0 -> x2, starting transfers between devices: none -> 11 us  [the longest x1 5.91 us: shards(): moved = lax.all_to_all(normed, SPLIT, 0, 0, tiled=True)]
    ppermute x24 -> x22, waiting for transfers between devices: 20.1 us -> 26 us  [permute(): return lax.ppermute(block, AXES, pairs_of(change))]
    all_to_all x0 -> x2, waiting for transfers between devices: none -> 4.6 us  [the longest x1 4.47 us: shards(): moved = lax.all_to_all(normed, SPLIT, 0, 0, tiled=True)]
    pallas_call x1 -> x2, Pallas kernels: 2.68 us -> 4.46 us  [the longest x1 2.41 us: pack(): pl.pallas_call(functools.partial(pack_kernel, len(arrays)), out_shape=jax...]
    ppermute x24 -> x22, starting transfers between devices: 35.7 us -> 34.1 us  [permute(): return lax.ppermute(block, AXES, pairs_of(change))]
    unnamed x40 -> x38, local copies, waits for them, and re-layouts: 14.9 us -> 14.6 us
  transfers between devices with their start and end apart: 26 -> 26, of which waited for: 10 -> 10; matrix products, arithmetic and copies ran while one was open for 3% -> 3% of each run, Pallas kernels for 9% -> 11%
where the time goes in v3:
time: 150 us; the launch traced here: 149 us
  starting transfers between devices  51.1 us (34%)
  waiting for transfers between devices  41.6 us (28%)
  Pallas kernels  23.5 us (16%)
  local copies, waits for them, and re-layouts  18.6 us (12%)
  between operations  13.7 us (9%)
    ppermute x22, starting transfers between devices, permute(): return lax.ppermute(block, AXES, pairs_of(change))  34.1 us
    ppermute x22, waiting for transfers between devices, permute(): return lax.ppermute(block, AXES, pairs_of(change))  26 us
    unnamed x38, local copies, waits for them, and re-layouts  14.6 us
    all_to_all x1, waiting for transfers between devices, shards(): packed = lax.all_to_all(packed, TP, 0, 0, tiled=True)  11 us
    pallas_call x1, Pallas kernels, partial_products(): pl.pallas_call(partial_kernel, out_shape=[jax.ShapeDtypeStruct((8 * rows,...  6.21 us
    pallas_call x1, Pallas kernels, attention_of(): pl.pallas_call(attention_kernel, out_shape=jax.ShapeDtypeStruct((batch, G...  6.04 us
    all_to_all x1, starting transfers between devices, shards(): moved = lax.all_to_all(normed, SPLIT, 0, 0, tiled=True)  5.91 us
    all_to_all x1, starting transfers between devices, shards(): packed = lax.all_to_all(packed, TP, 0, 0, tiled=True)  5.87 us
  transfers between devices with their start and end apart: 26, of which 10 were waited for; matrix products, arithmetic and copies ran while one was open for 3% of the time, Pallas kernels for 11%

profile of v3, /device:TPU:0, one launch (start us, length us, event | category | flops | bytes accessed | tf_op | source)
XLA Modules:
  0.0 149.0 jit_solution(7999444383094624472)
XLA Ops:
  6.5 2.0 %shard_map.91 = bf16[8,48,1024]{2,1,0:T(8,128)(2,1)} custom-call(bf16[32,8192]{1,0:T(8,128)(2,1)} %out_weight.1, bf16[128,1024]{1,0:T(8,128)(2,1)} %bitcast.13), custom_call_target="tpu_custom_call" | custom-call | tf_op jit(solution)/shard_map/pallas_call | solution.py:133
  8.6 5.9 %all-to-all-start = ((bf16[8,48,1024]{2,1,0:T(8,128)(2,1)}), bf16[8,48,1024]{2,1,0:T(8,128)(2,1)S(1)}, u32[]{:S(2)}, u32[]{:S(2)}) async-start(bf16[8,48,1024]{2,1,0:T(8,128)(2,1)} %shard_map.91), calls=%async_computation | async-start | bytes 1572864 | tf_op jit(solution)/shard_map/all_to_all | solution.py:418
  14.5 0.0 all-gather.2.cloned.1.call-start
  14.5 1.3 reshape.35.gain
  15.8 11.0 %all-to-all-done.packed = bf16[8,48,1024]{2,1,0:T(8,128)(2,1)S(1)} async-done(((bf16[8,48,1024]{2,1,0:T(8,128)(2,1)}), bf16[8,48,1024]{2,1,0:T(8,128)(2,1)S(1)}, u32[]{:S(2)}, u32[]{:S(2)}) %all-to-all-start) | async-done | bytes 786464 | tf_op jit(solution)/shard_map/all_to_all | solution.py:418
  26.8 0.9 copy-done.7
  27.7 2.1 %shard_map.92 = (bf16[4,2,16,1024]{3,2,1,0:T(8,128)(2,1)}, bf16[256,1024]{1,0:T(8,128)(2,1)}) custom-call(bf16[8,48,1024]{2,1,0:T(8,128)(2,1)} %copy-done.7, bf16[8,1024]{1,0:T(8,128)(2,1)} %reshape.35.gain), custom_call_target="tpu_custom_call" | custom-call | tf_op jit(solution)/shard_map/pallas_call | solution.py:161
  29.9 0.0 all-gather.2.cloned.1.call-update
  29.9 5.9 %all-to-all-start.1 = ((bf16[4,2,16,1024]{3,2,1,0:T(8,128)(2,1)}), bf16[4,2,16,1024]{3,2,1,0:T(8,128)(2,1)S(1)}, u32[]{:S(2)}, u32[]{:S(2)}) async-start(bf16[4,2,16,1024]{3,2,1,0:T(8,128)(2,1)} %get-tuple-element.13), calls=%async_computation.1 | async-start | bytes 524288 | tf_op jit(solution)/shard_map/all_to_all | solution.py:422
  35.8 2.4 %shard_map.93.refs_0_ = bf16[16,64,768]{2,1,0:T(8,128)(2,1)} custom-call(bf16[64,4096]{1,0:T(8,128)(2,1)} %refs_0_.1, bf16[64,1024]{1,0:T(8,128)(2,1)} %refs_1_.1, bf16[64,1024]{1,0:T(8,128)(2,1)} %refs_2_.1), custom_call_target="tpu_custom_call" | custom-call | tf_op jit(solution)/shard_map/pallas_call | solution.py:113
  38.2 4.5 %all-to-all-done.1.refs_1_.refs_0_ = bf16[4,2,16,1024]{3,2,1,0:T(8,128)(2,1)S(1)} async-done(((bf16[4,2,16,1024]{3,2,1,0:T(8,128)(2,1)}), bf16[4,2,16,1024]{3,2,1,0:T(8,128)(2,1)S(1)}, u32[]{:S(2)}, u32[]{:S(2)}) %all-to-all-start.1) | async-done | bytes 262176 | tf_op jit(solution)/shard_map/all_to_all | solution.py:422
  42.7 0.7 copy-done.8
  43.4 5.1 %all-to-all-start.2 = ((bf16[16,64,768]{2,1,0:T(8,128)(2,1)}), bf16[16,64,768]{2,1,0:T(8,128)(2,1)S(1)}, u32[]{:S(2)}, u32[]{:S(2)}) async-start(bf16[16,64,768]{2,1,0:T(8,128)(2,1)} %shard_map.94), calls=%async_computation.2 | async-start | bytes 3145728 | tf_op jit(solution)/shard_map/all_to_all | solution.py:425
  48.5 1.9 %collective-permute-start.4 = (bf16[4,2,16,1024]{3,2,1,0:T(8,128)(2,1)}, bf16[4,2,16,1024]{3,2,1,0:T(8,128)(2,1)S(1)}, u32[]{:S(2)}, u32[]{:S(2)}) collective-permute-start(bf16[4,2,16,1024]{3,2,1,0:T(8,128)(2,1)} %copy-done.8), channel_id=1, source_target_pairs={{0,1},{1,0},{2,3},{3,2},{4,5},{5,4},{6,7},{7,6},{8,9},{9,8},{10,11... | collective-permute-start | bytes 786440 | tf_op jit(solution)/shard_map/ppermute | solution.py:44
  50.4 1.5 collective-permute-start
  51.9 1.8 %collective-permute-start.1 = (bf16[4,2,16,1024]{3,2,1,0:T(8,128)(2,1)}, bf16[4,2,16,1024]{3,2,1,0:T(8,128)(2,1)S(1)}, u32[]{:S(2)}, u32[]{:S(2)}) collective-permute-start(bf16[4,2,16,1024]{3,2,1,0:T(8,128)(2,1)} %copy-done.8), channel_id=1, source_target_pairs={{0,6},{1,7},{2,0},{3,1},{4,2},{5,3},{6,4},{7,5},{8,14},{9,15},{10,... | collective-permute-start | bytes 786440 | tf_op jit(solution)/shard_map/ppermute | solution.py:44
  53.6 4.4 %collective-permute-done.4.refs_3_.refs_5_ = bf16[4,2,16,1024]{3,2,1,0:T(8,128)(2,1)S(1)} collective-permute-done((bf16[4,2,16,1024]{3,2,1,0:T(8,128)(2,1)}, bf16[4,2,16,1024]{3,2,1,0:T(8,128)(2,1)S(1)}, u32[]{:S(2)}, u32[]{:S(2)}) %collective-permute-start.4) | collective-permute-done | bytes 262176 | tf_op jit(solution)/shard_map/ppermute | solution.py:44
  58.1 14.5 %collective-permute-done.refs_1_ = bf16[4,2,16,1024]{3,2,1,0:T(8,128)(2,1)S(1)} collective-permute-done((bf16[4,2,16,1024]{3,2,1,0:T(8,128)(2,1)}, bf16[4,2,16,1024]{3,2,1,0:T(8,128)(2,1)S(1)}, u32[]{:S(2)}, u32[]{:S(2)}) %collective-permute-start) | collective-permute-done | bytes 262176 | tf_op jit(solution)/shard_map/ppermute | solution.py:44
  72.6 0.1 all-to-all-done.2
  72.7 0.6 copy-done.9
  73.3 0.1 copy-done.10
  73.4 0.5 copy-done.6
  73.9 1.3 collective-permute-start.5
  75.2 1.9 %collective-permute-start.6 = (bf16[4,2,16,1024]{3,2,1,0:T(8,128)(2,1)}, bf16[4,2,16,1024]{3,2,1,0:T(8,128)(2,1)S(1)}, u32[]{:S(2)}, u32[]{:S(2)}) collective-permute-start(bf16[4,2,16,1024]{3,2,1,0:T(8,128)(2,1)} %copy-done.11), channel_id=1, source_target_pairs={{0,6},{1,7},{2,0},{3,1},{4,2},{5,3},{6,4},{7,5},{8,14},{9,15},{10,... | collective-permute-start | bytes 786440 | tf_op jit(solution)/shard_map/ppermute | solution.py:44
  77.2 0.9 slice.32
  78.1 0.2 collective-permute-start.2
  78.2 0.9 slice.33
  79.1 3.3 %collective-permute-start.3 = (bf16[2,2,16,1024]{3,2,1,0:T(8,128)(2,1)S(1)}, bf16[2,2,16,1024]{3,2,1,0:T(8,128)(2,1)S(1)}, u32[]{:S(2)}, u32[]{:S(2)}) collective-permute-start(bf16[2,2,16,1024]{3,2,1,0:T(8,128)(2,1)S(1)} %slice.33), channel_id=1, source_target_pairs={{0,6},{1,7},{2,0},{3,1},{4,2},{5,3},{6,4},{7,5},{8,14},{9,15},{10,... | collective-permute-start | bytes 393224 | tf_op jit(solution)/shard_map/ppermute | solution.py:44
  82.4 2.0 %collective-permute-done.5.refs_6_ = bf16[4,2,16,1024]{3,2,1,0:T(8,128)(2,1)S(1)} collective-permute-done((bf16[4,2,16,1024]{3,2,1,0:T(8,128)(2,1)}, bf16[4,2,16,1024]{3,2,1,0:T(8,128)(2,1)S(1)}, u32[]{:S(2)}, u32[]{:S(2)}) %collective-permute-start.5) | collective-permute-done | bytes 262176 | tf_op jit(solution)/shard_map/ppermute | solution.py:44
  84.5 0.2 collective-permute-start.7
  84.6 3.2 %collective-permute-start.8 = (bf16[2,2,16,1024]{3,2,1,0:T(8,128)(2,1)S(1)}, bf16[2,2,16,1024]{3,2,1,0:T(8,128)(2,1)S(1)}, u32[]{:S(2)}, u32[]{:S(2)}) collective-permute-start(bf16[2,2,16,1024]{3,2,1,0:T(8,128)(2,1)S(1)} %slice.35), channel_id=1, source_target_pairs={{0,6},{1,7},{2,0},{3,1},{4,2},{5,3},{6,4},{7,5},{8,14},{9,15},{10,... | collective-permute-start | bytes 393224 | tf_op jit(solution)/shard_map/ppermute | solution.py:44
  87.9 0.1 convert_element_type.18
  87.9 0.6 stack.23.place
  88.6 2.1 %collective-permute-done.7.refs_8_ = bf16[2,2,16,1024]{3,2,1,0:T(8,128)(2,1)S(1)} collective-permute-done((bf16[2,2,16,1024]{3,2,1,0:T(8,128)(2,1)S(1)}, bf16[2,2,16,1024]{3,2,1,0:T(8,128)(2,1)S(1)}, u32[]{:S(2)}, u32[]{:S(2)}) %collective-permute-start.7) | collective-permute-done | bytes 131104 | tf_op jit(solution)/shard_map/ppermute | solution.py:44
  90.8 0.6 copy-done.17
  91.4 0.0 copy-done.18
  91.4 6.2 %shard_map.96 = (bf16[128,768]{1,0:T(8,128)(2,1)}, bf16[128,768]{1,0:T(8,128)(2,1)}, bf16[128,768]{1,0:T(8,128)(2,1)}, bf16[128,768]{1,0:T(8,128)(2,1)}) custom-call(s32[5]{0:T(128)} %stack.23.place, bf16[4,2,16,1024]{3,2,1,0:T(8,128)(2,1)} %copy-done.8, bf16[4,2,16,1024]{3,2,1,0:T(8,128)(2,1)} %copy-done.9, bf16[4,2,16,1024]{3,2,1,0:T(8,128)(2,1)} %copy-done.10, ...), custom_call_target="tpu_custom_call" | custom-call | flops 1610612736 | bytes 8388608 | tf_op jit(solution)/shard_map/pallas_call | solution.py:203
  97.6 2.8 %collective-permute-start.10 = (bf16[128,768]{1,0:T(8,128)(2,1)}, bf16[128,768]{1,0:T(8,128)(2,1)S(1)}, u32[]{:S(2)}, u32[]{:S(2)}) collective-permute-start(bf16[128,768]{1,0:T(8,128)(2,1)} %get-tuple-element.15), channel_id=1, source_target_pairs={{0,80},{1,81},{2,82},{3,83},{4,84},{5,85},{6,86},{7,87},{8,88},{9,... | collective-permute-start | bytes 589832 | tf_op jit(solution)/shard_map/ppermute | solution.py:44
  100.4 1.9 %collective-permute-start.11 = (bf16[128,768]{1,0:T(8,128)(2,1)}, bf16[128,768]{1,0:T(8,128)(2,1)S(1)}, u32[]{:S(2)}, u32[]{:S(2)}) collective-permute-start(bf16[128,768]{1,0:T(8,128)(2,1)} %get-tuple-element.16), channel_id=1, source_target_pairs={{0,64},{1,65},{2,66},{3,67},{4,68},{5,69},{6,70},{7,71},{8,72},{9,... | collective-permute-start | bytes 589832 | tf_op jit(solution)/shard_map/ppermute | solution.py:44
  102.4 0.3 collective-permute-start.12
  102.7 0.3 fusion
  103.0 0.1 broadcast_in_dim.2
  103.1 0.1 broadcast_in_dim_reshape.4.lengths
  103.2 0.1 pad_maximum_fusion
  103.3 0.0 copy-start
  103.3 3.4 %copy-done = bf16[64,1,512,128]{3,2,1,0:T(8,128)(2,1)S(1)} copy-done((bf16[64,1,512,128]{3,2,1,0:T(8,128)(2,1)S(1)}, bf16[64,1,512,128]{3,2,1,0:T(8,128)(2,1)}, u32[]{:S(2)}) %copy-start) | copy-done | bytes 8388632
  106.7 3.4 %copy-done.1 = bf16[64,1,512,128]{3,2,1,0:T(8,128)(2,1)S(1)} copy-done((bf16[64,1,512,128]{3,2,1,0:T(8,128)(2,1)S(1)}, bf16[64,1,512,128]{3,2,1,0:T(8,128)(2,1)}, u32[]{:S(2)}) %copy-start.1) | copy-done | bytes 8388632
  110.1 0.9 copy-done.3
  111.0 1.3 shard_map.97
  112.3 1.4 collective-permute-done.11.refs_2_
  113.7 6.0 %shard_map.98.refs_1_.refs_0_ = bf16[128,512]{1,0:T(8,128)(2,1)S(1)} custom-call(s32[512,1]{1,0:T(8,128)S(1)} %broadcast_in_dim_reshape.4.lengths, bf16[128,768]{1,0:T(8,128)(2,1)S(1)} %copy-done.4, bf16[128,768]{1,0:T(8,128)(2,1)S(1)} %collective-permute-done.10.refs_1_, bf16[128,768]{1,0:T(8,128)(2,1)S(1)} %collective-permute-done.11.refs_2_, ...), custom_call_target="tpu_custom_call" | custom-call | flops 134217728 | bytes 16777216 | tf_op jit(solution)/shard_map/pallas_call | solution.py:383
  119.8 0.7 collective-permute-start.17
  120.5 1.4 collective-permute-start.13
  122.0 1.8 %collective-permute-start.14 = (bf16[128,512]{1,0:T(8,128)(2,1)S(1)}, bf16[128,512]{1,0:T(8,128)(2,1)S(1)}, u32[]{:S(2)}, u32[]{:S(2)}) collective-permute-start(bf16[128,512]{1,0:T(8,128)(2,1)S(1)} %shard_map.98.refs_1_.refs_0_), channel_id=1, source_target_pairs={{0,6},{1,7},{2,0},{3,1},{4,2},{5,3},{6,4},{7,5},{8,14},{9,15},{10,... | collective-permute-start | bytes 393224 | tf_op jit(solution)/shard_map/ppermute | solution.py:44
  123.8 1.3 collective-permute-done.17.refs_5_
  125.0 1.2 collective-permute-start.18
  126.3 2.0 %collective-permute-start.19 = (bf16[128,512]{1,0:T(8,128)(2,1)S(1)}, bf16[128,512]{1,0:T(8,128)(2,1)S(1)}, u32[]{:S(2)}, u32[]{:S(2)}) collective-permute-start(bf16[128,512]{1,0:T(8,128)(2,1)S(1)} %collective-permute-done.17.refs_5_), channel_id=1, source_target_pairs={{0,6},{1,7},{2,0},{3,1},{4,2},{5,3},{6,4},{7,5},{8,14},{9,15},{10,... | collective-permute-start | bytes 393224 | tf_op jit(solution)/shard_map/ppermute | solution.py:44
  128.3 0.1 collective-permute-start.15
  128.4 3.3 %collective-permute-start.16 = (bf16[64,512]{1,0:T(8,128)(2,1)S(1)}, bf16[64,512]{1,0:T(8,128)(2,1)S(1)}, u32[]{:S(2)}, u32[]{:S(2)}) collective-permute-start(bf16[64,512]{1,0:T(8,128)(2,1)S(1)} %slice.37), channel_id=1, source_target_pairs={{0,6},{1,7},{2,0},{3,1},{4,2},{5,3},{6,4},{7,5},{8,14},{9,15},{10,... | collective-permute-start | bytes 196616 | tf_op jit(solution)/shard_map/ppermute | solution.py:44
  131.7 0.2 collective-permute-done.18.refs_6_
  132.0 3.3 %collective-permute-start.21 = (bf16[64,512]{1,0:T(8,128)(2,1)S(1)}, bf16[64,512]{1,0:T(8,128)(2,1)S(1)}, u32[]{:S(2)}, u32[]{:S(2)}) collective-permute-start(bf16[64,512]{1,0:T(8,128)(2,1)S(1)} %slice.39), channel_id=1, source_target_pairs={{0,6},{1,7},{2,0},{3,1},{4,2},{5,3},{6,4},{7,5},{8,14},{9,15},{10,... | collective-permute-start | bytes 196616 | tf_op jit(solution)/shard_map/ppermute | solution.py:44
  135.3 3.4 %copy-done.2 = bf16[4096,1024]{1,0:T(8,128)(2,1)S(1)} copy-done((bf16[4096,1024]{1,0:T(8,128)(2,1)S(1)}, bf16[4096,1024]{1,0:T(8,128)(2,1)}, u32[]{:S(2)}) %copy-start.2) | copy-done | bytes 8388632
  138.6 0.6 shard_map.99.refs_10_
  139.3 2.8 %shard_map.100 = bf16[128,1024]{1,0:T(8,128)(2,1)} custom-call(s32[5]{0:T(128)S(1)} %copy-done.5, bf16[128,512]{1,0:T(8,128)(2,1)S(1)} %shard_map.98.refs_1_.refs_0_, bf16[128,512]{1,0:T(8,128)(2,1)S(1)} %collective-permute-done.13.refs_1_, bf16[128,512]{1,0:T(8,128)(2,1)S(1)} %collective-permute-done.14.refs_2_, ...), custom_call_target="tpu_custom_call" | custom-call | flops 1073741824 | bytes 10485760 | tf_op jit(solution)/shard_map/pallas_call | solution.py:238
  (54 shorter events, 0.1 us)
Async XLA Ops:
  8.6 79.3 %copy-start.14 = (s32[64]{0:T(128)S(1)}, s32[64]{0:T(128)}, u32[]{:S(2)}) copy-start(s32[64]{0:T(128)} %param.17) | copy-start | bytes 772
  8.6 18.2 %all-to-all-start = ((bf16[8,48,1024]{2,1,0:T(8,128)(2,1)}), bf16[8,48,1024]{2,1,0:T(8,128)(2,1)S(1)}, u32[]{:S(2)}, u32[]{:S(2)}) async-start(bf16[8,48,1024]{2,1,0:T(8,128)(2,1)} %shard_map.91), calls=%async_computation | async-start | bytes 1572864 | tf_op jit(solution)/shard_map/all_to_all | solution.py:418
  14.5 120.8 %all-gather.2.cloned.1.call-start = ((), (), s32[]{:S(2)}) async-start(), calls=%async_computation.3 | async-start | bytes 8912896 | tf_op jit(solution)/shard_map/all_gather | solution.py:420
  26.8 0.9 copy-start.7
  29.9 12.8 %all-to-all-start.1 = ((bf16[4,2,16,1024]{3,2,1,0:T(8,128)(2,1)}), bf16[4,2,16,1024]{3,2,1,0:T(8,128)(2,1)S(1)}, u32[]{:S(2)}, u32[]{:S(2)}) async-start(bf16[4,2,16,1024]{3,2,1,0:T(8,128)(2,1)} %get-tuple-element.13), calls=%async_computation.1 | async-start | bytes 524288 | tf_op jit(solution)/shard_map/all_to_all | solution.py:422
  42.7 0.7 copy-start.8
  43.4 29.3 %all-to-all-start.2 = ((bf16[16,64,768]{2,1,0:T(8,128)(2,1)}), bf16[16,64,768]{2,1,0:T(8,128)(2,1)S(1)}, u32[]{:S(2)}, u32[]{:S(2)}) async-start(bf16[16,64,768]{2,1,0:T(8,128)(2,1)} %shard_map.94), calls=%async_computation.2 | async-start | bytes 3145728 | tf_op jit(solution)/shard_map/all_to_all | solution.py:425
  48.5 9.6 %collective-permute-start.4 = (bf16[4,2,16,1024]{3,2,1,0:T(8,128)(2,1)}, bf16[4,2,16,1024]{3,2,1,0:T(8,128)(2,1)S(1)}, u32[]{:S(2)}, u32[]{:S(2)}) collective-permute-start(bf16[4,2,16,1024]{3,2,1,0:T(8,128)(2,1)} %copy-done.8), channel_id=1, source_target_pairs={{0,1},{1,0},{2,3},{3,2},{4,5},{5,4},{6,7},{7,6},{8,9},{9,8},{10,11... | collective-permute-start | bytes 786440 | tf_op jit(solution)/shard_map/ppermute | solution.py:44
  50.4 22.2 %collective-permute-start = (bf16[4,2,16,1024]{3,2,1,0:T(8,128)(2,1)}, bf16[4,2,16,1024]{3,2,1,0:T(8,128)(2,1)S(1)}, u32[]{:S(2)}, u32[]{:S(2)}) collective-permute-start(bf16[4,2,16,1024]{3,2,1,0:T(8,128)(2,1)} %copy-done.8), channel_id=1, source_target_pairs={{0,2},{1,3},{2,4},{3,5},{4,6},{5,7},{6,0},{7,1},{8,10},{9,11},{10,... | collective-permute-start | bytes 786440 | tf_op jit(solution)/shard_map/ppermute | solution.py:44
  51.9 20.7 %collective-permute-start.1 = (bf16[4,2,16,1024]{3,2,1,0:T(8,128)(2,1)}, bf16[4,2,16,1024]{3,2,1,0:T(8,128)(2,1)S(1)}, u32[]{:S(2)}, u32[]{:S(2)}) collective-permute-start(bf16[4,2,16,1024]{3,2,1,0:T(8,128)(2,1)} %copy-done.8), channel_id=1, source_target_pairs={{0,6},{1,7},{2,0},{3,1},{4,2},{5,3},{6,4},{7,5},{8,14},{9,15},{10,... | collective-permute-start | bytes 786440 | tf_op jit(solution)/shard_map/ppermute | solution.py:44
  58.1 14.6 %copy-start.11 = (bf16[4,2,16,1024]{3,2,1,0:T(8,128)(2,1)}, bf16[4,2,16,1024]{3,2,1,0:T(8,128)(2,1)S(1)}, u32[]{:S(2)}) copy-start(bf16[4,2,16,1024]{3,2,1,0:T(8,128)(2,1)S(1)} %collective-permute-done.4.refs_3_.refs_5_) | copy-start | bytes 786436
  72.6 0.7 copy-start.9
  72.6 0.8 copy-start.10
  72.7 1.2 copy-start.6
  73.9 16.8 %collective-permute-start.9 = (bf16[2,512,768]{2,1,0:T(8,128)(2,1)}, bf16[2,512,768]{2,1,0:T(8,128)(2,1)}, u32[]{:S(2)}, u32[]{:S(2)}) collective-permute-start(bf16[2,512,768]{2,1,0:T(8,128)(2,1)} %shard_map.95.refs_10_), channel_id=1, source_target_pairs={{0,8},{1,9},{2,10},{3,11},{4,12},{5,13},{6,14},{7,15},{8,0},{9,1},... | collective-permute-start | bytes 4718600 | tf_op jit(solution)/shard_map/ppermute | solution.py:44
  73.9 10.5 %collective-permute-start.5 = (bf16[4,2,16,1024]{3,2,1,0:T(8,128)(2,1)}, bf16[4,2,16,1024]{3,2,1,0:T(8,128)(2,1)S(1)}, u32[]{:S(2)}, u32[]{:S(2)}) collective-permute-start(bf16[4,2,16,1024]{3,2,1,0:T(8,128)(2,1)} %copy-done.11), channel_id=1, source_target_pairs={{0,2},{1,3},{2,4},{3,5},{4,6},{5,7},{6,0},{7,1},{8,10},{9,11},{10,... | collective-permute-start | bytes 786440 | tf_op jit(solution)/shard_map/ppermute | solution.py:44
  75.2 9.4 %collective-permute-start.6 = (bf16[4,2,16,1024]{3,2,1,0:T(8,128)(2,1)}, bf16[4,2,16,1024]{3,2,1,0:T(8,128)(2,1)S(1)}, u32[]{:S(2)}, u32[]{:S(2)}) collective-permute-start(bf16[4,2,16,1024]{3,2,1,0:T(8,128)(2,1)} %copy-done.11), channel_id=1, source_target_pairs={{0,6},{1,7},{2,0},{3,1},{4,2},{5,3},{6,4},{7,5},{8,14},{9,15},{10,... | collective-permute-start | bytes 786440 | tf_op jit(solution)/shard_map/ppermute | solution.py:44
  78.1 10.5 %collective-permute-start.2 = (bf16[2,2,16,1024]{3,2,1,0:T(8,128)(2,1)S(1)}, bf16[2,2,16,1024]{3,2,1,0:T(8,128)(2,1)S(1)}, u32[]{:S(2)}, u32[]{:S(2)}) collective-permute-start(bf16[2,2,16,1024]{3,2,1,0:T(8,128)(2,1)S(1)} %slice.32), channel_id=1, source_target_pairs={{0,2},{1,3},{2,4},{3,5},{4,6},{5,7},{6,0},{7,1},{8,10},{9,11},{10,... | collective-permute-start | bytes 393224 | tf_op jit(solution)/shard_map/ppermute | solution.py:44
  79.1 9.4 %collective-permute-start.3 = (bf16[2,2,16,1024]{3,2,1,0:T(8,128)(2,1)S(1)}, bf16[2,2,16,1024]{3,2,1,0:T(8,128)(2,1)S(1)}, u32[]{:S(2)}, u32[]{:S(2)}) collective-permute-start(bf16[2,2,16,1024]{3,2,1,0:T(8,128)(2,1)S(1)} %slice.33), channel_id=1, source_target_pairs={{0,6},{1,7},{2,0},{3,1},{4,2},{5,3},{6,4},{7,5},{8,14},{9,15},{10,... | collective-permute-start | bytes 393224 | tf_op jit(solution)/shard_map/ppermute | solution.py:44
  84.4 6.3 %copy-start.12 = (bf16[4,2,16,1024]{3,2,1,0:T(8,128)(2,1)}, bf16[4,2,16,1024]{3,2,1,0:T(8,128)(2,1)S(1)}, u32[]{:S(2)}) copy-start(bf16[4,2,16,1024]{3,2,1,0:T(8,128)(2,1)S(1)} %collective-permute-done.5.refs_6_) | copy-start | bytes 786436
  84.5 6.2 %collective-permute-start.7 = (bf16[2,2,16,1024]{3,2,1,0:T(8,128)(2,1)S(1)}, bf16[2,2,16,1024]{3,2,1,0:T(8,128)(2,1)S(1)}, u32[]{:S(2)}, u32[]{:S(2)}) collective-permute-start(bf16[2,2,16,1024]{3,2,1,0:T(8,128)(2,1)S(1)} %slice.34), channel_id=1, source_target_pairs={{0,2},{1,3},{2,4},{3,5},{4,6},{5,7},{6,0},{7,1},{8,10},{9,11},{10,... | collective-permute-start | bytes 393224 | tf_op jit(solution)/shard_map/ppermute | solution.py:44
  84.6 6.1 %copy-start.13 = (bf16[4,2,16,1024]{3,2,1,0:T(8,128)(2,1)}, bf16[4,2,16,1024]{3,2,1,0:T(8,128)(2,1)S(1)}, u32[]{:S(2)}) copy-start(bf16[4,2,16,1024]{3,2,1,0:T(8,128)(2,1)S(1)} %collective-permute-done.6.refs_7_) | copy-start | bytes 786436
  84.6 6.1 %collective-permute-start.8 = (bf16[2,2,16,1024]{3,2,1,0:T(8,128)(2,1)S(1)}, bf16[2,2,16,1024]{3,2,1,0:T(8,128)(2,1)S(1)}, u32[]{:S(2)}, u32[]{:S(2)}) collective-permute-start(bf16[2,2,16,1024]{3,2,1,0:T(8,128)(2,1)S(1)} %slice.35), channel_id=1, source_target_pairs={{0,6},{1,7},{2,0},{3,1},{4,2},{5,3},{6,4},{7,5},{8,14},{9,15},{10,... | collective-permute-start | bytes 393224 | tf_op jit(solution)/shard_map/ppermute | solution.py:44
  88.6 2.2 %copy-start.15 = (bf16[2,2,16,1024]{3,2,1,0:T(8,128)(2,1)}, bf16[2,2,16,1024]{3,2,1,0:T(8,128)(2,1)S(1)}, u32[]{:S(2)}) copy-start(bf16[2,2,16,1024]{3,2,1,0:T(8,128)(2,1)S(1)} %collective-permute-done.2.refs_3_) | copy-start | bytes 393220
  88.6 2.2 %copy-start.16 = (bf16[2,2,16,1024]{3,2,1,0:T(8,128)(2,1)}, bf16[2,2,16,1024]{3,2,1,0:T(8,128)(2,1)S(1)}, u32[]{:S(2)}) copy-start(bf16[2,2,16,1024]{3,2,1,0:T(8,128)(2,1)S(1)} %collective-permute-done.3.refs_4_) | copy-start | bytes 393220
  90.7 0.7 copy-start.17
  90.7 0.7 copy-start.18
  97.6 14.7 %collective-permute-start.10 = (bf16[128,768]{1,0:T(8,128)(2,1)}, bf16[128,768]{1,0:T(8,128)(2,1)S(1)}, u32[]{:S(2)}, u32[]{:S(2)}) collective-permute-start(bf16[128,768]{1,0:T(8,128)(2,1)} %get-tuple-element.15), channel_id=1, source_target_pairs={{0,80},{1,81},{2,82},{3,83},{4,84},{5,85},{6,86},{7,87},{8,88},{9,... | collective-permute-start | bytes 589832 | tf_op jit(solution)/shard_map/ppermute | solution.py:44
  100.4 13.3 %collective-permute-start.11 = (bf16[128,768]{1,0:T(8,128)(2,1)}, bf16[128,768]{1,0:T(8,128)(2,1)S(1)}, u32[]{:S(2)}, u32[]{:S(2)}) collective-permute-start(bf16[128,768]{1,0:T(8,128)(2,1)} %get-tuple-element.16), channel_id=1, source_target_pairs={{0,64},{1,65},{2,66},{3,67},{4,68},{5,69},{6,70},{7,71},{8,72},{9,... | collective-permute-start | bytes 589832 | tf_op jit(solution)/shard_map/ppermute | solution.py:44
  102.4 11.4 %collective-permute-start.12 = (bf16[128,768]{1,0:T(8,128)(2,1)}, bf16[128,768]{1,0:T(8,128)(2,1)S(1)}, u32[]{:S(2)}, u32[]{:S(2)}) collective-permute-start(bf16[128,768]{1,0:T(8,128)(2,1)} %get-tuple-element.17), channel_id=1, source_target_pairs={{0,16},{1,17},{2,18},{3,19},{4,20},{5,21},{6,22},{7,23},{8,24},{9,... | collective-permute-start | bytes 589832 | tf_op jit(solution)/shard_map/ppermute | solution.py:44
  103.3 3.4 %copy-start = (bf16[64,1,512,128]{3,2,1,0:T(8,128)(2,1)S(1)}, bf16[64,1,512,128]{3,2,1,0:T(8,128)(2,1)}, u32[]{:S(2)}) copy-start(bf16[64,1,512,128]{3,2,1,0:T(8,128)(2,1)} %param.15) | copy-start | bytes 25165828
  106.7 3.4 %copy-start.1 = (bf16[64,1,512,128]{3,2,1,0:T(8,128)(2,1)S(1)}, bf16[64,1,512,128]{3,2,1,0:T(8,128)(2,1)}, u32[]{:S(2)}) copy-start(bf16[64,1,512,128]{3,2,1,0:T(8,128)(2,1)} %param.16) | copy-start | bytes 25165828
  110.1 0.9 copy-start.3
  111.0 2.7 %copy-start.4 = (bf16[128,768]{1,0:T(8,128)(2,1)S(1)}, bf16[128,768]{1,0:T(8,128)(2,1)}, u32[]{:S(2)}) copy-start(bf16[128,768]{1,0:T(8,128)(2,1)} %get-tuple-element.14.refs_2_.refs_0_) | copy-start | bytes 589828
  119.8 5.3 %collective-permute-start.17 = (bf16[128,512]{1,0:T(8,128)(2,1)S(1)}, bf16[128,512]{1,0:T(8,128)(2,1)S(1)}, u32[]{:S(2)}, u32[]{:S(2)}) collective-permute-start(bf16[128,512]{1,0:T(8,128)(2,1)S(1)} %shard_map.98.refs_1_.refs_0_), channel_id=1, source_target_pairs={{0,1},{1,0},{2,3},{3,2},{4,5},{5,4},{6,7},{7,6},{8,9},{9,8},{10,11... | collective-permute-start | bytes 393224 | tf_op jit(solution)/shard_map/ppermute | solution.py:44
  120.5 7.8 %collective-permute-start.13 = (bf16[128,512]{1,0:T(8,128)(2,1)S(1)}, bf16[128,512]{1,0:T(8,128)(2,1)S(1)}, u32[]{:S(2)}, u32[]{:S(2)}) collective-permute-start(bf16[128,512]{1,0:T(8,128)(2,1)S(1)} %shard_map.98.refs_1_.refs_0_), channel_id=1, source_target_pairs={{0,2},{1,3},{2,4},{3,5},{4,6},{5,7},{6,0},{7,1},{8,10},{9,11},{10,... | collective-permute-start | bytes 393224 | tf_op jit(solution)/shard_map/ppermute | solution.py:44
  122.0 6.5 %collective-permute-start.14 = (bf16[128,512]{1,0:T(8,128)(2,1)S(1)}, bf16[128,512]{1,0:T(8,128)(2,1)S(1)}, u32[]{:S(2)}, u32[]{:S(2)}) collective-permute-start(bf16[128,512]{1,0:T(8,128)(2,1)S(1)} %shard_map.98.refs_1_.refs_0_), channel_id=1, source_target_pairs={{0,6},{1,7},{2,0},{3,1},{4,2},{5,3},{6,4},{7,5},{8,14},{9,15},{10,... | collective-permute-start | bytes 393224 | tf_op jit(solution)/shard_map/ppermute | solution.py:44
  125.0 6.9 %collective-permute-start.18 = (bf16[128,512]{1,0:T(8,128)(2,1)S(1)}, bf16[128,512]{1,0:T(8,128)(2,1)S(1)}, u32[]{:S(2)}, u32[]{:S(2)}) collective-permute-start(bf16[128,512]{1,0:T(8,128)(2,1)S(1)} %collective-permute-done.17.refs_5_), channel_id=1, source_target_pairs={{0,2},{1,3},{2,4},{3,5},{4,6},{5,7},{6,0},{7,1},{8,10},{9,11},{10,... | collective-permute-start | bytes 393224 | tf_op jit(solution)/shard_map/ppermute | solution.py:44
  126.3 5.7 %collective-permute-start.19 = (bf16[128,512]{1,0:T(8,128)(2,1)S(1)}, bf16[128,512]{1,0:T(8,128)(2,1)S(1)}, u32[]{:S(2)}, u32[]{:S(2)}) collective-permute-start(bf16[128,512]{1,0:T(8,128)(2,1)S(1)} %collective-permute-done.17.refs_5_), channel_id=1, source_target_pairs={{0,6},{1,7},{2,0},{3,1},{4,2},{5,3},{6,4},{7,5},{8,14},{9,15},{10,... | collective-permute-start | bytes 393224 | tf_op jit(solution)/shard_map/ppermute | solution.py:44
  128.3 11.0 %collective-permute-start.15 = (bf16[64,512]{1,0:T(8,128)(2,1)S(1)}, bf16[64,512]{1,0:T(8,128)(2,1)S(1)}, u32[]{:S(2)}, u32[]{:S(2)}) collective-permute-start(bf16[64,512]{1,0:T(8,128)(2,1)S(1)} %slice.36), channel_id=1, source_target_pairs={{0,2},{1,3},{2,4},{3,5},{4,6},{5,7},{6,0},{7,1},{8,10},{9,11},{10,... | collective-permute-start | bytes 196616 | tf_op jit(solution)/shard_map/ppermute | solution.py:44
  128.4 10.9 %collective-permute-start.16 = (bf16[64,512]{1,0:T(8,128)(2,1)S(1)}, bf16[64,512]{1,0:T(8,128)(2,1)S(1)}, u32[]{:S(2)}, u32[]{:S(2)}) collective-permute-start(bf16[64,512]{1,0:T(8,128)(2,1)S(1)} %slice.37), channel_id=1, source_target_pairs={{0,6},{1,7},{2,0},{3,1},{4,2},{5,3},{6,4},{7,5},{8,14},{9,15},{10,... | collective-permute-start | bytes 196616 | tf_op jit(solution)/shard_map/ppermute | solution.py:44
  131.9 7.4 %collective-permute-start.20 = (bf16[64,512]{1,0:T(8,128)(2,1)S(1)}, bf16[64,512]{1,0:T(8,128)(2,1)S(1)}, u32[]{:S(2)}, u32[]{:S(2)}) collective-permute-start(bf16[64,512]{1,0:T(8,128)(2,1)S(1)} %slice.38), channel_id=1, source_target_pairs={{0,2},{1,3},{2,4},{3,5},{4,6},{5,7},{6,0},{7,1},{8,10},{9,11},{10,... | collective-permute-start | bytes 196616 | tf_op jit(solution)/shard_map/ppermute | solution.py:44
  132.0 7.4 %copy-start.5 = (s32[5]{0:T(128)S(1)}, s32[5]{0:T(128)}, u32[]{:S(2)}) copy-start(s32[5]{0:T(128)} %stack.23.place) | copy-start | bytes 64
  132.0 7.3 %collective-permute-start.21 = (bf16[64,512]{1,0:T(8,128)(2,1)S(1)}, bf16[64,512]{1,0:T(8,128)(2,1)S(1)}, u32[]{:S(2)}, u32[]{:S(2)}) collective-permute-start(bf16[64,512]{1,0:T(8,128)(2,1)S(1)} %slice.39), channel_id=1, source_target_pairs={{0,6},{1,7},{2,0},{3,1},{4,2},{5,3},{6,4},{7,5},{8,14},{9,15},{10,... | collective-permute-start | bytes 196616 | tf_op jit(solution)/shard_map/ppermute | solution.py:44
  135.3 3.4 %copy-start.2 = (bf16[4096,1024]{1,0:T(8,128)(2,1)S(1)}, bf16[4096,1024]{1,0:T(8,128)(2,1)}, u32[]{:S(2)}) copy-start(bf16[4096,1024]{1,0:T(8,128)(2,1)} %all-gather.2.cloned.1.call-done.refs_0_) | copy-start | bytes 25165828
Sparse Core Ops, SparseCore 0:
  30.0 94.6 all-gather.1

commit v4 on v3

--- a/solution.py
+++ b/solution.py
@@ -119,22 +119,30 @@
     )(*arrays)
 
 
-def mix_kernel(out_weight, inputs, packed):
+def mix_kernel(out_weight, inputs, packed, sems):
     rows = inputs.shape[0] // 8
-    width = inputs.shape[1]
+    deep, width = out_weight.shape[0], inputs.shape[1]
+    copies = []
     for t in range(8):
-        packed[t, :rows] = inputs[t * rows : (t + 1) * rows]
-        packed[t, rows:] = out_weight[:, t * width : (t + 1) * width]
+        mine = inputs.at[pl.ds(t * rows, rows)]
+        cut = out_weight.at[:, pl.ds(t * width, width)]
+        copies.append(pltpu.make_async_copy(mine, packed.at[t, pl.ds(0, rows)], sems.at[t, 0]))
+        copies.append(pltpu.make_async_copy(cut, packed.at[t, pl.ds(rows, deep)], sems.at[t, 1]))
+    for copy in copies:
+        copy.start()
+    for copy in copies:
+        copy.wait()
 
 
 def mix(out_weight, inputs):
     batch, width = inputs.shape
-    vmem = pl.BlockSpec(memory_space=pltpu.VMEM)
+    anywhere = pl.BlockSpec(memory_space=pl.ANY)
     return pl.pallas_call(
         mix_kernel,
         out_shape=jax.ShapeDtypeStruct((8, batch // 8 + out_weight.shape[0], width), jnp.bfloat16),
-        in_specs=[vmem] * 2,
-        out_specs=vmem,
+        in_specs=[anywhere] * 2,
+        out_specs=pl.BlockSpec(memory_space=pltpu.VMEM),
+        scratch_shapes=[pltpu.SemaphoreType.DMA((8, 2))],
         compiler_params=pltpu.CompilerParams(vmem_limit_bytes=VMEM_BYTES),
     )(out_weight, inputs)
 
@@ -375,7 +383,7 @@
             out[s * rows : (s + 1) * rows, k * HD : (k + 1) * HD] = sums[:, s * GROUP + k, :].astype(out.dtype)
 
 
-def attention_of(parts, cosine, sine, key_cache, value_cache, lengths, chunk=8):
+def attention_of(parts, cosine, sine, key_cache, value_cache, lengths, chunk=64):
     batch, columns = parts[0].shape
     rows, spots, _ = key_cache.shape
     heads = STEPS * GROUP

time: 150 us -> 147 us (0.980)
  Pallas kernels: 23.5 us -> 21.2 us
    pallas_call x1, Pallas kernels: 6.04 us -> 3.57 us  [attention_of(): pl.pallas_call(attention_kernel, out_shape=jax.ShapeDtypeStruct((batch, G...]
  transfers between devices with their start and end apart: 26 -> 26, of which waited for: 10 -> 10; matrix products, arithmetic and copies ran while one was open for 3% -> 3% of each run, Pallas kernels for 11% -> 10%
where the time goes in v4:
time: 147 us
  starting transfers between devices  51 us (35%)
  waiting for transfers between devices  41.5 us (28%)
  Pallas kernels  21.2 us (14%)
  local copies, waits for them, and re-layouts  18.7 us (13%)
  between operations  13.7 us (9%)
    ppermute x22, starting transfers between devices, permute(): return lax.ppermute(block, AXES, pairs_of(change))  34.2 us
    ppermute x22, waiting for transfers between devices, permute(): return lax.ppermute(block, AXES, pairs_of(change))  25.9 us
    unnamed x38, local copies, waits for them, and re-layouts  14.6 us
    all_to_all x1, waiting for transfers between devices, shards(): packed = lax.all_to_all(packed, TP, 0, 0, tiled=True)  11 us
    pallas_call x1, Pallas kernels, partial_products(): pl.pallas_call(partial_kernel, out_shape=[jax.ShapeDtypeStruct((8 * rows,...  6.21 us
    all_to_all x1, starting transfers between devices, shards(): moved = lax.all_to_all(normed, SPLIT, 0, 0, tiled=True)  5.91 us
    all_to_all x1, starting transfers between devices, shards(): packed = lax.all_to_all(packed, TP, 0, 0, tiled=True)  5.75 us
    all_to_all x1, starting transfers between devices, shards(): mine = lax.all_to_all(cut, (REST,) + TP, 0, 0, tiled=True)  5.1 us
  transfers between devices with their start and end apart: 26, of which 10 were waited for; matrix products, arithmetic and copies ran while one was open for 3% of the time, Pallas kernels for 10%

profile of v4, /device:TPU:0, one launch (start us, length us, event | category | flops | bytes accessed | tf_op | source)
XLA Modules:
  0.0 146.5 jit_solution(6238623683449995661)
XLA Ops:
  6.5 2.2 %shard_map.91 = bf16[8,48,1024]{2,1,0:T(8,128)(2,1)} custom-call(bf16[32,8192]{1,0:T(8,128)(2,1)} %out_weight.1, bf16[128,1024]{1,0:T(8,128)(2,1)} %bitcast.13), custom_call_target="tpu_custom_call" | custom-call | tf_op jit(solution)/shard_map/pallas_call | solution.py:140
  8.7 0.0 copy-start.14
  8.7 5.7 %all-to-all-start = ((bf16[8,48,1024]{2,1,0:T(8,128)(2,1)}), bf16[8,48,1024]{2,1,0:T(8,128)(2,1)S(1)}, u32[]{:S(2)}, u32[]{:S(2)}) async-start(bf16[8,48,1024]{2,1,0:T(8,128)(2,1)} %shard_map.91), calls=%async_computation | async-start | bytes 1572864 | tf_op jit(solution)/shard_map/all_to_all | solution.py:426
  14.5 0.0 all-gather.2.cloned.1.call-start
  14.5 1.3 reshape.35.gain
  15.9 11.0 %all-to-all-done.packed = bf16[8,48,1024]{2,1,0:T(8,128)(2,1)S(1)} async-done(((bf16[8,48,1024]{2,1,0:T(8,128)(2,1)}), bf16[8,48,1024]{2,1,0:T(8,128)(2,1)S(1)}, u32[]{:S(2)}, u32[]{:S(2)}) %all-to-all-start) | async-done | bytes 786464 | tf_op jit(solution)/shard_map/all_to_all | solution.py:426
  26.9 0.9 copy-done.7
  27.8 2.1 %shard_map.92 = (bf16[4,2,16,1024]{3,2,1,0:T(8,128)(2,1)}, bf16[256,1024]{1,0:T(8,128)(2,1)}) custom-call(bf16[8,48,1024]{2,1,0:T(8,128)(2,1)} %copy-done.7, bf16[8,1024]{1,0:T(8,128)(2,1)} %reshape.35.gain), custom_call_target="tpu_custom_call" | custom-call | tf_op jit(solution)/shard_map/pallas_call | solution.py:169
  29.9 0.0 all-gather.2.cloned.1.call-update
  29.9 5.9 %all-to-all-start.1 = ((bf16[4,2,16,1024]{3,2,1,0:T(8,128)(2,1)}), bf16[4,2,16,1024]{3,2,1,0:T(8,128)(2,1)S(1)}, u32[]{:S(2)}, u32[]{:S(2)}) async-start(bf16[4,2,16,1024]{3,2,1,0:T(8,128)(2,1)} %get-tuple-element.13), calls=%async_computation.1 | async-start | bytes 524288 | tf_op jit(solution)/shard_map/all_to_all | solution.py:430
  35.8 2.4 %shard_map.93.refs_0_ = bf16[16,64,768]{2,1,0:T(8,128)(2,1)} custom-call(bf16[64,4096]{1,0:T(8,128)(2,1)} %refs_0_.1, bf16[64,1024]{1,0:T(8,128)(2,1)} %refs_1_.1, bf16[64,1024]{1,0:T(8,128)(2,1)} %refs_2_.1), custom_call_target="tpu_custom_call" | custom-call | tf_op jit(solution)/shard_map/pallas_call | solution.py:113
  38.2 4.5 %all-to-all-done.1.refs_1_.refs_0_ = bf16[4,2,16,1024]{3,2,1,0:T(8,128)(2,1)S(1)} async-done(((bf16[4,2,16,1024]{3,2,1,0:T(8,128)(2,1)}), bf16[4,2,16,1024]{3,2,1,0:T(8,128)(2,1)S(1)}, u32[]{:S(2)}, u32[]{:S(2)}) %all-to-all-start.1) | async-done | bytes 262176 | tf_op jit(solution)/shard_map/all_to_all | solution.py:430
  42.7 0.7 copy-done.8
  43.4 5.1 %all-to-all-start.2 = ((bf16[16,64,768]{2,1,0:T(8,128)(2,1)}), bf16[16,64,768]{2,1,0:T(8,128)(2,1)S(1)}, u32[]{:S(2)}, u32[]{:S(2)}) async-start(bf16[16,64,768]{2,1,0:T(8,128)(2,1)} %shard_map.94), calls=%async_computation.2 | async-start | bytes 3145728 | tf_op jit(solution)/shard_map/all_to_all | solution.py:433
  48.5 1.9 %collective-permute-start.4 = (bf16[4,2,16,1024]{3,2,1,0:T(8,128)(2,1)}, bf16[4,2,16,1024]{3,2,1,0:T(8,128)(2,1)S(1)}, u32[]{:S(2)}, u32[]{:S(2)}) collective-permute-start(bf16[4,2,16,1024]{3,2,1,0:T(8,128)(2,1)} %copy-done.8), channel_id=1, source_target_pairs={{0,1},{1,0},{2,3},{3,2},{4,5},{5,4},{6,7},{7,6},{8,9},{9,8},{10,11... | collective-permute-start | bytes 786440 | tf_op jit(solution)/shard_map/ppermute | solution.py:44
  50.4 1.5 collective-permute-start
  51.9 1.8 %collective-permute-start.1 = (bf16[4,2,16,1024]{3,2,1,0:T(8,128)(2,1)}, bf16[4,2,16,1024]{3,2,1,0:T(8,128)(2,1)S(1)}, u32[]{:S(2)}, u32[]{:S(2)}) collective-permute-start(bf16[4,2,16,1024]{3,2,1,0:T(8,128)(2,1)} %copy-done.8), channel_id=1, source_target_pairs={{0,6},{1,7},{2,0},{3,1},{4,2},{5,3},{6,4},{7,5},{8,14},{9,15},{10,... | collective-permute-start | bytes 786440 | tf_op jit(solution)/shard_map/ppermute | solution.py:44
  53.7 4.4 %collective-permute-done.4.refs_3_.refs_5_ = bf16[4,2,16,1024]{3,2,1,0:T(8,128)(2,1)S(1)} collective-permute-done((bf16[4,2,16,1024]{3,2,1,0:T(8,128)(2,1)}, bf16[4,2,16,1024]{3,2,1,0:T(8,128)(2,1)S(1)}, u32[]{:S(2)}, u32[]{:S(2)}) %collective-permute-start.4) | collective-permute-done | bytes 262176 | tf_op jit(solution)/shard_map/ppermute | solution.py:44
  58.1 14.5 %collective-permute-done.refs_1_ = bf16[4,2,16,1024]{3,2,1,0:T(8,128)(2,1)S(1)} collective-permute-done((bf16[4,2,16,1024]{3,2,1,0:T(8,128)(2,1)}, bf16[4,2,16,1024]{3,2,1,0:T(8,128)(2,1)S(1)}, u32[]{:S(2)}, u32[]{:S(2)}) %collective-permute-start) | collective-permute-done | bytes 262176 | tf_op jit(solution)/shard_map/ppermute | solution.py:44
  72.6 0.1 all-to-all-done.2
  72.7 0.6 copy-done.9
  73.3 0.1 copy-done.10
  73.5 0.5 copy-done.6
  74.0 1.3 collective-permute-start.5
  75.3 1.9 %collective-permute-start.6 = (bf16[4,2,16,1024]{3,2,1,0:T(8,128)(2,1)}, bf16[4,2,16,1024]{3,2,1,0:T(8,128)(2,1)S(1)}, u32[]{:S(2)}, u32[]{:S(2)}) collective-permute-start(bf16[4,2,16,1024]{3,2,1,0:T(8,128)(2,1)} %copy-done.11), channel_id=1, source_target_pairs={{0,6},{1,7},{2,0},{3,1},{4,2},{5,3},{6,4},{7,5},{8,14},{9,15},{10,... | collective-permute-start | bytes 786440 | tf_op jit(solution)/shard_map/ppermute | solution.py:44
  77.2 0.9 slice.32
  78.1 0.2 collective-permute-start.2
  78.3 0.9 slice.33
  79.2 3.3 %collective-permute-start.3 = (bf16[2,2,16,1024]{3,2,1,0:T(8,128)(2,1)S(1)}, bf16[2,2,16,1024]{3,2,1,0:T(8,128)(2,1)S(1)}, u32[]{:S(2)}, u32[]{:S(2)}) collective-permute-start(bf16[2,2,16,1024]{3,2,1,0:T(8,128)(2,1)S(1)} %slice.33), channel_id=1, source_target_pairs={{0,6},{1,7},{2,0},{3,1},{4,2},{5,3},{6,4},{7,5},{8,14},{9,15},{10,... | collective-permute-start | bytes 393224 | tf_op jit(solution)/shard_map/ppermute | solution.py:44
  82.5 2.0 %collective-permute-done.5.refs_6_ = bf16[4,2,16,1024]{3,2,1,0:T(8,128)(2,1)S(1)} collective-permute-done((bf16[4,2,16,1024]{3,2,1,0:T(8,128)(2,1)}, bf16[4,2,16,1024]{3,2,1,0:T(8,128)(2,1)S(1)}, u32[]{:S(2)}, u32[]{:S(2)}) %collective-permute-start.5) | collective-permute-done | bytes 262176 | tf_op jit(solution)/shard_map/ppermute | solution.py:44
  84.5 0.2 collective-permute-start.7
  84.7 3.2 %collective-permute-start.8 = (bf16[2,2,16,1024]{3,2,1,0:T(8,128)(2,1)S(1)}, bf16[2,2,16,1024]{3,2,1,0:T(8,128)(2,1)S(1)}, u32[]{:S(2)}, u32[]{:S(2)}) collective-permute-start(bf16[2,2,16,1024]{3,2,1,0:T(8,128)(2,1)S(1)} %slice.35), channel_id=1, source_target_pairs={{0,6},{1,7},{2,0},{3,1},{4,2},{5,3},{6,4},{7,5},{8,14},{9,15},{10,... | collective-permute-start | bytes 393224 | tf_op jit(solution)/shard_map/ppermute | solution.py:44
  87.9 0.1 convert_element_type.18
  88.0 0.6 stack.23.place
  88.6 2.1 %collective-permute-done.7.refs_8_ = bf16[2,2,16,1024]{3,2,1,0:T(8,128)(2,1)S(1)} collective-permute-done((bf16[2,2,16,1024]{3,2,1,0:T(8,128)(2,1)S(1)}, bf16[2,2,16,1024]{3,2,1,0:T(8,128)(2,1)S(1)}, u32[]{:S(2)}, u32[]{:S(2)}) %collective-permute-start.7) | collective-permute-done | bytes 131104 | tf_op jit(solution)/shard_map/ppermute | solution.py:44
  90.8 0.6 copy-done.17
  91.4 0.0 copy-done.18
  91.5 6.2 %shard_map.96 = (bf16[128,768]{1,0:T(8,128)(2,1)}, bf16[128,768]{1,0:T(8,128)(2,1)}, bf16[128,768]{1,0:T(8,128)(2,1)}, bf16[128,768]{1,0:T(8,128)(2,1)}) custom-call(s32[5]{0:T(128)} %stack.23.place, bf16[4,2,16,1024]{3,2,1,0:T(8,128)(2,1)} %copy-done.8, bf16[4,2,16,1024]{3,2,1,0:T(8,128)(2,1)} %copy-done.9, bf16[4,2,16,1024]{3,2,1,0:T(8,128)(2,1)} %copy-done.10, ...), custom_call_target="tpu_custom_call" | custom-call | flops 1610612736 | bytes 8388608 | tf_op jit(solution)/shard_map/pallas_call | solution.py:211
  97.7 2.8 %collective-permute-start.10 = (bf16[128,768]{1,0:T(8,128)(2,1)}, bf16[128,768]{1,0:T(8,128)(2,1)S(1)}, u32[]{:S(2)}, u32[]{:S(2)}) collective-permute-start(bf16[128,768]{1,0:T(8,128)(2,1)} %get-tuple-element.15), channel_id=1, source_target_pairs={{0,80},{1,81},{2,82},{3,83},{4,84},{5,85},{6,86},{7,87},{8,88},{9,... | collective-permute-start | bytes 589832 | tf_op jit(solution)/shard_map/ppermute | solution.py:44
  100.4 1.9 %collective-permute-start.11 = (bf16[128,768]{1,0:T(8,128)(2,1)}, bf16[128,768]{1,0:T(8,128)(2,1)S(1)}, u32[]{:S(2)}, u32[]{:S(2)}) collective-permute-start(bf16[128,768]{1,0:T(8,128)(2,1)} %get-tuple-element.16), channel_id=1, source_target_pairs={{0,64},{1,65},{2,66},{3,67},{4,68},{5,69},{6,70},{7,71},{8,72},{9,... | collective-permute-start | bytes 589832 | tf_op jit(solution)/shard_map/ppermute | solution.py:44
  102.4 0.3 collective-permute-start.12
  102.7 0.3 fusion
  103.1 0.1 broadcast_in_dim.2
  103.1 0.1 broadcast_in_dim_reshape.4.lengths
  103.3 0.1 pad_maximum_fusion
  103.4 3.4 %copy-done = bf16[64,1,512,128]{3,2,1,0:T(8,128)(2,1)S(1)} copy-done((bf16[64,1,512,128]{3,2,1,0:T(8,128)(2,1)S(1)}, bf16[64,1,512,128]{3,2,1,0:T(8,128)(2,1)}, u32[]{:S(2)}) %copy-start) | copy-done | bytes 8388632
  106.8 3.4 %copy-done.1 = bf16[64,1,512,128]{3,2,1,0:T(8,128)(2,1)S(1)} copy-done((bf16[64,1,512,128]{3,2,1,0:T(8,128)(2,1)S(1)}, bf16[64,1,512,128]{3,2,1,0:T(8,128)(2,1)}, u32[]{:S(2)}) %copy-start.1) | copy-done | bytes 8388632
  110.1 0.9 copy-done.3
  111.1 1.3 shard_map.97
  112.4 1.4 collective-permute-done.11.refs_2_
  113.8 3.6 %shard_map.98.refs_1_.refs_0_ = bf16[128,512]{1,0:T(8,128)(2,1)S(1)} custom-call(s32[512,1]{1,0:T(8,128)S(1)} %broadcast_in_dim_reshape.4.lengths, bf16[128,768]{1,0:T(8,128)(2,1)S(1)} %copy-done.4, bf16[128,768]{1,0:T(8,128)(2,1)S(1)} %collective-permute-done.10.refs_1_, bf16[128,768]{1,0:T(8,128)(2,1)S(1)} %collective-permute-done.11.refs_2_, ...), custom_call_target="tpu_custom_call" | custom-call | flops 134217728 | bytes 16777216 | tf_op jit(solution)/shard_map/pallas_call | solution.py:391
  117.3 0.7 collective-permute-start.17
  118.1 1.4 collective-permute-start.13
  119.5 1.8 %collective-permute-start.14 = (bf16[128,512]{1,0:T(8,128)(2,1)S(1)}, bf16[128,512]{1,0:T(8,128)(2,1)S(1)}, u32[]{:S(2)}, u32[]{:S(2)}) collective-permute-start(bf16[128,512]{1,0:T(8,128)(2,1)S(1)} %shard_map.98.refs_1_.refs_0_), channel_id=1, source_target_pairs={{0,6},{1,7},{2,0},{3,1},{4,2},{5,3},{6,4},{7,5},{8,14},{9,15},{10,... | collective-permute-start | bytes 393224 | tf_op jit(solution)/shard_map/ppermute | solution.py:44
  121.3 1.3 collective-permute-done.17.refs_5_
  122.6 1.2 collective-permute-start.18
  123.9 2.0 %collective-permute-start.19 = (bf16[128,512]{1,0:T(8,128)(2,1)S(1)}, bf16[128,512]{1,0:T(8,128)(2,1)S(1)}, u32[]{:S(2)}, u32[]{:S(2)}) collective-permute-start(bf16[128,512]{1,0:T(8,128)(2,1)S(1)} %collective-permute-done.17.refs_5_), channel_id=1, source_target_pairs={{0,6},{1,7},{2,0},{3,1},{4,2},{5,3},{6,4},{7,5},{8,14},{9,15},{10,... | collective-permute-start | bytes 393224 | tf_op jit(solution)/shard_map/ppermute | solution.py:44
  125.9 0.1 collective-permute-start.15
  126.0 3.3 %collective-permute-start.16 = (bf16[64,512]{1,0:T(8,128)(2,1)S(1)}, bf16[64,512]{1,0:T(8,128)(2,1)S(1)}, u32[]{:S(2)}, u32[]{:S(2)}) collective-permute-start(bf16[64,512]{1,0:T(8,128)(2,1)S(1)} %slice.37), channel_id=1, source_target_pairs={{0,6},{1,7},{2,0},{3,1},{4,2},{5,3},{6,4},{7,5},{8,14},{9,15},{10,... | collective-permute-start | bytes 196616 | tf_op jit(solution)/shard_map/ppermute | solution.py:44
  129.2 0.2 collective-permute-done.18.refs_6_
  129.5 3.3 %collective-permute-start.21 = (bf16[64,512]{1,0:T(8,128)(2,1)S(1)}, bf16[64,512]{1,0:T(8,128)(2,1)S(1)}, u32[]{:S(2)}, u32[]{:S(2)}) collective-permute-start(bf16[64,512]{1,0:T(8,128)(2,1)S(1)} %slice.39), channel_id=1, source_target_pairs={{0,6},{1,7},{2,0},{3,1},{4,2},{5,3},{6,4},{7,5},{8,14},{9,15},{10,... | collective-permute-start | bytes 196616 | tf_op jit(solution)/shard_map/ppermute | solution.py:44
  132.8 3.4 %copy-done.2 = bf16[4096,1024]{1,0:T(8,128)(2,1)S(1)} copy-done((bf16[4096,1024]{1,0:T(8,128)(2,1)S(1)}, bf16[4096,1024]{1,0:T(8,128)(2,1)}, u32[]{:S(2)}) %copy-start.2) | copy-done | bytes 8388632
  136.2 0.6 shard_map.99.refs_10_
  136.9 2.8 %shard_map.100 = bf16[128,1024]{1,0:T(8,128)(2,1)} custom-call(s32[5]{0:T(128)S(1)} %copy-done.5, bf16[128,512]{1,0:T(8,128)(2,1)S(1)} %shard_map.98.refs_1_.refs_0_, bf16[128,512]{1,0:T(8,128)(2,1)S(1)} %collective-permute-done.13.refs_1_, bf16[128,512]{1,0:T(8,128)(2,1)S(1)} %collective-permute-done.14.refs_2_, ...), custom_call_target="tpu_custom_call" | custom-call | flops 1073741824 | bytes 10485760 | tf_op jit(solution)/shard_map/pallas_call | solution.py:246
  (54 shorter events, 0.1 us)
Async XLA Ops:
  8.7 79.2 %copy-start.14 = (s32[64]{0:T(128)S(1)}, s32[64]{0:T(128)}, u32[]{:S(2)}) copy-start(s32[64]{0:T(128)} %param.17) | copy-start | bytes 772
  8.7 18.1 %all-to-all-start = ((bf16[8,48,1024]{2,1,0:T(8,128)(2,1)}), bf16[8,48,1024]{2,1,0:T(8,128)(2,1)S(1)}, u32[]{:S(2)}, u32[]{:S(2)}) async-start(bf16[8,48,1024]{2,1,0:T(8,128)(2,1)} %shard_map.91), calls=%async_computation | async-start | bytes 1572864 | tf_op jit(solution)/shard_map/all_to_all | solution.py:426
  14.5 118.3 %all-gather.2.cloned.1.call-start = ((), (), s32[]{:S(2)}) async-start(), calls=%async_computation.3 | async-start | bytes 8912896 | tf_op jit(solution)/shard_map/all_gather | solution.py:428
  26.9 0.9 copy-start.7
  29.9 12.8 %all-to-all-start.1 = ((bf16[4,2,16,1024]{3,2,1,0:T(8,128)(2,1)}), bf16[4,2,16,1024]{3,2,1,0:T(8,128)(2,1)S(1)}, u32[]{:S(2)}, u32[]{:S(2)}) async-start(bf16[4,2,16,1024]{3,2,1,0:T(8,128)(2,1)} %get-tuple-element.13), calls=%async_computation.1 | async-start | bytes 524288 | tf_op jit(solution)/shard_map/all_to_all | solution.py:430
  42.7 0.7 copy-start.8
  43.4 29.3 %all-to-all-start.2 = ((bf16[16,64,768]{2,1,0:T(8,128)(2,1)}), bf16[16,64,768]{2,1,0:T(8,128)(2,1)S(1)}, u32[]{:S(2)}, u32[]{:S(2)}) async-start(bf16[16,64,768]{2,1,0:T(8,128)(2,1)} %shard_map.94), calls=%async_computation.2 | async-start | bytes 3145728 | tf_op jit(solution)/shard_map/all_to_all | solution.py:433
  48.5 9.6 %collective-permute-start.4 = (bf16[4,2,16,1024]{3,2,1,0:T(8,128)(2,1)}, bf16[4,2,16,1024]{3,2,1,0:T(8,128)(2,1)S(1)}, u32[]{:S(2)}, u32[]{:S(2)}) collective-permute-start(bf16[4,2,16,1024]{3,2,1,0:T(8,128)(2,1)} %copy-done.8), channel_id=1, source_target_pairs={{0,1},{1,0},{2,3},{3,2},{4,5},{5,4},{6,7},{7,6},{8,9},{9,8},{10,11... | collective-permute-start | bytes 786440 | tf_op jit(solution)/shard_map/ppermute | solution.py:44
  50.4 22.2 %collective-permute-start = (bf16[4,2,16,1024]{3,2,1,0:T(8,128)(2,1)}, bf16[4,2,16,1024]{3,2,1,0:T(8,128)(2,1)S(1)}, u32[]{:S(2)}, u32[]{:S(2)}) collective-permute-start(bf16[4,2,16,1024]{3,2,1,0:T(8,128)(2,1)} %copy-done.8), channel_id=1, source_target_pairs={{0,2},{1,3},{2,4},{3,5},{4,6},{5,7},{6,0},{7,1},{8,10},{9,11},{10,... | collective-permute-start | bytes 786440 | tf_op jit(solution)/shard_map/ppermute | solution.py:44
  51.9 20.7 %collective-permute-start.1 = (bf16[4,2,16,1024]{3,2,1,0:T(8,128)(2,1)}, bf16[4,2,16,1024]{3,2,1,0:T(8,128)(2,1)S(1)}, u32[]{:S(2)}, u32[]{:S(2)}) collective-permute-start(bf16[4,2,16,1024]{3,2,1,0:T(8,128)(2,1)} %copy-done.8), channel_id=1, source_target_pairs={{0,6},{1,7},{2,0},{3,1},{4,2},{5,3},{6,4},{7,5},{8,14},{9,15},{10,... | collective-permute-start | bytes 786440 | tf_op jit(solution)/shard_map/ppermute | solution.py:44
  58.1 14.6 %copy-start.11 = (bf16[4,2,16,1024]{3,2,1,0:T(8,128)(2,1)}, bf16[4,2,16,1024]{3,2,1,0:T(8,128)(2,1)S(1)}, u32[]{:S(2)}) copy-start(bf16[4,2,16,1024]{3,2,1,0:T(8,128)(2,1)S(1)} %collective-permute-done.4.refs_3_.refs_5_) | copy-start | bytes 786436
  72.6 0.7 copy-start.9
  72.6 0.8 copy-start.10
  72.7 1.2 copy-start.6
  74.0 16.8 %collective-permute-start.9 = (bf16[2,512,768]{2,1,0:T(8,128)(2,1)}, bf16[2,512,768]{2,1,0:T(8,128)(2,1)}, u32[]{:S(2)}, u32[]{:S(2)}) collective-permute-start(bf16[2,512,768]{2,1,0:T(8,128)(2,1)} %shard_map.95.refs_10_), channel_id=1, source_target_pairs={{0,8},{1,9},{2,10},{3,11},{4,12},{5,13},{6,14},{7,15},{8,0},{9,1},... | collective-permute-start | bytes 4718600 | tf_op jit(solution)/shard_map/ppermute | solution.py:44
  74.0 10.5 %collective-permute-start.5 = (bf16[4,2,16,1024]{3,2,1,0:T(8,128)(2,1)}, bf16[4,2,16,1024]{3,2,1,0:T(8,128)(2,1)S(1)}, u32[]{:S(2)}, u32[]{:S(2)}) collective-permute-start(bf16[4,2,16,1024]{3,2,1,0:T(8,128)(2,1)} %copy-done.11), channel_id=1, source_target_pairs={{0,2},{1,3},{2,4},{3,5},{4,6},{5,7},{6,0},{7,1},{8,10},{9,11},{10,... | collective-permute-start | bytes 786440 | tf_op jit(solution)/shard_map/ppermute | solution.py:44
  75.3 9.4 %collective-permute-start.6 = (bf16[4,2,16,1024]{3,2,1,0:T(8,128)(2,1)}, bf16[4,2,16,1024]{3,2,1,0:T(8,128)(2,1)S(1)}, u32[]{:S(2)}, u32[]{:S(2)}) collective-permute-start(bf16[4,2,16,1024]{3,2,1,0:T(8,128)(2,1)} %copy-done.11), channel_id=1, source_target_pairs={{0,6},{1,7},{2,0},{3,1},{4,2},{5,3},{6,4},{7,5},{8,14},{9,15},{10,... | collective-permute-start | bytes 786440 | tf_op jit(solution)/shard_map/ppermute | solution.py:44
  78.1 10.5 %collective-permute-start.2 = (bf16[2,2,16,1024]{3,2,1,0:T(8,128)(2,1)S(1)}, bf16[2,2,16,1024]{3,2,1,0:T(8,128)(2,1)S(1)}, u32[]{:S(2)}, u32[]{:S(2)}) collective-permute-start(bf16[2,2,16,1024]{3,2,1,0:T(8,128)(2,1)S(1)} %slice.32), channel_id=1, source_target_pairs={{0,2},{1,3},{2,4},{3,5},{4,6},{5,7},{6,0},{7,1},{8,10},{9,11},{10,... | collective-permute-start | bytes 393224 | tf_op jit(solution)/shard_map/ppermute | solution.py:44
  79.2 9.4 %collective-permute-start.3 = (bf16[2,2,16,1024]{3,2,1,0:T(8,128)(2,1)S(1)}, bf16[2,2,16,1024]{3,2,1,0:T(8,128)(2,1)S(1)}, u32[]{:S(2)}, u32[]{:S(2)}) collective-permute-start(bf16[2,2,16,1024]{3,2,1,0:T(8,128)(2,1)S(1)} %slice.33), channel_id=1, source_target_pairs={{0,6},{1,7},{2,0},{3,1},{4,2},{5,3},{6,4},{7,5},{8,14},{9,15},{10,... | collective-permute-start | bytes 393224 | tf_op jit(solution)/shard_map/ppermute | solution.py:44
  84.5 6.3 %copy-start.12 = (bf16[4,2,16,1024]{3,2,1,0:T(8,128)(2,1)}, bf16[4,2,16,1024]{3,2,1,0:T(8,128)(2,1)S(1)}, u32[]{:S(2)}) copy-start(bf16[4,2,16,1024]{3,2,1,0:T(8,128)(2,1)S(1)} %collective-permute-done.5.refs_6_) | copy-start | bytes 786436
  84.5 6.2 %collective-permute-start.7 = (bf16[2,2,16,1024]{3,2,1,0:T(8,128)(2,1)S(1)}, bf16[2,2,16,1024]{3,2,1,0:T(8,128)(2,1)S(1)}, u32[]{:S(2)}, u32[]{:S(2)}) collective-permute-start(bf16[2,2,16,1024]{3,2,1,0:T(8,128)(2,1)S(1)} %slice.34), channel_id=1, source_target_pairs={{0,2},{1,3},{2,4},{3,5},{4,6},{5,7},{6,0},{7,1},{8,10},{9,11},{10,... | collective-permute-start | bytes 393224 | tf_op jit(solution)/shard_map/ppermute | solution.py:44
  84.7 6.1 %copy-start.13 = (bf16[4,2,16,1024]{3,2,1,0:T(8,128)(2,1)}, bf16[4,2,16,1024]{3,2,1,0:T(8,128)(2,1)S(1)}, u32[]{:S(2)}) copy-start(bf16[4,2,16,1024]{3,2,1,0:T(8,128)(2,1)S(1)} %collective-permute-done.6.refs_7_) | copy-start | bytes 786436
  84.7 6.1 %collective-permute-start.8 = (bf16[2,2,16,1024]{3,2,1,0:T(8,128)(2,1)S(1)}, bf16[2,2,16,1024]{3,2,1,0:T(8,128)(2,1)S(1)}, u32[]{:S(2)}, u32[]{:S(2)}) collective-permute-start(bf16[2,2,16,1024]{3,2,1,0:T(8,128)(2,1)S(1)} %slice.35), channel_id=1, source_target_pairs={{0,6},{1,7},{2,0},{3,1},{4,2},{5,3},{6,4},{7,5},{8,14},{9,15},{10,... | collective-permute-start | bytes 393224 | tf_op jit(solution)/shard_map/ppermute | solution.py:44
  88.6 2.2 %copy-start.15 = (bf16[2,2,16,1024]{3,2,1,0:T(8,128)(2,1)}, bf16[2,2,16,1024]{3,2,1,0:T(8,128)(2,1)S(1)}, u32[]{:S(2)}) copy-start(bf16[2,2,16,1024]{3,2,1,0:T(8,128)(2,1)S(1)} %collective-permute-done.2.refs_3_) | copy-start | bytes 393220
  88.6 2.2 %copy-start.16 = (bf16[2,2,16,1024]{3,2,1,0:T(8,128)(2,1)}, bf16[2,2,16,1024]{3,2,1,0:T(8,128)(2,1)S(1)}, u32[]{:S(2)}) copy-start(bf16[2,2,16,1024]{3,2,1,0:T(8,128)(2,1)S(1)} %collective-permute-done.3.refs_4_) | copy-start | bytes 393220
  90.7 0.7 copy-start.17
  90.8 0.7 copy-start.18
  97.7 14.7 %collective-permute-start.10 = (bf16[128,768]{1,0:T(8,128)(2,1)}, bf16[128,768]{1,0:T(8,128)(2,1)S(1)}, u32[]{:S(2)}, u32[]{:S(2)}) collective-permute-start(bf16[128,768]{1,0:T(8,128)(2,1)} %get-tuple-element.15), channel_id=1, source_target_pairs={{0,80},{1,81},{2,82},{3,83},{4,84},{5,85},{6,86},{7,87},{8,88},{9,... | collective-permute-start | bytes 589832 | tf_op jit(solution)/shard_map/ppermute | solution.py:44
  100.4 13.3 %collective-permute-start.11 = (bf16[128,768]{1,0:T(8,128)(2,1)}, bf16[128,768]{1,0:T(8,128)(2,1)S(1)}, u32[]{:S(2)}, u32[]{:S(2)}) collective-permute-start(bf16[128,768]{1,0:T(8,128)(2,1)} %get-tuple-element.16), channel_id=1, source_target_pairs={{0,64},{1,65},{2,66},{3,67},{4,68},{5,69},{6,70},{7,71},{8,72},{9,... | collective-permute-start | bytes 589832 | tf_op jit(solution)/shard_map/ppermute | solution.py:44
  102.4 11.4 %collective-permute-start.12 = (bf16[128,768]{1,0:T(8,128)(2,1)}, bf16[128,768]{1,0:T(8,128)(2,1)S(1)}, u32[]{:S(2)}, u32[]{:S(2)}) collective-permute-start(bf16[128,768]{1,0:T(8,128)(2,1)} %get-tuple-element.17), channel_id=1, source_target_pairs={{0,16},{1,17},{2,18},{3,19},{4,20},{5,21},{6,22},{7,23},{8,24},{9,... | collective-permute-start | bytes 589832 | tf_op jit(solution)/shard_map/ppermute | solution.py:44
  103.4 3.4 %copy-start = (bf16[64,1,512,128]{3,2,1,0:T(8,128)(2,1)S(1)}, bf16[64,1,512,128]{3,2,1,0:T(8,128)(2,1)}, u32[]{:S(2)}) copy-start(bf16[64,1,512,128]{3,2,1,0:T(8,128)(2,1)} %param.15) | copy-start | bytes 25165828
  106.8 3.4 %copy-start.1 = (bf16[64,1,512,128]{3,2,1,0:T(8,128)(2,1)S(1)}, bf16[64,1,512,128]{3,2,1,0:T(8,128)(2,1)}, u32[]{:S(2)}) copy-start(bf16[64,1,512,128]{3,2,1,0:T(8,128)(2,1)} %param.16) | copy-start | bytes 25165828
  110.1 0.9 copy-start.3
  111.1 2.7 %copy-start.4 = (bf16[128,768]{1,0:T(8,128)(2,1)S(1)}, bf16[128,768]{1,0:T(8,128)(2,1)}, u32[]{:S(2)}) copy-start(bf16[128,768]{1,0:T(8,128)(2,1)} %get-tuple-element.14.refs_2_.refs_0_) | copy-start | bytes 589828
  117.3 5.3 %collective-permute-start.17 = (bf16[128,512]{1,0:T(8,128)(2,1)S(1)}, bf16[128,512]{1,0:T(8,128)(2,1)S(1)}, u32[]{:S(2)}, u32[]{:S(2)}) collective-permute-start(bf16[128,512]{1,0:T(8,128)(2,1)S(1)} %shard_map.98.refs_1_.refs_0_), channel_id=1, source_target_pairs={{0,1},{1,0},{2,3},{3,2},{4,5},{5,4},{6,7},{7,6},{8,9},{9,8},{10,11... | collective-permute-start | bytes 393224 | tf_op jit(solution)/shard_map/ppermute | solution.py:44
  118.1 7.8 %collective-permute-start.13 = (bf16[128,512]{1,0:T(8,128)(2,1)S(1)}, bf16[128,512]{1,0:T(8,128)(2,1)S(1)}, u32[]{:S(2)}, u32[]{:S(2)}) collective-permute-start(bf16[128,512]{1,0:T(8,128)(2,1)S(1)} %shard_map.98.refs_1_.refs_0_), channel_id=1, source_target_pairs={{0,2},{1,3},{2,4},{3,5},{4,6},{5,7},{6,0},{7,1},{8,10},{9,11},{10,... | collective-permute-start | bytes 393224 | tf_op jit(solution)/shard_map/ppermute | solution.py:44
  119.5 6.5 %collective-permute-start.14 = (bf16[128,512]{1,0:T(8,128)(2,1)S(1)}, bf16[128,512]{1,0:T(8,128)(2,1)S(1)}, u32[]{:S(2)}, u32[]{:S(2)}) collective-permute-start(bf16[128,512]{1,0:T(8,128)(2,1)S(1)} %shard_map.98.refs_1_.refs_0_), channel_id=1, source_target_pairs={{0,6},{1,7},{2,0},{3,1},{4,2},{5,3},{6,4},{7,5},{8,14},{9,15},{10,... | collective-permute-start | bytes 393224 | tf_op jit(solution)/shard_map/ppermute | solution.py:44
  122.6 6.8 %collective-permute-start.18 = (bf16[128,512]{1,0:T(8,128)(2,1)S(1)}, bf16[128,512]{1,0:T(8,128)(2,1)S(1)}, u32[]{:S(2)}, u32[]{:S(2)}) collective-permute-start(bf16[128,512]{1,0:T(8,128)(2,1)S(1)} %collective-permute-done.17.refs_5_), channel_id=1, source_target_pairs={{0,2},{1,3},{2,4},{3,5},{4,6},{5,7},{6,0},{7,1},{8,10},{9,11},{10,... | collective-permute-start | bytes 393224 | tf_op jit(solution)/shard_map/ppermute | solution.py:44
  123.9 5.6 %collective-permute-start.19 = (bf16[128,512]{1,0:T(8,128)(2,1)S(1)}, bf16[128,512]{1,0:T(8,128)(2,1)S(1)}, u32[]{:S(2)}, u32[]{:S(2)}) collective-permute-start(bf16[128,512]{1,0:T(8,128)(2,1)S(1)} %collective-permute-done.17.refs_5_), channel_id=1, source_target_pairs={{0,6},{1,7},{2,0},{3,1},{4,2},{5,3},{6,4},{7,5},{8,14},{9,15},{10,... | collective-permute-start | bytes 393224 | tf_op jit(solution)/shard_map/ppermute | solution.py:44
  125.9 11.0 %collective-permute-start.15 = (bf16[64,512]{1,0:T(8,128)(2,1)S(1)}, bf16[64,512]{1,0:T(8,128)(2,1)S(1)}, u32[]{:S(2)}, u32[]{:S(2)}) collective-permute-start(bf16[64,512]{1,0:T(8,128)(2,1)S(1)} %slice.36), channel_id=1, source_target_pairs={{0,2},{1,3},{2,4},{3,5},{4,6},{5,7},{6,0},{7,1},{8,10},{9,11},{10,... | collective-permute-start | bytes 196616 | tf_op jit(solution)/shard_map/ppermute | solution.py:44
  126.0 10.9 %collective-permute-start.16 = (bf16[64,512]{1,0:T(8,128)(2,1)S(1)}, bf16[64,512]{1,0:T(8,128)(2,1)S(1)}, u32[]{:S(2)}, u32[]{:S(2)}) collective-permute-start(bf16[64,512]{1,0:T(8,128)(2,1)S(1)} %slice.37), channel_id=1, source_target_pairs={{0,6},{1,7},{2,0},{3,1},{4,2},{5,3},{6,4},{7,5},{8,14},{9,15},{10,... | collective-permute-start | bytes 196616 | tf_op jit(solution)/shard_map/ppermute | solution.py:44
  129.4 7.4 %collective-permute-start.20 = (bf16[64,512]{1,0:T(8,128)(2,1)S(1)}, bf16[64,512]{1,0:T(8,128)(2,1)S(1)}, u32[]{:S(2)}, u32[]{:S(2)}) collective-permute-start(bf16[64,512]{1,0:T(8,128)(2,1)S(1)} %slice.38), channel_id=1, source_target_pairs={{0,2},{1,3},{2,4},{3,5},{4,6},{5,7},{6,0},{7,1},{8,10},{9,11},{10,... | collective-permute-start | bytes 196616 | tf_op jit(solution)/shard_map/ppermute | solution.py:44
  129.4 7.4 %copy-start.5 = (s32[5]{0:T(128)S(1)}, s32[5]{0:T(128)}, u32[]{:S(2)}) copy-start(s32[5]{0:T(128)} %stack.23.place) | copy-start | bytes 64
  129.5 7.4 %collective-permute-start.21 = (bf16[64,512]{1,0:T(8,128)(2,1)S(1)}, bf16[64,512]{1,0:T(8,128)(2,1)S(1)}, u32[]{:S(2)}, u32[]{:S(2)}) collective-permute-start(bf16[64,512]{1,0:T(8,128)(2,1)S(1)} %slice.39), channel_id=1, source_target_pairs={{0,6},{1,7},{2,0},{3,1},{4,2},{5,3},{6,4},{7,5},{8,14},{9,15},{10,... | collective-permute-start | bytes 196616 | tf_op jit(solution)/shard_map/ppermute | solution.py:44
  132.8 3.4 %copy-start.2 = (bf16[4096,1024]{1,0:T(8,128)(2,1)S(1)}, bf16[4096,1024]{1,0:T(8,128)(2,1)}, u32[]{:S(2)}) copy-start(bf16[4096,1024]{1,0:T(8,128)(2,1)} %all-gather.2.cloned.1.call-done.refs_0_) | copy-start | bytes 25165828
Sparse Core Ops, SparseCore 0:
  30.0 94.6 all-gather.1
